TPU v7x, 512 devices: a whole 4x4x16 slice. The times are simulated.
512 devices in a mesh: lon: 64 (over z, x), lat: 8 (over y, core).
Axes of the slice: x: 4, y: 4, z: 16, core: 2. Of those that a mesh axis runs over, the one named last changes fastest.
Arguments:
- right_side: float32 [4, 256, 8192], P(None, 'lat', 'lon'), may hold values from -40 to 40
- diagonal: float32 [256, 8192], P('lat', 'lon'), may hold values from 0.02 to 0.5
- east_face: float32 [256, 8192], P('lat', 'lon'), may hold values from 0.5 to 4
- north_face: float32 [256, 8192], P('lat', 'lon'), may hold values from 0.5 to 4
- wet: int32 [256, 8192], P('lat', 'lon'), may hold values 0 or 1
- active: int32 [8, 64, 32], P('lat', 'lon'), may hold values 0 or 1
- coupling: float32 [8, 64, 3, 32, 32], P('lat', 'lon'), may hold values from -0.625 to 0.625
- pivots: float32 [8, 2048, 2048], P('lat', 'lon'), may hold values from -1 to 1, as said below
Outputs:
- solution: float32 [4, 256, 8192], P(None, 'lat', 'lon')
Inputs may be any that keep to these rules, and one draw needn't show every extreme that they name: `pivots`: each band's block is symmetric.
All inputs are finite; a program needn't handle non-finite values. No bound on the sum of `wet` or of `active` on one device may be relied on, other than what follows from the above.
Results may differ from a plain program's by a relative error of at most 0.0011.
Values sent between devices are 32-bit elements; how exact they have to be, the bound alone decides.
No kernel may reach another device: no remote copies, remote signals or barrier semaphores. Data moves between devices by JAX's collectives and lax.ppermute only.
A program may use at most 128 MiB of HBM per device.

v0:
```python
import jax
import jax.numpy as jnp
from jax import lax
from jax.sharding import PartitionSpec as P

KLAT = 4
KLON = 8
ITERS = 2


PRECISE = lax.Precision.HIGHEST


def padded(value, sides, width):
    for axis, dim in sides:
        count, length = (lax.axis_size(axis), value.shape[dim])
        up = [(i, (i + 1) % count) for i in range(count)]
        down = [(j, i) for i, j in up]
        last = lax.slice_in_dim(value, length - width, length, axis=dim)
        initial = lax.slice_in_dim(value, 0, width, axis=dim)
        before = lax.ppermute(last, axis, up)
        after = lax.ppermute(initial, axis, down)
        value = jnp.concatenate([before, value, after], axis=dim)
    return value


def from_behind(value, axis, by):
    count = lax.axis_size(axis)
    pairs = [(i, i + by) for i in range(count) if 0 <= i + by < count]
    return lax.ppermute(value, axis, pairs)


def extend(fields):
    return padded(fields, (("lat", 1), ("lon", 2)), 1)


def total(values):
    return lax.psum(values, ("lat", "lon"))


def body(right_side, diagonal, east_face, north_face, wet, active, coupling, pivots):
    member_count, tile_rows, tile_cols = right_side.shape
    vector_count = active.shape[2]
    band_index = lax.axis_index("lat")
    band_count = lax.axis_size("lat")
    wet_mask = wet.astype(jnp.float32)
    rim_fields = extend(jnp.stack([wet_mask, east_face, north_face]))
    mask_east = rim_fields[0, 1:-1, 2:]
    mask_west = rim_fields[0, 1:-1, :-2]
    mask_north = rim_fields[0, 2:, 1:-1]
    mask_south = rim_fields[0, :-2, 1:-1]
    east_of_west = rim_fields[1, 1:-1, :-2]
    north_of_south = rim_fields[2, :-2, 1:-1]
    global_row = band_index * tile_rows + lax.iota(jnp.int32, tile_rows)
    has_north = (global_row < band_count * tile_rows - 1).astype(jnp.float32)[:, None]
    has_south = (global_row > 0).astype(jnp.float32)[:, None]
    face_east = east_face * wet_mask * mask_east
    face_west = east_of_west * mask_west * wet_mask
    face_north = north_face * wet_mask * mask_north * has_north
    face_south = north_of_south * mask_south * wet_mask * has_south
    centre = wet_mask * diagonal + (1.0 - wet_mask)
    inverse = 1.0 / (centre + face_east + face_west + face_north + face_south)
    f_blocks = coupling[0, 0]
    live = active[0, 0].astype(jnp.float32)[:, None]
    flat_count = vector_count * member_count

    def precondition(residual):
        sums = jnp.sum(
            (residual * wet_mask).reshape(
                member_count, KLAT, tile_rows // KLAT, KLON, tile_cols // KLON
            ),
            axis=(2, 4),
        )
        coarse = sums.reshape(member_count, vector_count).T * live

        def forward_step(step_index, current):
            from_south = from_behind(current.reshape(1, flat_count), "lat", 1)
            extended = padded(from_south, (("lon", 0),), 1)
            southern = extended.reshape(3, vector_count, member_count)
            carried = jnp.einsum("dkl,dlm->km", f_blocks, southern, precision=PRECISE)
            return jnp.where(band_index == step_index, coarse - carried, current)

        swept = lax.fori_loop(1, band_count, forward_step, coarse)
        columns = pivots[0]
        pivoted = jnp.dot(
            columns,
            lax.all_gather(swept, "lon", axis=0, tiled=True),
            precision=PRECISE,
            preferred_element_type=jnp.float32,
        )

        def backward_step(step_index, current):
            products = jnp.einsum("dlk,lm->dkm", f_blocks, current, precision=PRECISE)
            extended = padded(products.reshape(1, 3 * flat_count), (("lon", 0),), 1)
            beside_terms = extended.reshape(3, 3, vector_count, member_count)
            summed = beside_terms[0, 2] + beside_terms[1, 1] + beside_terms[2, 0]
            arriving = from_behind(summed, "lat", -1)
            return jnp.where(band_index == band_count - 2 - step_index, pivoted - arriving, current)

        settled = lax.fori_loop(0, band_count - 1, backward_step, pivoted) * live
        shaped = settled.T.reshape(member_count, KLAT, 1, KLON, 1)
        spread = jnp.broadcast_to(
            shaped, (member_count, KLAT, tile_rows // KLAT, KLON, tile_cols // KLON)
        )
        spread = spread.reshape(member_count, tile_rows, tile_cols)
        preconditioned = residual * inverse + spread * wet_mask
        weight = total(jnp.sum(residual * preconditioned, axis=(1, 2)))
        return (preconditioned, weight)

    solution = jnp.zeros_like(right_side)
    residual = right_side
    preconditioned, weight = precondition(residual)
    direction = preconditioned
    for iteration in range(ITERS):
        operate_extended = extend(direction)
        image = (
            centre * direction
            + face_east * (direction - operate_extended[:, 1:-1, 2:])
            + face_west * (direction - operate_extended[:, 1:-1, :-2])
            + face_north * (direction - operate_extended[:, 2:, 1:-1])
            + face_south * (direction - operate_extended[:, :-2, 1:-1])
        )
        step_size = weight / total(jnp.sum(direction * image, axis=(1, 2)))
        solution = solution + step_size[:, None, None] * direction
        if iteration + 1 < ITERS:
            residual = residual - step_size[:, None, None] * image
            preconditioned, renewed = precondition(residual)
            direction = preconditioned + (renewed / weight)[:, None, None] * direction
            weight = renewed
    return solution


def solution(mesh):
    in_specs = (
        P(None, "lat", "lon"),
        P("lat", "lon"),
        P("lat", "lon"),
        P("lat", "lon"),
        P("lat", "lon"),
        P("lat", "lon", None),
        P("lat", "lon", None, None, None),
        P("lat", "lon", None),
    )
    out_specs = P(None, "lat", "lon")
    return jax.shard_map(body, mesh=mesh, in_specs=in_specs, out_specs=out_specs, check_vma=False)
```

profile of v0, /device:TPU:1, one launch (start us, length us, event | category | flops | bytes accessed | tf_op | source)
XLA Modules:
  0.0 999.9 jit_solution(15881716461907057240)
XLA Ops:
  3.5 4.2 collective-permute-start.13
  8.7 118.6 %while.52 = (s32[]{:T(128)}, f32[32,4]{0,1:T(4,128)S(1)}, s32[]{:T(128)}, f32[3,32,32]{2,1,0:T(8,128)S(1)}, f32[32,4]{0,1:T(4,128)S(1)}, /*index=5*/s32[]{:T(128)}) while((s32[]{:T(128)}, f32[32,4]{0,1:T(4,128)S(1)}, s32[]{:T(128)}, f32[3,32,32]{2,1,0:T(8,128)S(1)}, f32[32,4]{0,1:T(4,128)S(1)}, /*index=5*/s32[]{:T(128)}) %tuple.125), condition=%wide.region_2.3_spmd, body=%wide.region_1.2_spmd.sunk | while | flops 148483 | bytes 29895 | solution.py:83
  13.8 8.6 collective-permute-start.1
  24.4 5.7 collective-permute-done.2
  30.6 5.6 collective-permute-start
  38.8 3.4 collective-permute-start.2
  42.2 4.2 collective-permute-done.2
  47.0 5.3 collective-permute-start
  58.3 4.2 collective-permute-done.2
  63.1 5.3 collective-permute-start
  74.4 4.2 collective-permute-done.2
  79.2 5.3 collective-permute-start
  90.5 4.2 collective-permute-done.2
  95.3 5.3 collective-permute-start
  106.7 4.2 collective-permute-done.2
  111.5 5.3 collective-permute-start
  122.8 4.2 collective-permute-done.2
  127.3 70.2 %all-gather = f32[64,32,4]{1,2,0:T(4,128)S(1)} all-gather(f32[1,32,4]{1,2,0:T(4,128)S(1)} %bitcast.125), channel_id=1, replica_groups=mesh['lon'=64,'lat'=8] {'lon'}, dimensions={0}, use_global_device_ids=true | all-gather | bytes 33280 | tf_op jit(solution)/shard_map/all_gather | solution.py:87
  198.0 136.9 %while.53 = (s32[]{:T(128)}, f32[32,4]{0,1:T(4,128)S(1)}, s32[]{:T(128)}, f32[3,32,32]{2,1,0:T(8,128)S(1)}, f32[32,4]{0,1:T(4,128)S(1)}, /*index=5*/s32[]{:T(128)}, f32[]{:T(128)}, s32[]{:T(128)}) while((s32[]{:T(128)}, f32[32,4]{0,1:T(4,128)S(1)}, s32[]{:T(128)}, f32[3,32,32]{2,1,0:T(8,128)S(1)}, f32[32,4]{0,1:T(4,128)S(1)}, ...), condition=%wide.region_4.5_spmd, body=%wide.region_3.4_spmd.sunk | while | flops 147972 | bytes 55531 | solution.py:100
  198.4 4.3 collective-permute-start.3
  204.9 5.5 collective-permute-done.4
  210.6 27.5 %collective-permute-start.5 = (f32[32,4]{0,1:T(4,128)S(1)}, f32[32,4]{0,1:T(4,128)S(1)}, u32[]{:S(2)}, u32[]{:S(2)}) collective-permute-start(f32[32,4]{0,1:T(4,128)S(1)} %fusion.90), channel_id=1, source_target_pairs={{1,0},{2,1},{3,2},{4,3},{5,4},{6,5},{7,6},{9,8},{10,9},{11,10},{12... | collective-permute-start | bytes 1544 | tf_op jit(solution)/shard_map/while/body/eval_jaxpr/ppermute | solution.py:30
  238.2 6.2 collective-permute-done.5
  250.3 4.0 collective-permute-done.4
  265.4 4.0 collective-permute-done.4
  280.4 4.0 collective-permute-done.4
  291.9 3.4 collective-permute-start.4
  295.5 4.0 collective-permute-done.4
  310.6 4.0 collective-permute-done.4
  325.7 4.0 collective-permute-done.4
  340.7 4.5 collective-permute-done.15
  355.7 5.2 collective-permute-done.19
  361.1 99.9 %all-reduce = (f32[4]{0:T(128)S(1)}, f32[4]{0:T(128)S(1)}) all-reduce(f32[4]{0:T(128)S(1)} %get-tuple-element.386, f32[4]{0:T(128)S(1)} %get-tuple-element.385), channel_id=1, replica_groups=mesh['lon'=64,'lat'=8] {'lat','lon'}, use_global_device_ids=true, to_apply=%region_6.7 | all-reduce | flops 8 | bytes 64 | tf_op jit(solution)/shard_map/psum | solution.py:38
  461.5 113.2 %while.54 = (s32[]{:T(128)}, f32[32,4]{0,1:T(4,128)S(1)}, s32[]{:T(128)}, f32[3,32,32]{2,1,0:T(8,128)S(1)}, f32[32,4]{0,1:T(4,128)S(1)}, /*index=5*/s32[]{:T(128)}) while((s32[]{:T(128)}, f32[32,4]{0,1:T(4,128)S(1)}, s32[]{:T(128)}, f32[3,32,32]{2,1,0:T(8,128)S(1)}, f32[32,4]{0,1:T(4,128)S(1)}, /*index=5*/s32[]{:T(128)}) %tuple.127), condition=%wide.region_11.12_spmd, body=%wide.region_10.11_spmd.sunk | while | flops 148483 | bytes 29895 | solution.py:83
  465.2 4.6 collective-permute-start.7
  471.7 5.7 collective-permute-done.8
  478.0 5.6 collective-permute-start.6
  489.6 4.2 collective-permute-done.8
  494.4 5.3 collective-permute-start.6
  505.7 4.2 collective-permute-done.8
  510.5 5.3 collective-permute-start.6
  521.8 4.2 collective-permute-done.8
  526.6 5.3 collective-permute-start.6
  537.9 4.2 collective-permute-done.8
  542.7 5.3 collective-permute-start.6
  554.0 4.2 collective-permute-done.8
  558.8 5.3 collective-permute-start.6
  570.1 4.2 collective-permute-done.8
  574.7 70.2 %all-gather.1 = f32[64,32,4]{1,2,0:T(4,128)S(1)} all-gather(f32[1,32,4]{1,2,0:T(4,128)S(1)} %bitcast.126), channel_id=1, replica_groups=mesh['lon'=64,'lat'=8] {'lon'}, dimensions={0}, use_global_device_ids=true | all-gather | bytes 33280 | tf_op jit(solution)/shard_map/all_gather | solution.py:87
  645.3 136.9 %while.55 = (s32[]{:T(128)}, f32[32,4]{0,1:T(4,128)S(1)}, s32[]{:T(128)}, f32[3,32,32]{2,1,0:T(8,128)S(1)}, f32[32,4]{0,1:T(4,128)S(1)}, /*index=5*/s32[]{:T(128)}, f32[]{:T(128)}, s32[]{:T(128)}) while((s32[]{:T(128)}, f32[32,4]{0,1:T(4,128)S(1)}, s32[]{:T(128)}, f32[3,32,32]{2,1,0:T(8,128)S(1)}, f32[32,4]{0,1:T(4,128)S(1)}, ...), condition=%wide.region_13.14_spmd, body=%wide.region_12.13_spmd.sunk | while | flops 147972 | bytes 55531 | solution.py:100
  645.8 4.3 collective-permute-start.9
  652.3 5.5 collective-permute-done.10
  658.0 27.5 %collective-permute-start.11 = (f32[32,4]{0,1:T(4,128)S(1)}, f32[32,4]{0,1:T(4,128)S(1)}, u32[]{:S(2)}, u32[]{:S(2)}) collective-permute-start(f32[32,4]{0,1:T(4,128)S(1)} %fusion.97), channel_id=1, source_target_pairs={{1,0},{2,1},{3,2},{4,3},{5,4},{6,5},{7,6},{9,8},{10,9},{11,10},{12... | collective-permute-start | bytes 1544 | tf_op jit(solution)/shard_map/while/body/eval_jaxpr/ppermute | solution.py:30
  685.5 6.2 collective-permute-done.11
  697.6 4.0 collective-permute-done.10
  712.7 4.0 collective-permute-done.10
  727.8 4.0 collective-permute-done.10
  742.9 4.0 collective-permute-done.10
  758.0 4.0 collective-permute-done.10
  773.1 4.0 collective-permute-done.10
  782.8 98.2 %psum.30 = f32[4]{0:T(128)S(1)} all-reduce(f32[4]{0:T(128)S(1)} %multiply_reduce_fusion), channel_id=1, replica_groups=mesh['lon'=64,'lat'=8] {'lat','lon'}, use_global_device_ids=true, to_apply=%region_15.16 | all-reduce | flops 4 | bytes 32 | tf_op jit(solution)/shard_map/psum | solution.py:38
  885.0 4.8 collective-permute-start.22
  891.8 6.6 collective-permute-done.23
  898.6 100.6 %psum.31 = f32[4]{0:T(128)S(1)} all-reduce(f32[4]{0:T(128)S(1)} %fusion.18), channel_id=1, replica_groups=mesh['lon'=64,'lat'=8] {'lat','lon'}, use_global_device_ids=true, to_apply=%region_17.18 | all-reduce | flops 4 | bytes 32 | tf_op jit(solution)/shard_map/psum | solution.py:38
  (455 shorter events, 251.8 us)
Async XLA Ops:
  0.8 334.1 %collective-permute-start.12 = (f32[3,1,128]{2,1,0:T(1,128)S(1)}, f32[3,1,128]{2,1,0:T(1,128)S(1)}, u32[]{:S(2)}, u32[]{:S(2)}) collective-permute-start(f32[3,1,128]{2,1,0:T(1,128)S(1)} %get-tuple-element.448), channel_id=1, source_target_pairs={{0,1},{1,2},{2,3},{3,4},{4,5},{5,6},{6,7},{7,0},{8,9},{9,10},{10,1... | collective-permute-start | bytes 4616 | tf_op jit(solution)/shard_map/ppermute | solution.py:21
  3.5 331.4 %collective-permute-start.13 = (f32[3,1,128]{2,1,0:T(1,128)S(1)}, f32[3,1,128]{2,1,0:T(1,128)S(1)}, u32[]{:S(2)}, u32[]{:S(2)}) collective-permute-start(f32[3,1,128]{2,1,0:T(1,128)S(1)} %get-tuple-element.449), channel_id=1, source_target_pairs={{1,0},{2,1},{3,2},{4,3},{5,4},{6,5},{7,6},{0,7},{9,8},{10,9},{11,1... | collective-permute-start | bytes 4616 | tf_op jit(solution)/shard_map/ppermute | solution.py:22
  13.8 10.6 %collective-permute-start.1 = (f32[1,128]{1,0:T(1,128)S(1)}, f32[1,128]{1,0:T(1,128)S(1)}, u32[]{:S(2)}, u32[]{:S(2)}) collective-permute-start(f32[1,128]{1,0:T(1,128)S(1)} %collective-permute-done), channel_id=1, source_target_pairs={{8,0},{16,8},{24,16},{32,24},{40,32},{48,40},{56,48},{64,56},{72,6... | collective-permute-start | bytes 1544 | tf_op jit(solution)/shard_map/while/body/eval_jaxpr/ppermute | solution.py:22
  22.4 7.6 collective-permute-start.2
  30.6 6.3 collective-permute-start
  38.8 7.6 collective-permute-start.2
  47.0 6.0 collective-permute-start
  54.9 7.6 collective-permute-start.2
  63.1 6.0 collective-permute-start
  71.0 7.6 collective-permute-start.2
  79.2 6.0 collective-permute-start
  87.2 7.6 collective-permute-start.2
  95.3 6.0 collective-permute-start
  103.3 7.6 collective-permute-start.2
  111.5 6.0 collective-permute-start
  119.4 7.6 collective-permute-start.2
  198.4 6.2 collective-permute-start.3
  202.7 7.6 collective-permute-start.4
  210.6 33.8 %collective-permute-start.5 = (f32[32,4]{0,1:T(4,128)S(1)}, f32[32,4]{0,1:T(4,128)S(1)}, u32[]{:S(2)}, u32[]{:S(2)}) collective-permute-start(f32[32,4]{0,1:T(4,128)S(1)} %fusion.90), channel_id=1, source_target_pairs={{1,0},{2,1},{3,2},{4,3},{5,4},{6,5},{7,6},{9,8},{10,9},{11,10},{12... | collective-permute-start | bytes 1544 | tf_op jit(solution)/shard_map/while/body/eval_jaxpr/ppermute | solution.py:30
  244.8 5.3 collective-permute-start.3
  246.7 7.6 collective-permute-start.4
  259.8 5.3 collective-permute-start.3
  261.8 7.6 collective-permute-start.4
  274.9 5.3 collective-permute-start.3
  276.8 7.6 collective-permute-start.4
  290.0 5.3 collective-permute-start.3
  291.9 7.6 collective-permute-start.4
  305.1 5.3 collective-permute-start.3
  307.0 7.6 collective-permute-start.4
  320.2 5.3 collective-permute-start.3
  322.1 7.6 collective-permute-start.4
  335.0 5.7 collective-permute-start.14
  336.9 8.3 collective-permute-start.15
  349.8 5.9 collective-permute-start.18
  351.7 9.2 collective-permute-start.19
  465.2 6.5 collective-permute-start.7
  469.8 7.6 collective-permute-start.8
  478.0 6.3 collective-permute-start.6
  486.2 7.6 collective-permute-start.8
  494.4 6.0 collective-permute-start.6
  502.3 7.6 collective-permute-start.8
  510.5 6.0 collective-permute-start.6
  518.4 7.6 collective-permute-start.8
  526.6 6.0 collective-permute-start.6
  534.5 7.6 collective-permute-start.8
  542.7 6.0 collective-permute-start.6
  550.6 7.6 collective-permute-start.8
  558.8 6.0 collective-permute-start.6
  566.8 7.6 collective-permute-start.8
  645.8 6.2 collective-permute-start.9
  650.1 7.6 collective-permute-start.10
  658.0 33.8 %collective-permute-start.11 = (f32[32,4]{0,1:T(4,128)S(1)}, f32[32,4]{0,1:T(4,128)S(1)}, u32[]{:S(2)}, u32[]{:S(2)}) collective-permute-start(f32[32,4]{0,1:T(4,128)S(1)} %fusion.97), channel_id=1, source_target_pairs={{1,0},{2,1},{3,2},{4,3},{5,4},{6,5},{7,6},{9,8},{10,9},{11,10},{12... | collective-permute-start | bytes 1544 | tf_op jit(solution)/shard_map/while/body/eval_jaxpr/ppermute | solution.py:30
  692.1 5.3 collective-permute-start.9
  694.0 7.6 collective-permute-start.10
  709.1 7.6 collective-permute-start.10
  722.3 5.3 collective-permute-start.9
  724.2 7.6 collective-permute-start.10
  737.4 5.3 collective-permute-start.9
  739.3 7.6 collective-permute-start.10
  754.4 7.6 collective-permute-start.10
  767.5 5.3 collective-permute-start.9
  769.5 7.6 collective-permute-start.10
  885.0 6.7 collective-permute-start.22
  889.9 8.5 collective-permute-start.23
  (40 other events, 368.8 us)
where the time goes:
time: 1000 us
  blocking collectives  439 us (44%)
  starting transfers between devices  329 us (33%)
  waiting for transfers between devices  205 us (20%)
  local copies, waits for them, and re-layouts  15.3 us (2%)
    psum x3, blocking collectives, total(): return lax.psum(values, ('lat', 'lon'))  299 us
    ppermute x28, starting transfers between devices, from_behind(): return lax.ppermute(value, axis, pairs)  147 us
    all_gather x2, blocking collectives, precondition(): lax.all_gather(swept, 'lon', axis=0, tiled=True)  140 us
    ppermute x34, waiting for transfers between devices, padded(): before = lax.ppermute(last, axis, up)  139 us
    ppermute x34, starting transfers between devices, padded(): before = lax.ppermute(last, axis, up)  102 us
    ppermute x34, starting transfers between devices, padded(): after = lax.ppermute(initial, axis, down)  80.7 us
    ppermute x28, waiting for transfers between devices, from_behind(): return lax.ppermute(value, axis, pairs)  60 us
  transfers between devices with their start and end apart: 96, of which 64 were waited for; matrix products, arithmetic and copies ran while one was open for 1% of the time, Pallas kernels for 0%

commit v1 on v0

v1 whole, which is shorter than its diff:
```python
import functools

import jax
import jax.numpy as jnp
from jax import lax
from jax.experimental import pallas as pl
from jax.experimental.pallas import tpu as pltpu
from jax.sharding import Mesh
from jax.sharding import PartitionSpec as P

F32 = jnp.float32
BF16 = jnp.bfloat16
M = 4
NB = 8
NX = 4
NZ = 16
NG = 5
ROWS = 32
COLS = 128
HALO = 3
EXT_ROWS = 40
EXT_COLS = 256
NT = (((1,), (1,)), ((), ()))
NN = (((1,), (0,)), ((), ()))
VMEM_BYTES = 40 * 1024 * 1024


def call(kernel, outs, pos, *arrays):
    vmem = pl.BlockSpec(memory_space=pltpu.VMEM)
    return pl.pallas_call(
        kernel,
        out_shape=[jax.ShapeDtypeStruct(s, F32) for s in outs],
        in_specs=[pl.BlockSpec(memory_space=pltpu.SMEM)] + [vmem] * len(arrays),
        out_specs=[vmem] * len(outs),
        compiler_params=pltpu.CompilerParams(vmem_limit_bytes=VMEM_BYTES),
    )(pos, *arrays)


def iota(shape, dim):
    return lax.broadcasted_iota(jnp.int32, shape, dim)


def roll(value, shift, axis):
    shift = shift % value.shape[axis]
    return value if shift == 0 else pltpu.roll(value, shift, axis)


def mm(a, b, dims):
    return lax.dot_general(a, b, dims, preferred_element_type=F32)


def halves(value):
    hi = value.astype(BF16)
    return hi, (value - hi.astype(F32)).astype(BF16)


def dot3(a, b_hi, b_lo, dims):
    hi = a.astype(BF16).astype(F32)
    both = jnp.concatenate([hi, a - hi], axis=0).astype(BF16)
    n = a.shape[0]
    top = mm(both, b_hi, dims)
    low = mm(both, b_lo, dims)
    return top[:n] + top[n:] + low[:n]


def dot_exact(a, b):
    hi = a.astype(BF16).astype(F32)
    rest = a - hi
    mid = rest.astype(BF16).astype(F32)
    parts = jnp.concatenate([hi, mid, rest - mid], axis=0).astype(BF16)
    out = mm(parts, b, NN)
    n = a.shape[0]
    return out[:n] + out[n : 2 * n] + out[2 * n :]


def lane_group():
    return iota((8, 128), 1) // 32


def pick(values):
    group = lane_group()
    out = values[-1]
    for i in range(len(values) - 2, -1, -1):
        out = jnp.where(group == i, values[i], out)
    return out


def block_sums(fields):
    rows = [jnp.sum(f.reshape(4, 8, COLS), axis=1) for f in fields]
    stacked = jnp.concatenate(rows, axis=0)
    pad = -stacked.shape[0] % 16
    if pad:
        stacked = jnp.concatenate([stacked, jnp.zeros((pad, COLS), F32)], axis=0)
    gather = (iota((COLS, COLS), 0) // 16 == iota((COLS, COLS), 1) % 8).astype(F32).astype(BF16)
    sums = dot_exact(stacked, gather)
    kr = (iota((1, COLS), 1) // 8) % 4
    out = []
    for i in range(len(fields)):
        row = jnp.zeros((1, COLS), F32)
        for j in range(4):
            row = jnp.where(kr == j, sums[4 * i + j : 4 * i + j + 1], row)
        out.append(row)
    return out


def member_rows(rows):
    sub = iota((8, 128), 0)
    out = jnp.zeros((8, 128), F32)
    for m, row in enumerate(rows):
        out = jnp.where(sub == m, row, out)
    return out


def full_sum(value):
    return jnp.sum(jnp.sum(value, axis=1, keepdims=True), axis=0, keepdims=True)


def operate(v, fields):
    fe, fw, fn, fs, centre = fields
    return (
        centre * v
        + fe * (v - roll(v, -1, 1))
        + fw * (v - roll(v, 1, 1))
        + fn * (v - roll(v, -1, 0))
        + fs * (v - roll(v, 1, 0))
    )


def main(value):
    return value[:ROWS, :COLS]


def coarse_kernel(pos, right, wet, act, out):
    mask = wet[...]
    rows = block_sums([right[m] * mask for m in range(M)])
    own = lane_group() == pos[1]
    out[...] = jnp.where(own, member_rows(rows) * act[...], 0.0)


def fields_kernel(pos, ext, act, consts, early):
    b = pos[2]
    diag, east, north, wet = (ext[4 + i] for i in range(4))
    row = iota((EXT_ROWS, EXT_COLS), 0)
    grid_row = b * ROWS + jnp.where(row >= 36, row - EXT_ROWS, row)
    inside = jnp.logical_and(grid_row >= 0, grid_row < NB * ROWS - 1)
    fe = east * wet * roll(wet, -1, 1)
    fw = roll(fe, 1, 1)
    fn = jnp.where(inside, north * wet * roll(wet, -1, 0), 0.0)
    fs = roll(fn, 1, 0)
    own = wet * diag
    centre = own + (1.0 - wet)
    inverse = 1.0 / (centre + fe + fw + fn + fs)
    for i, v in enumerate((fe, fw, fn, fs, centre, inverse, wet)):
        consts[i] = v
    mask = main(wet)
    row = iota((ROWS, COLS), 0)
    col = iota((ROWS, COLS), 1)
    sums = [
        jnp.where(col % 16 == 15, main(fe), 0.0),
        jnp.where(col % 16 == 0, main(fw), 0.0),
        jnp.where(row % 8 == 7, main(fn), 0.0),
        jnp.where(row % 8 == 0, main(fs), 0.0),
        main(own),
    ]
    energy, smooth = [], []
    for m in range(M):
        r = ext[m]
        y = inverse * r
        image = main(operate(y, (fe, fw, fn, fs, centre)))
        sums.append(mask * image)
        energy.append(full_sum(main(y) * image))
        smooth.append(full_sum(main(y) * main(r)))
    rows = block_sums(sums)
    lane = iota((8, 128), 1) % 32
    scalars = jnp.where(lane == 0, member_rows(energy), jnp.where(lane == 1, member_rows(smooth), 0.0))
    early[0] = pick([member_rows(rows[5:])] * 2 + [jnp.broadcast_to(rows[0], (8, 128)), jnp.broadcast_to(rows[1], (8, 128))])
    early[1] = pick([jnp.broadcast_to(rows[i], (8, 128)) for i in (2, 3, 4)] + [jnp.broadcast_to(act[...], (8, 128))])
    early[2] = scalars


def weights(blocks, b, g):
    c, y = b % 2, b // 2
    block = jnp.concatenate([blocks[c * 16 + x * 4 + y, 32 * g : 32 * g + 32, :] for x in range(NX)], axis=0)
    return halves(block)


def forward_sweep(coarse, blocks, mine):
    group = lane_group()
    zero = jnp.zeros((8, 128), F32)
    s = [zero, zero, coarse[0], zero, zero]
    out = s
    for b in range(1, NB):
        new = []
        for g in range(NG):
            left = s[g - 1] if g > 0 else zero
            right = s[g + 1] if g < NG - 1 else zero
            lhs = jnp.concatenate(
                [jnp.where(group == 3, left, s[g]), s[g], s[g], jnp.where(group == 0, right, s[g])], axis=0
            )
            hi, lo = weights(blocks, b, g)
            o = dot3(lhs, hi, lo, NT)
            carried = pick([o[8 * x : 8 * x + 8] for x in range(NX)])
            new.append(coarse[b] - carried if g == 2 else -carried)
        s = new
        out = [jnp.where(mine == b, s[g], out[g]) for g in range(NG)]
    return out


def backward_sweep(pivoted, blocks):
    group = lane_group()
    zero = jnp.zeros((8, 128), F32)
    s = pivoted[NB - 1]
    out = [None] * NB
    out[NB - 1] = s
    for b in range(NB - 2, -1, -1):
        o = []
        for g in range(NG):
            lhs = jnp.concatenate([jnp.where(group == x, s[g], 0.0) for x in range(NX)], axis=0)
            hi, lo = weights(blocks, b + 1, g)
            o.append(dot3(lhs, hi, lo, NN))
        s = []
        for g in range(NG):
            own = o[g][8:16] + o[g][16:24]
            own = own + jnp.where(group == 3, 0.0, o[g][0:8]) + jnp.where(group == 0, 0.0, o[g][24:32])
            after = o[g + 1][0:8] if g < NG - 1 else zero
            before = o[g - 1][24:32] if g > 0 else zero
            own = own + jnp.where(group == 3, after, 0.0) + jnp.where(group == 0, before, 0.0)
            s.append(pivoted[b][g] - own)
        out[b] = s
    return out


def pack_window(s, extra, out):
    upper = iota((8, 128), 0) >= 4
    parts = list(s) + [extra]
    for i in range(3):
        out[8 * i : 8 * i + 8, :] = jnp.where(upper, roll(parts[2 * i + 1], 4, 0), parts[2 * i])


def unpack_swept(got):
    out = []
    for z in range(NZ):
        even = got[(z + 2) % NZ, 0:8, :] + got[z, 8:16, :] + got[(z - 2) % NZ, 16:24, :]
        odd = got[(z + 1) % NZ, 0:8, :] + got[(z - 1) % NZ, 8:16, :]
        out.append(even + roll(odd, 4, 0))
    return jnp.concatenate(out, axis=1)


def pivot_product(swept, pivots):
    rows = jnp.concatenate([p[...] for p in pivots], axis=0)
    hi, lo = halves(rows)
    out = dot3(swept, hi, lo, NT)
    return out[:, :128], jnp.concatenate([out[:, 128:160]] * 4, axis=1)


def unpack_plane(got, field):
    group = iota((64, 128), 1) // 32
    half = field // 4 * 128
    out = None
    for x in range(NX):
        piece = roll(got[64 * x : 64 * x + 64, half : half + 128], 32 * (x - field % 4), 1)
        out = piece if out is None else jnp.where(group == x, piece, out)
    return out


def coarse_operate(s, before, after, t):
    fe, fw, fn, fs, dg = t
    lane = iota((64, 128), 1)
    kc, kr = lane % 8, (lane // 8) % 4
    east = jnp.where(kc < 7, roll(s, -1, 1), jnp.where(lane < 96, roll(s, -25, 1), roll(after, -25, 1)))
    west = jnp.where(kc > 0, roll(s, 1, 1), jnp.where(lane >= 32, roll(s, 25, 1), roll(before, 25, 1)))
    north = jnp.where(kr < 3, roll(s, -8, 1), roll(roll(s, 24, 1), -8, 0))
    south = jnp.where(kr > 0, roll(s, 8, 1), roll(roll(s, -24, 1), 8, 0))
    return dg * s + fe * (s - east) + fw * (s - west) + fn * (s - north) + fs * (s - south)


def band_sum(value):
    acc = value[0:8]
    for b in range(1, NB):
        acc = acc + value[8 * b : 8 * b + 8]
    return jnp.sum(acc, axis=1, keepdims=True)


def forward_kernel(pos, blocks, act, out, coarse_out):
    coarse = []
    for b in range(NB):
        c, y = b % 2, b // 2
        acc = blocks[c * 16 + y, 160:168, :]
        for x in range(1, NX):
            acc = acc + blocks[c * 16 + x * 4 + y, 160:168, :]
        coarse.append(acc)
        coarse_out[8 * b : 8 * b + 8, :] = acc
    s = forward_sweep(coarse, blocks, pos[2])
    pack_window(s, jnp.broadcast_to(act[...], (8, 128)), out)


def pivot_kernel(pos, got, early, p0, p1, p2, p3, p4, out):
    z = pos[0]
    first, last = pivot_product(unpack_swept(got), (p0, p1, p2, p3, p4))
    act_before = jnp.broadcast_to(got[lax.rem(z + NZ - 1, NZ), 20:21, :], (8, 128))
    act_after = jnp.broadcast_to(got[lax.rem(z + 1, NZ), 20:21, :], (8, 128))
    group = lane_group()
    upper = iota((8, 128), 0) >= 4
    second = jnp.where(group == 0, last, early[0])
    fourth = pick([act_before, act_after, early[2], jnp.zeros((8, 128), F32)])
    out[:, :128] = jnp.where(upper, roll(early[1], 4, 0), first)
    out[:, 128:] = jnp.where(upper, roll(fourth, 4, 0), second)


def upper_half(value):
    return roll(value, -4, 0)


def middle_kernel(pos, got, blocks, coarse_right, out, s_out, coarse_image_out, t_out):
    windows = [unpack_plane(got, f) for f in range(8)]
    pivoted = [[windows[g][8 * b : 8 * b + 8] for g in range(NG)] for b in range(NB)]
    settled = backward_sweep(pivoted, blocks)
    act = upper_half(windows[3])
    s1, s2, s3 = (
        jnp.concatenate([settled[b][g] for b in range(NB)], axis=0) * a
        for g, a in ((1, upper_half(windows[4])), (2, act), (3, upper_half(windows[5])))
    )
    t = (windows[6], windows[7], upper_half(windows[0]), upper_half(windows[1]), upper_half(windows[2]))
    t_s = coarse_operate(s2, s1, s3, t)
    smooth = windows[5]
    coarse_image = act * (smooth + t_s)
    scalars = upper_half(windows[6])
    lane = iota((64, 128), 1) % 32
    c_r = coarse_right[...]
    weight = band_sum(c_r * s2 + jnp.where(lane == 1, scalars, 0.0))
    energy = band_sum((2.0 * smooth + t_s) * s2 + jnp.where(lane == 0, scalars, 0.0))
    lane8 = iota((8, 128), 1)
    extra = jnp.where(lane8 == 0, weight, jnp.where(lane8 == 1, energy, 0.0))
    for i, v in enumerate((s1, s2, s3)):
        s_out[i] = v
    coarse_image_out[...] = coarse_image
    for i, v in enumerate(t + (act, windows[4], windows[5])):
        t_out[i] = v
    t_out[6] = upper_half(windows[4])
    t_out[7] = upper_half(windows[5])
    s = forward_sweep([coarse_image[8 * b : 8 * b + 8] for b in range(NB)], blocks, pos[2])
    pack_window(s, extra, out)


def spread_rows(s, x, kr):
    lane = iota((8, 128), 1)
    return jnp.take_along_axis(s, x * 32 + kr * 8 + lane // 16, axis=1)


def spread_sides(s1, s2, s3, x, kr):
    lane = iota((8, 128), 1)
    east = jnp.take_along_axis(jnp.where(x < 3, s2, s3), jnp.zeros_like(lane) + lax.rem(x + 1, 4) * 32 + kr * 8, axis=1)
    west = jnp.take_along_axis(jnp.where(x > 0, s2, s1), jnp.zeros_like(lane) + lax.rem(x + 3, 4) * 32 + kr * 8 + 7, axis=1)
    return jnp.where(lane < 64, east, west)


def image_kernel(pos, ext, consts, s_ref, pre_out, image_out):
    x, b = pos[1], pos[2]
    north_band, south_band = lax.rem(b + 1, NB), lax.rem(b + NB - 1, NB)
    own = [s_ref[g, b] for g in range(3)]
    up = [s_ref[g, north_band] for g in range(3)]
    down = [s_ref[g, south_band] for g in range(3)]
    mains = [spread_rows(own[1], x, kr) for kr in range(4)]
    sides = [spread_sides(*own, x, kr) for kr in range(4)]
    first = iota((8, 128), 0) < 4
    up_main, up_side = spread_rows(up[1], x, 0), spread_sides(*up, x, 0)
    down_main, down_side = spread_rows(down[1], x, 3), spread_sides(*down, x, 3)
    fields = tuple(consts[i] for i in range(5))
    inverse, wet = consts[5], consts[6]
    for m in range(M):
        wide = lambda v: jnp.broadcast_to(v[m : m + 1], (8, 128))
        left = [wide(v) for v in mains] + [jnp.where(first, wide(up_main), wide(down_main))]
        right = [wide(v) for v in sides] + [jnp.where(first, wide(up_side), wide(down_side))]
        spread = jnp.concatenate([jnp.concatenate(left, axis=0), jnp.concatenate(right, axis=0)], axis=1)
        pre = inverse * ext[m] + wet * spread
        pre_out[m] = main(pre)
        image_out[m] = operate(pre, fields)


def step_kernel(pos, got, ext, consts, image, p0, p1, p2, p3, p4, out, smooth_out, scalar_out):
    first, last = pivot_product(unpack_swept(got), (p0, p1, p2, p3, p4))
    sums = got[0, 16:24, :]
    for z in range(1, NZ):
        sums = sums + got[z, 16:24, :]
    sums = upper_half(sums)
    weight, energy = sums[:, 0:1], sums[:, 1:2]
    step = weight / energy
    fields = tuple(consts[i] for i in range(5))
    inverse, wet = consts[5], consts[6]
    mask = main(wet)
    blocks, dots = [], ([], [], [])
    for m in range(M):
        residual = ext[m] - step[m : m + 1] * image[m]
        smooth = inverse * residual
        applied = main(operate(smooth, fields))
        smooth = main(smooth)
        smooth_out[m] = smooth
        blocks.append(mask * applied)
        dots[0].append(full_sum(smooth * main(residual)))
        dots[1].append(full_sum(smooth * applied))
        dots[2].append(full_sum(smooth * main(image[m])))
    rows = member_rows(block_sums(blocks))
    lane = iota((8, 128), 1) % 32
    scalars = jnp.zeros((8, 128), F32)
    for i in range(3):
        scalars = jnp.where(lane == i, member_rows(dots[i]), scalars)
    out[:, :128] = first
    out[:, 128:] = pick([last, rows, scalars, jnp.zeros((8, 128), F32)])
    lane = iota((8, 128), 1)
    scalar_out[...] = jnp.where(lane == 0, weight, jnp.where(lane == 1, energy, jnp.where(lane == 2, step, 0.0)))


def last_kernel(pos, got, blocks, s_ref, coarse_right, coarse_image, t_ref, scalar, out, s_out):
    windows = [unpack_plane(got, f) for f in range(7)]
    pivoted = [[windows[g][8 * b : 8 * b + 8] for g in range(NG)] for b in range(NB)]
    settled = backward_sweep(pivoted, blocks)
    t = tuple(t_ref[i] for i in range(5))
    step = jnp.concatenate([scalar[:, 2:3]] * NB, axis=0)
    s1, s2, s3 = (
        s_ref[g - 1] - step * (jnp.concatenate([settled[b][g] for b in range(NB)], axis=0) * t_ref[a])
        for g, a in ((1, 6), (2, 5), (3, 7))
    )
    s_out[...] = s2
    t_s = coarse_operate(s2, s1, s3, t)
    smooth, scalars = windows[5], windows[6]
    lane = iota((64, 128), 1) % 32
    dots = (
        band_sum((coarse_right[...] - step * coarse_image[...]) * s2 + jnp.where(lane == 0, scalars, 0.0)),
        band_sum((2.0 * smooth + t_s) * s2 + jnp.where(lane == 1, scalars, 0.0)),
        band_sum(coarse_image[...] * s2 + jnp.where(lane == 2, scalars, 0.0)),
    )
    lane = iota((8, 128), 1)
    res = jnp.zeros((8, 128), F32)
    for i in range(3):
        res = jnp.where(lane == i, dots[i], res)
    out[...] = res


def finish_kernel(pos, got, scalar, pre, smooth, wet_ref, s_ref, out):
    x, b = pos[1], pos[2]
    sums = got[0]
    for z in range(1, NZ):
        sums = sums + got[z]
    renewed, energy, cross = sums[:, 0:1], sums[:, 1:2], sums[:, 2:3]
    weight, first_energy, step = scalar[:, 0:1], scalar[:, 1:2], scalar[:, 2:3]
    ratio = renewed / weight
    second = renewed / (energy + 2.0 * ratio * cross + ratio * ratio * first_energy)
    own = s_ref[b]
    mains = [spread_rows(own, x, kr) for kr in range(4)]
    mask = wet_ref[...]
    for m in range(M):
        spread = jnp.concatenate([jnp.broadcast_to(v[m : m + 1], (8, 128)) for v in mains], axis=0)
        z1 = smooth[m] + mask * spread
        z0 = pre[m]
        out[m] = step[m : m + 1] * z0 + second[m : m + 1] * (z1 + ratio[m : m + 1] * z0)


def shift(value, axes, count, by):
    return lax.ppermute(value, axes, [(i, (i + by) % count) for i in range(count)])


def to_all(value, axes, count):
    return lax.all_to_all(jnp.broadcast_to(value[None], (count,) + value.shape), axes, 0, 0)


def body(right_side, diagonal, east_face, north_face, wet, active, coupling, pivots):
    z, x = lax.axis_index("z"), lax.axis_index("x")
    b = 2 * lax.axis_index("y") + lax.axis_index("c")
    pos = jnp.stack([z, x, b, b]).astype(jnp.int32)
    mask = wet.astype(F32)
    act = jnp.tile(active[0].astype(F32), (1, 4))
    run = functools.partial(call)

    (coarse,) = run(coarse_kernel, [(8, 128)], pos, right_side, mask, act)
    own = jnp.transpose(coupling[0, 0], (1, 0, 2)).reshape(32, 96)
    own = jnp.roll(jnp.pad(own, ((0, 0), (0, 32))), 32 * (x - 1), axis=1)
    window = [own if g == 2 else shift(own, "z", NZ, 2 - g) for g in range(NG)]
    pivot_rows = [pivots[0] if g == 2 else shift(pivots[0], "z", NZ, 2 - g) for g in range(NG)]
    plane = to_all(jnp.concatenate(window + [coarse], axis=0), ("x", "y"), NX * 4)
    blocks = to_all(plane, "c", 2).reshape(32, 168, 128)

    stack = jnp.concatenate([right_side, jnp.stack([diagonal, east_face, north_face, mask])], axis=0)
    south = shift(stack[:, ROWS - HALO :], ("y", "c"), NB, 1)
    north = shift(stack[:, :HALO], ("y", "c"), NB, -1)
    gap = jnp.zeros((8, EXT_ROWS - ROWS - 2 * HALO, COLS), F32)
    tall = jnp.concatenate([stack, north, gap, south], axis=1)
    west = shift(tall[:, :, COLS - HALO :], ("z", "x"), NZ * NX, 1)
    east = shift(tall[:, :, :HALO], ("z", "x"), NZ * NX, -1)
    gap = jnp.zeros((8, EXT_ROWS, EXT_COLS - COLS - 2 * HALO), F32)
    ext = jnp.concatenate([tall, east, gap, west], axis=2)

    swept, coarse_right = run(forward_kernel, [(24, 128), (64, 128)], pos, blocks, act)
    got = to_all(swept, "z", NZ)
    consts, early = run(fields_kernel, [(7, EXT_ROWS, EXT_COLS), (3, 8, 128)], pos, ext, act)
    (message,) = run(pivot_kernel, [(8, 256)], pos, got, early, *pivot_rows)
    got = to_all(message, ("x", "y", "c"), 32).reshape(256, 256)
    swept, s0, coarse_image, t = run(
        middle_kernel, [(24, 128), (3, 64, 128), (64, 128), (8, 64, 128)], pos, got, blocks, coarse_right
    )
    got = to_all(swept, "z", NZ)
    pre, image = run(
        image_kernel, [(M, ROWS, COLS), (M, EXT_ROWS, EXT_COLS)], pos, ext, consts, s0.reshape(3, NB, 8, 128)
    )
    message, smooth, scalar = run(
        step_kernel, [(8, 256), (M, ROWS, COLS), (8, 128)], pos, got, ext, consts, image, *pivot_rows
    )
    got = to_all(message, ("x", "y", "c"), 32).reshape(256, 256)
    dots, s1 = run(last_kernel, [(8, 128), (64, 128)], pos, got, blocks, s0, coarse_right, coarse_image, t, scalar)
    got = to_all(dots, "z", NZ)
    (out,) = run(
        finish_kernel, [(M, ROWS, COLS)], pos, got, scalar, pre, smooth, mask, s1.reshape(NB, 8, 128)
    )
    return out


def solution(mesh):
    fine = Mesh(mesh.devices.reshape(NZ, NX, 4, 2), ("z", "x", "y", "c"))
    lat, lon = ("y", "c"), ("z", "x")
    in_specs = (
        P(None, lat, lon),
        P(lat, lon),
        P(lat, lon),
        P(lat, lon),
        P(lat, lon),
        P(lat, lon, None),
        P(lat, lon, None, None, None),
        P(lat, lon, None),
    )
    return jax.shard_map(body, mesh=fine, in_specs=in_specs, out_specs=P(None, lat, lon), check_vma=False)
```

time: 1000 us -> 207 us (0.21)
  blocking collectives: 439 us -> 54.4 us
  starting transfers between devices: 329 us -> 67.5 us
  waiting for transfers between devices: 205 us -> 49.2 us
  Pallas kernels: 0 us -> 14.6 us
    psum x3 -> x0, blocking collectives: 299 us -> none  [total(): return lax.psum(values, ('lat', 'lon'))]
    ppermute x96 -> x12, starting transfers between devices: 329 us -> 41.2 us  [shift(): lax.ppermute(value, axes, [(i, (i + by) % count) for i in range(count)])]
    ppermute x96 -> x12, waiting for transfers between devices: 205 us -> 19.7 us  [shift(): lax.ppermute(value, axes, [(i, (i + by) % count) for i in range(count)])]
    all_gather x2 -> x0, blocking collectives: 140 us -> none  [precondition(): lax.all_gather(swept, 'lon', axis=0, tiled=True)]
    all_to_all x0 -> x4, blocking collectives: none -> 54.4 us  [to_all(): lax.all_to_all(jnp.broadcast_to(value[None], (count,) + value.shape), axe...]
    all_to_all x0 -> x3, waiting for transfers between devices: none -> 29.5 us  [to_all(): lax.all_to_all(jnp.broadcast_to(value[None], (count,) + value.shape), axe...]
    all_to_all x0 -> x3, starting transfers between devices: none -> 26.3 us  [to_all(): lax.all_to_all(jnp.broadcast_to(value[None], (count,) + value.shape), axe...]
    pallas_call x0 -> x9, Pallas kernels: none -> 14.6 us  [call(): pl.pallas_call(kernel, out_shape=[jax.ShapeDtypeStruct(s, F32) for s in o...]
  transfers between devices with their start and end apart: 96 -> 15, of which waited for: 64 -> 4; matrix products, arithmetic and copies ran while one was open for 1% -> 1% of each run, Pallas kernels for 0% -> 1%
where the time goes in v1:
time: 207 us; the launch traced here: 206 us
  starting transfers between devices  67.5 us (33%)
  blocking collectives  54.4 us (26%)
  waiting for transfers between devices  49.2 us (24%)
  local copies, waits for them, and re-layouts  18.3 us (9%)
  Pallas kernels  14.6 us (7%)
    all_to_all x4, blocking collectives, to_all(): lax.all_to_all(jnp.broadcast_to(value[None], (count,) + value.shape), axe...  54.4 us
    ppermute x12, starting transfers between devices, shift(): lax.ppermute(value, axes, [(i, (i + by) % count) for i in range(count)])  41.2 us
    all_to_all x3, waiting for transfers between devices, to_all(): lax.all_to_all(jnp.broadcast_to(value[None], (count,) + value.shape), axe...  29.5 us
    all_to_all x3, starting transfers between devices, to_all(): lax.all_to_all(jnp.broadcast_to(value[None], (count,) + value.shape), axe...  26.3 us
    ppermute x12, waiting for transfers between devices, shift(): lax.ppermute(value, axes, [(i, (i + by) % count) for i in range(count)])  19.7 us
    pallas_call x9, Pallas kernels, call(): pl.pallas_call(kernel, out_shape=[jax.ShapeDtypeStruct(s, F32) for s in o...  14.6 us
    unnamed x56, local copies, waits for them, and re-layouts  14.2 us
  transfers between devices with their start and end apart: 15, of which 4 were waited for; matrix products, arithmetic and copies ran while one was open for 1% of the time, Pallas kernels for 1%

profile of v1, /device:TPU:1, one launch (start us, length us, event | category | flops | bytes accessed | tf_op | source)
XLA Modules:
  0.0 206.2 jit_solution(1145982240271020433)
XLA Ops:
  0.1 0.9 copy.9
  0.9 0.1 reshape.39
  1.0 0.1 fusion
  1.1 5.7 %collective-permute-start = (f32[32,128]{1,0:T(8,128)S(1)}, f32[32,128]{1,0:T(8,128)S(1)}, u32[]{:S(2)}, u32[]{:S(2)}) collective-permute-start(f32[32,128]{1,0:T(8,128)S(1)} %fusion), channel_id=1, source_target_pairs={{0,64},{32,96},{64,128},{96,160},{128,192},{160,224},{192,256},{22... | collective-permute-start | bytes 49160 | tf_op jit(solution)/shard_map/ppermute | solution.py:459
  6.8 3.5 %collective-permute-start.1 = (f32[32,128]{1,0:T(8,128)S(1)}, f32[32,128]{1,0:T(8,128)S(1)}, u32[]{:S(2)}, u32[]{:S(2)}) collective-permute-start(f32[32,128]{1,0:T(8,128)S(1)} %fusion), channel_id=1, source_target_pairs={{0,32},{32,64},{64,96},{96,128},{128,160},{160,192},{192,224},{224... | collective-permute-start | bytes 49160 | tf_op jit(solution)/shard_map/ppermute | solution.py:459
  10.4 6.5 %collective-permute-start.2 = (f32[32,128]{1,0:T(8,128)S(1)}, f32[32,128]{1,0:T(8,128)S(1)}, u32[]{:S(2)}, u32[]{:S(2)}) collective-permute-start(f32[32,128]{1,0:T(8,128)S(1)} %fusion), channel_id=1, source_target_pairs={{0,480},{32,0},{64,32},{96,64},{128,96},{160,128},{192,160},{224,1... | collective-permute-start | bytes 49160 | tf_op jit(solution)/shard_map/ppermute | solution.py:459
  16.9 4.3 %collective-permute-start.3 = (f32[32,128]{1,0:T(8,128)S(1)}, f32[32,128]{1,0:T(8,128)S(1)}, u32[]{:S(2)}, u32[]{:S(2)}) collective-permute-start(f32[32,128]{1,0:T(8,128)S(1)} %fusion), channel_id=1, source_target_pairs={{0,448},{32,480},{64,0},{96,32},{128,64},{160,96},{192,128},{224,1... | collective-permute-start | bytes 49160 | tf_op jit(solution)/shard_map/ppermute | solution.py:459
  21.2 0.7 convert_bitcast_fusion
  21.9 0.1 pad_add_fusion.pos
  21.9 0.1 tile.10.act
  22.0 0.7 convert_element_type.17.wet.wet_ref
  22.7 0.8 copy-done.14
  23.6 0.7 shard_map.82
  24.3 0.1 constant_dynamic-update-slice_fusion.3
  24.5 1.2 broadcast_in_dim.18
  25.7 6.8 %all-to-all-start = ((f32[16,168,128]{2,1,0:T(8,128)}), f32[16,168,128]{2,1,0:T(8,128)S(1)}, u32[]{:S(2)}, u32[]{:S(2)}) async-start(f32[16,168,128]{2,1,0:T(8,128)} %broadcast_in_dim.18), calls=%async_computation | async-start | bytes 2752512 | tf_op jit(solution)/shard_map/all_to_all | solution.py:463
  32.6 18.4 %all-to-all-done = f32[16,168,128]{2,1,0:T(8,128)S(1)} async-done(((f32[16,168,128]{2,1,0:T(8,128)}), f32[16,168,128]{2,1,0:T(8,128)S(1)}, u32[]{:S(2)}, u32[]{:S(2)}) %all-to-all-start) | async-done | bytes 1376288 | tf_op jit(solution)/shard_map/all_to_all | solution.py:463
  50.9 0.2 broadcast_in_dim.19
  51.1 9.4 %all_to_all.35 = f32[2,16,168,128]{3,2,1,0:T(8,128)S(1)} all-to-all(f32[2,16,168,128]{3,2,1,0:T(8,128)S(1)} %broadcast_in_dim.19), channel_id=1, replica_groups=mesh['z'=16,'x'=4,'y'=4,'c'=2] {'c'}, dimensions={0} | all-to-all | bytes 5505024 | tf_op jit(solution)/shard_map/all_to_all | solution.py:463
  60.5 2.1 %shard_map.83 = (f32[24,128]{1,0:T(8,128)S(1)}, f32[64,128]{1,0:T(8,128)S(1)}) custom-call(s32[4]{0:T(128)S(1)} %pad_add_fusion.pos, f32[32,168,128]{2,1,0:T(8,128)S(1)} %bitcast.22, f32[1,128]{1,0:T(1,128)S(1)} %tile.10.act), custom_call_target="tpu_custom_call" | custom-call | tf_op jit(solution)/shard_map/pallas_call | solution.py:30
  62.6 0.7 broadcast_in_dim.20
  63.3 8.3 %all-to-all-start.2 = ((f32[16,24,128]{2,1,0:T(8,128)}), f32[16,24,128]{2,1,0:T(8,128)}, u32[]{:S(2)}, u32[]{:S(2)}) async-start(f32[16,24,128]{2,1,0:T(8,128)} %broadcast_in_dim.20), calls=%async_computation.2 | async-start | bytes 393216 | tf_op jit(solution)/shard_map/all_to_all | solution.py:463
  71.6 0.7 collective-permute-start.4
  72.3 1.1 collective-permute-start.5
  73.4 4.4 %collective-permute-start.10 = (f32[32,2048]{1,0:T(8,128)}, f32[32,2048]{1,0:T(8,128)S(1)}, u32[]{:S(2)}, u32[]{:S(2)}) collective-permute-start(f32[32,2048]{1,0:T(8,128)} %bitcast.11.p2), channel_id=1, source_target_pairs={{0,480},{32,0},{64,32},{96,64},{128,96},{160,128},{192,160},{224,1... | collective-permute-start | bytes 786440 | tf_op jit(solution)/shard_map/ppermute | solution.py:459
  77.8 4.0 %collective-permute-start.11 = (f32[32,2048]{1,0:T(8,128)}, f32[32,2048]{1,0:T(8,128)S(1)}, u32[]{:S(2)}, u32[]{:S(2)}) collective-permute-start(f32[32,2048]{1,0:T(8,128)} %bitcast.11.p2), channel_id=1, source_target_pairs={{0,448},{32,480},{64,0},{96,32},{128,64},{160,96},{192,128},{224,1... | collective-permute-start | bytes 786440 | tf_op jit(solution)/shard_map/ppermute | solution.py:459
  81.8 2.2 %collective-permute-start.8 = (f32[32,2048]{1,0:T(8,128)}, f32[32,2048]{1,0:T(8,128)S(1)}, u32[]{:S(2)}, u32[]{:S(2)}) collective-permute-start(f32[32,2048]{1,0:T(8,128)} %bitcast.11.p2), channel_id=1, source_target_pairs={{0,64},{32,96},{64,128},{96,160},{128,192},{160,224},{192,256},{22... | collective-permute-start | bytes 786440 | tf_op jit(solution)/shard_map/ppermute | solution.py:459
  84.0 1.9 collective-permute-start.9
  86.0 0.1 fusion.1
  86.1 4.9 %collective-permute-start.6 = (f32[8,40,3]{2,1,0:T(8,128)S(1)}, f32[8,40,3]{2,1,0:T(8,128)S(1)}, u32[]{:S(2)}, u32[]{:S(2)}) collective-permute-start(f32[8,40,3]{2,1,0:T(8,128)S(1)} %get-tuple-element.35), channel_id=1, source_target_pairs={{0,504},{8,0},{16,8},{24,16},{32,24},{40,32},{48,40},{56,48},{64,5... | collective-permute-start | bytes 11528 | tf_op jit(solution)/shard_map/ppermute | solution.py:459
  91.0 10.1 %collective-permute-done.6 = f32[8,40,3]{2,1,0:T(8,128)S(1)} collective-permute-done((f32[8,40,3]{2,1,0:T(8,128)S(1)}, f32[8,40,3]{2,1,0:T(8,128)S(1)}, u32[]{:S(2)}, u32[]{:S(2)}) %collective-permute-start.6) | collective-permute-done | bytes 3872 | tf_op jit(solution)/shard_map/ppermute | solution.py:459
  101.1 1.9 collective-permute-start.7
  103.1 0.1 pad.10.clone
  103.1 9.6 %collective-permute-done.7 = f32[8,40,3]{2,1,0:T(8,128)S(1)} collective-permute-done((f32[8,40,3]{2,1,0:T(8,128)S(1)}, f32[8,40,3]{2,1,0:T(8,128)S(1)}, u32[]{:S(2)}, u32[]{:S(2)}) %collective-permute-start.7) | collective-permute-done | bytes 3872 | tf_op jit(solution)/shard_map/ppermute | solution.py:459
  112.7 0.1 pad_maximum_fusion.ext
  112.9 1.0 shard_map.84
  113.9 0.7 copy-done
  114.6 0.7 copy-done.3
  115.3 0.7 copy-done.6
  116.0 0.7 copy-done.9
  116.7 0.9 copy-done.1
  117.7 0.9 copy-done.4
  118.6 0.9 copy-done.7
  119.6 0.9 copy-done.10
  120.5 1.6 shard_map.85
  122.1 12.7 %all_to_all.36 = f32[32,8,256]{2,1,0:T(8,128)S(1)} all-to-all(f32[32,8,256]{2,1,0:T(8,128)S(1)} %broadcast_in_dim.23), channel_id=1, replica_groups=mesh['z'=16,'x'=4,'y'=4,'c'=2] {'x','y','c'}, dimensions={0} | all-to-all | bytes 524288 | tf_op jit(solution)/shard_map/all_to_all | solution.py:463
  134.8 3.4 %shard_map.86 = (f32[24,128]{1,0:T(8,128)S(1)}, f32[3,64,128]{2,1,0:T(8,128)S(1)}, f32[64,128]{1,0:T(8,128)S(1)}, f32[8,64,128]{2,1,0:T(8,128)S(1)}) custom-call(s32[4]{0:T(128)S(1)} %pad_add_fusion.pos, f32[256,256]{1,0:T(8,128)S(1)} %bitcast.26, f32[32,168,128]{2,1,0:T(8,128)S(1)} %bitcast.23, f32[64,128]{1,0:T(8,128)S(1)} %get-tuple-element.22.coarse_right), custom_call_target="tpu_custom_call" | custom-call | tf_op jit(solution)/shard_map/pallas_call | solution.py:30
  138.2 0.7 copy-done.12
  138.9 0.7 broadcast_in_dim.24
  139.6 11.3 %all-to-all-start.4 = ((f32[16,24,128]{2,1,0:T(8,128)}), f32[16,24,128]{2,1,0:T(8,128)}, u32[]{:S(2)}, u32[]{:S(2)}) async-start(f32[16,24,128]{2,1,0:T(8,128)} %broadcast_in_dim.24), calls=%async_computation.4 | async-start | bytes 393216 | tf_op jit(solution)/shard_map/all_to_all | solution.py:463
  150.9 0.8 shard_map.87
  151.8 0.7 copy-done.16
  152.4 0.6 copy-done.18
  153.0 11.1 %all-to-all-done.4.got = f32[16,24,128]{2,1,0:T(8,128)} async-done(((f32[16,24,128]{2,1,0:T(8,128)}), f32[16,24,128]{2,1,0:T(8,128)}, u32[]{:S(2)}, u32[]{:S(2)}) %all-to-all-start.4) | async-done | bytes 196640 | tf_op jit(solution)/shard_map/all_to_all | solution.py:463
  164.1 0.9 copy-done.2
  165.1 0.9 copy-done.5
  166.0 0.9 copy-done.8
  167.0 0.9 copy-done.11
  167.9 0.9 copy-done.17
  168.9 1.7 shard_map.88
  170.6 15.8 %all_to_all.37 = f32[32,8,256]{2,1,0:T(8,128)S(1)} all-to-all(f32[32,8,256]{2,1,0:T(8,128)S(1)} %broadcast_in_dim.25), channel_id=1, replica_groups=mesh['z'=16,'x'=4,'y'=4,'c'=2] {'x','y','c'}, dimensions={0} | all-to-all | bytes 524288 | tf_op jit(solution)/shard_map/all_to_all | solution.py:463
  186.4 1.9 shard_map.89
  188.3 16.5 %all_to_all.38.got = f32[16,8,128]{2,1,0:T(8,128)S(1)} all-to-all(f32[16,8,128]{2,1,0:T(8,128)S(1)} %broadcast_in_dim.26), channel_id=1, replica_groups=mesh['z'=16,'x'=4,'y'=4,'c'=2] {'z'}, dimensions={0} | all-to-all | bytes 131072 | tf_op jit(solution)/shard_map/all_to_all | solution.py:463
  204.8 1.4 shard_map.90
  (61 shorter events, 0.2 us)
Async XLA Ops:
  0.0 32.5 %copy-start.20 = (s32[32,128]{1,0:T(8,128)S(1)}, s32[32,128]{1,0:T(8,128)}, u32[]{:S(2)}) copy-start(s32[32,128]{1,0:T(8,128)} %param.12) | copy-start | bytes 49156
  0.0 32.4 %copy-start.15 = (f32[4,32,128]{2,1,0:T(8,128)S(1)}, f32[4,32,128]{2,1,0:T(8,128)}, u32[]{:S(2)}) copy-start(f32[4,32,128]{2,1,0:T(8,128)} %right.1) | copy-start | bytes 196612
  0.0 32.5 %copy-start.21 = (f32[32,128]{1,0:T(8,128)S(1)}, f32[32,128]{1,0:T(8,128)}, u32[]{:S(2)}) copy-start(f32[32,128]{1,0:T(8,128)} %param.9) | copy-start | bytes 49156
  0.0 32.5 %copy-start.22 = (f32[32,128]{1,0:T(8,128)S(1)}, f32[32,128]{1,0:T(8,128)}, u32[]{:S(2)}) copy-start(f32[32,128]{1,0:T(8,128)} %param.10) | copy-start | bytes 49156
  0.0 32.5 %copy-start.23 = (f32[32,128]{1,0:T(8,128)S(1)}, f32[32,128]{1,0:T(8,128)}, u32[]{:S(2)}) copy-start(f32[32,128]{1,0:T(8,128)} %param.11) | copy-start | bytes 49156
  1.1 23.2 %collective-permute-start = (f32[32,128]{1,0:T(8,128)S(1)}, f32[32,128]{1,0:T(8,128)S(1)}, u32[]{:S(2)}, u32[]{:S(2)}) collective-permute-start(f32[32,128]{1,0:T(8,128)S(1)} %fusion), channel_id=1, source_target_pairs={{0,64},{32,96},{64,128},{96,160},{128,192},{160,224},{192,256},{22... | collective-permute-start | bytes 49160 | tf_op jit(solution)/shard_map/ppermute | solution.py:459
  6.8 17.5 %collective-permute-start.1 = (f32[32,128]{1,0:T(8,128)S(1)}, f32[32,128]{1,0:T(8,128)S(1)}, u32[]{:S(2)}, u32[]{:S(2)}) collective-permute-start(f32[32,128]{1,0:T(8,128)S(1)} %fusion), channel_id=1, source_target_pairs={{0,32},{32,64},{64,96},{96,128},{128,160},{160,192},{192,224},{224... | collective-permute-start | bytes 49160 | tf_op jit(solution)/shard_map/ppermute | solution.py:459
  10.4 14.0 %collective-permute-start.2 = (f32[32,128]{1,0:T(8,128)S(1)}, f32[32,128]{1,0:T(8,128)S(1)}, u32[]{:S(2)}, u32[]{:S(2)}) collective-permute-start(f32[32,128]{1,0:T(8,128)S(1)} %fusion), channel_id=1, source_target_pairs={{0,480},{32,0},{64,32},{96,64},{128,96},{160,128},{192,160},{224,1... | collective-permute-start | bytes 49160 | tf_op jit(solution)/shard_map/ppermute | solution.py:459
  16.9 7.5 %collective-permute-start.3 = (f32[32,128]{1,0:T(8,128)S(1)}, f32[32,128]{1,0:T(8,128)S(1)}, u32[]{:S(2)}, u32[]{:S(2)}) collective-permute-start(f32[32,128]{1,0:T(8,128)S(1)} %fusion), channel_id=1, source_target_pairs={{0,448},{32,480},{64,0},{96,32},{128,64},{160,96},{192,128},{224,1... | collective-permute-start | bytes 49160 | tf_op jit(solution)/shard_map/ppermute | solution.py:459
  22.7 0.8 copy-start.14
  25.7 25.2 %all-to-all-start = ((f32[16,168,128]{2,1,0:T(8,128)}), f32[16,168,128]{2,1,0:T(8,128)S(1)}, u32[]{:S(2)}, u32[]{:S(2)}) async-start(f32[16,168,128]{2,1,0:T(8,128)} %broadcast_in_dim.18), calls=%async_computation | async-start | bytes 2752512 | tf_op jit(solution)/shard_map/all_to_all | solution.py:463
  63.3 53.4 %all-to-all-start.2 = ((f32[16,24,128]{2,1,0:T(8,128)}), f32[16,24,128]{2,1,0:T(8,128)}, u32[]{:S(2)}, u32[]{:S(2)}) async-start(f32[16,24,128]{2,1,0:T(8,128)} %broadcast_in_dim.20), calls=%async_computation.2 | async-start | bytes 393216 | tf_op jit(solution)/shard_map/all_to_all | solution.py:463
  71.6 12.4 %collective-permute-start.4 = (f32[8,3,128]{2,1,0:T(4,128)S(1)}, f32[8,3,128]{2,1,0:T(4,128)S(1)}, u32[]{:S(2)}, u32[]{:S(2)}) collective-permute-start(f32[8,3,128]{2,1,0:T(4,128)S(1)} %get-tuple-element.37), channel_id=1, source_target_pairs={{0,7},{1,0},{2,1},{3,2},{4,3},{5,4},{6,5},{7,6},{8,15},{9,8},{10,9... | collective-permute-start | bytes 36872 | tf_op jit(solution)/shard_map/ppermute | solution.py:459
  72.3 13.7 %collective-permute-start.5 = (f32[8,3,128]{2,1,0:T(4,128)S(1)}, f32[8,3,128]{2,1,0:T(4,128)S(1)}, u32[]{:S(2)}, u32[]{:S(2)}) collective-permute-start(f32[8,3,128]{2,1,0:T(4,128)S(1)} %get-tuple-element.38), channel_id=1, source_target_pairs={{0,1},{1,2},{2,3},{3,4},{4,5},{5,6},{6,7},{7,0},{8,9},{9,10},{10,1... | collective-permute-start | bytes 36872 | tf_op jit(solution)/shard_map/ppermute | solution.py:459
  73.4 40.5 %collective-permute-start.10 = (f32[32,2048]{1,0:T(8,128)}, f32[32,2048]{1,0:T(8,128)S(1)}, u32[]{:S(2)}, u32[]{:S(2)}) collective-permute-start(f32[32,2048]{1,0:T(8,128)} %bitcast.11.p2), channel_id=1, source_target_pairs={{0,480},{32,0},{64,32},{96,64},{128,96},{160,128},{192,160},{224,1... | collective-permute-start | bytes 786440 | tf_op jit(solution)/shard_map/ppermute | solution.py:459
  77.8 36.7 %collective-permute-start.11 = (f32[32,2048]{1,0:T(8,128)}, f32[32,2048]{1,0:T(8,128)S(1)}, u32[]{:S(2)}, u32[]{:S(2)}) collective-permute-start(f32[32,2048]{1,0:T(8,128)} %bitcast.11.p2), channel_id=1, source_target_pairs={{0,448},{32,480},{64,0},{96,32},{128,64},{160,96},{192,128},{224,1... | collective-permute-start | bytes 786440 | tf_op jit(solution)/shard_map/ppermute | solution.py:459
  81.8 33.4 %collective-permute-start.8 = (f32[32,2048]{1,0:T(8,128)}, f32[32,2048]{1,0:T(8,128)S(1)}, u32[]{:S(2)}, u32[]{:S(2)}) collective-permute-start(f32[32,2048]{1,0:T(8,128)} %bitcast.11.p2), channel_id=1, source_target_pairs={{0,64},{32,96},{64,128},{96,160},{128,192},{160,224},{192,256},{22... | collective-permute-start | bytes 786440 | tf_op jit(solution)/shard_map/ppermute | solution.py:459
  84.0 31.9 %collective-permute-start.9 = (f32[32,2048]{1,0:T(8,128)}, f32[32,2048]{1,0:T(8,128)S(1)}, u32[]{:S(2)}, u32[]{:S(2)}) collective-permute-start(f32[32,2048]{1,0:T(8,128)} %bitcast.11.p2), channel_id=1, source_target_pairs={{0,32},{32,64},{64,96},{96,128},{128,160},{160,192},{192,224},{224... | collective-permute-start | bytes 786440 | tf_op jit(solution)/shard_map/ppermute | solution.py:459
  86.1 15.0 %collective-permute-start.6 = (f32[8,40,3]{2,1,0:T(8,128)S(1)}, f32[8,40,3]{2,1,0:T(8,128)S(1)}, u32[]{:S(2)}, u32[]{:S(2)}) collective-permute-start(f32[8,40,3]{2,1,0:T(8,128)S(1)} %get-tuple-element.35), channel_id=1, source_target_pairs={{0,504},{8,0},{16,8},{24,16},{32,24},{40,32},{48,40},{56,48},{64,5... | collective-permute-start | bytes 11528 | tf_op jit(solution)/shard_map/ppermute | solution.py:459
  101.1 11.6 %collective-permute-start.7 = (f32[8,40,3]{2,1,0:T(8,128)S(1)}, f32[8,40,3]{2,1,0:T(8,128)S(1)}, u32[]{:S(2)}, u32[]{:S(2)}) collective-permute-start(f32[8,40,3]{2,1,0:T(8,128)S(1)} %get-tuple-element.36), channel_id=1, source_target_pairs={{0,8},{8,16},{16,24},{24,32},{32,40},{40,48},{48,56},{56,64},{64,7... | collective-permute-start | bytes 11528 | tf_op jit(solution)/shard_map/ppermute | solution.py:459
  113.8 0.7 copy-start
  114.6 0.7 copy-start.3
  115.3 0.7 copy-start.6
  116.0 0.7 copy-start.9
  116.7 1.0 copy-start.1
  117.7 0.9 copy-start.4
  118.6 0.9 copy-start.7
  119.6 0.9 copy-start.10
  138.2 0.7 copy-start.12
  139.6 24.5 %all-to-all-start.4 = ((f32[16,24,128]{2,1,0:T(8,128)}), f32[16,24,128]{2,1,0:T(8,128)}, u32[]{:S(2)}, u32[]{:S(2)}) async-start(f32[16,24,128]{2,1,0:T(8,128)} %broadcast_in_dim.24), calls=%async_computation.4 | async-start | bytes 393216 | tf_op jit(solution)/shard_map/all_to_all | solution.py:463
  151.7 0.7 copy-start.16
  152.4 0.6 copy-start.18
  164.1 1.0 copy-start.2
  165.1 0.9 copy-start.5
  166.0 0.9 copy-start.8
  167.0 0.9 copy-start.11
  167.9 0.9 copy-start.17
  168.9 17.5 %copy-start.13 = (f32[8,64,128]{2,1,0:T(8,128)S(1)}, f32[8,64,128]{2,1,0:T(8,128)}, u32[]{:S(2)}) copy-start(f32[8,64,128]{2,1,0:T(8,128)} %copy-done.12) | copy-start | bytes 786436
  170.5 34.2 %copy-start.19 = (f32[4,32,128]{2,1,0:T(8,128)S(1)}, f32[4,32,128]{2,1,0:T(8,128)}, u32[]{:S(2)}) copy-start(f32[4,32,128]{2,1,0:T(8,128)} %copy-done.18) | copy-start | bytes 196612

commit v2 on v1

--- a/solution.py
+++ b/solution.py
@@ -1,5 +1,3 @@
-import functools
-
 import jax
 import jax.numpy as jnp
 from jax import lax
@@ -22,14 +20,15 @@
 EXT_COLS = 256
 NT = (((1,), (1,)), ((), ()))
 NN = (((1,), (0,)), ((), ()))
-VMEM_BYTES = 40 * 1024 * 1024
+VMEM_BYTES = 12 * 1024 * 1024
 
 
 def call(kernel, outs, pos, *arrays):
+    outs = [o if o[1] == BF16 else (o, F32) for o in outs]
     vmem = pl.BlockSpec(memory_space=pltpu.VMEM)
     return pl.pallas_call(
         kernel,
-        out_shape=[jax.ShapeDtypeStruct(s, F32) for s in outs],
+        out_shape=[jax.ShapeDtypeStruct(s, d) for s, d in outs],
         in_specs=[pl.BlockSpec(memory_space=pltpu.SMEM)] + [vmem] * len(arrays),
         out_specs=[vmem] * len(outs),
         compiler_params=pltpu.CompilerParams(vmem_limit_bytes=VMEM_BYTES),
@@ -130,16 +129,73 @@
     return value[:ROWS, :COLS]
 
 
-def coarse_kernel(pos, right, wet, act, out):
-    mask = wet[...]
-    rows = block_sums([right[m] * mask for m in range(M)])
-    own = lane_group() == pos[1]
-    out[...] = jnp.where(own, member_rows(rows) * act[...], 0.0)
-
-
-def fields_kernel(pos, ext, act, consts, early):
-    b = pos[2]
-    diag, east, north, wet = (ext[4 + i] for i in range(4))
+def start_kernel(pos, right, diag, east, north, wet, active, coupling, stack, act_out, tile, coarse):
+    mask = wet[...].astype(F32)
+    act = jnp.concatenate([jnp.broadcast_to(active[...].astype(F32), (8, 32))] * 4, axis=1)
+    act_out[...] = act
+    fields = [right[m] for m in range(M)] + [diag[...], east[...], north[...], mask]
+    for f, v in enumerate(fields):
+        stack[f] = v
+    tail = jnp.concatenate([coupling[e, 24:, :] for e in range(3)], axis=0)
+    tile[:24, :] = jnp.concatenate([coupling[e, :24, :] for e in range(3)] + [tail], axis=1)
+    every = jnp.concatenate(fields, axis=0)
+    hi = every.astype(BF16).astype(F32)
+    mid = (every - hi).astype(BF16).astype(F32)
+    parts = jnp.concatenate([hi, mid, every - hi - mid], axis=0).astype(BF16)
+    row, lane = iota((16, COLS), 0), iota((16, COLS), 1)
+    column = jnp.where(row < 8, row, row - 8 + COLS - HALO)
+    chosen = jnp.logical_and(lane == column, row % 8 < HALO).astype(F32).astype(BF16)
+    columns = mm(chosen, parts, NT)
+    columns = columns[:, :256] + columns[:, 256:512] + columns[:, 512:]
+    upper = iota((8, 128), 0) >= 4
+    for i in range(2):
+        part = columns[8 * i : 8 * i + 8]
+        tile[24 + 8 * i : 32 + 8 * i, :] = jnp.where(upper, roll(part[:, 128:], 4, 0), part[:, :128])
+    rows = block_sums([fields[m] * mask for m in range(M)])
+    coarse[...] = jnp.where(lane_group() == pos[1], member_rows(rows) * act, 0.0)
+
+
+def gather_kernel(pos, t0, t1, t2, t3, t4, coarse, out):
+    x = pos[1]
+    onward = jnp.where(x == NX - 1, t1[32:40, :], t2[32:40, :])
+    back = jnp.where(x == 0, t3[24:32, :], t2[24:32, :])
+    tiles = [t[:24, :] for t in (t0, t1, t2, t3, t4)]
+    rows = jnp.concatenate(tiles + [coarse[...]], axis=0)
+    for d in range(NX * 4):
+        out[d, :128, :] = rows
+        out[d, 128:, :] = jnp.where(lax.rem(x + 1, NX) == d // 4, onward, back)
+
+
+def side(blocks, band, sender):
+    return blocks[lax.rem(band, 2) * 16 + sender * 4 + lax.div(band, 2), 128:136, :]
+
+
+def fields_kernel(pos, stack, north_rows, south_rows, blocks, act, ext, consts, early):
+    x, b = pos[1], pos[2]
+    after, before = lax.rem(x + 1, NX), lax.rem(x + NX - 1, NX)
+    sides = []
+    for band in (b, lax.rem(b + 1, NB), lax.rem(b + NB - 1, NB)):
+        sides += [side(blocks, band, after), side(blocks, band, before)]
+    turned = jnp.transpose(jnp.concatenate(sides + [jnp.zeros((80, 128), F32)], axis=0))
+    first = iota((8, 128), 0) < 4
+
+    def columns(rows, slot, h):
+        lane = iota(rows.shape, 1)
+        east_part = roll(rows, -(16 * slot + 4 * h), 1)
+        west_part = roll(rows, 128 - HALO - (16 * slot + 8 + 4 * h), 1)
+        return jnp.where(lane < HALO, east_part, jnp.where(lane >= 128 - HALO, west_part, 0.0))
+
+    fields = []
+    for f in range(8):
+        rows = turned[32 * (f % 4) : 32 * (f % 4) + 32]
+        h = f // 4
+        corner = jnp.where(first, columns(rows[:8], 1, h), columns(rows[24:], 2, h))
+        left = jnp.concatenate([stack[f], jnp.where(first, north_rows[f], south_rows[f])], axis=0)
+        right = jnp.concatenate([columns(rows, 0, h), corner], axis=0)
+        fields.append(jnp.concatenate([left, right], axis=1))
+    for m in range(M):
+        ext[m] = fields[m]
+    diag, east, north, wet = fields[4:]
     row = iota((EXT_ROWS, EXT_COLS), 0)
     grid_row = b * ROWS + jnp.where(row >= 36, row - EXT_ROWS, row)
     inside = jnp.logical_and(grid_row >= 0, grid_row < NB * ROWS - 1)
@@ -164,7 +220,7 @@
     ]
     energy, smooth = [], []
     for m in range(M):
-        r = ext[m]
+        r = fields[m]
         y = inverse * r
         image = main(operate(y, (fe, fw, fn, fs, centre)))
         sums.append(mask * image)
@@ -174,17 +230,28 @@
     lane = iota((8, 128), 1) % 32
     scalars = jnp.where(lane == 0, member_rows(energy), jnp.where(lane == 1, member_rows(smooth), 0.0))
     early[0] = pick([member_rows(rows[5:])] * 2 + [jnp.broadcast_to(rows[0], (8, 128)), jnp.broadcast_to(rows[1], (8, 128))])
-    early[1] = pick([jnp.broadcast_to(rows[i], (8, 128)) for i in (2, 3, 4)] + [jnp.broadcast_to(act[...], (8, 128))])
+    early[1] = pick([jnp.broadcast_to(rows[i], (8, 128)) for i in (2, 3, 4)] + [act[...]])
     early[2] = scalars
 
 
-def weights(blocks, b, g):
+def unpack_tile(tile, x):
+    group = iota((24, 128), 1) // 32
+    top = roll(jnp.where(group < 3, tile, 0.0), 32 * (x - 1), 1)
+    group = lane_group()
+    rest = jnp.zeros((8, 128), F32)
+    for e in range(3):
+        to = (e + x - 1) % 4
+        rest = jnp.where(group == to, roll(tile[8 * e : 8 * e + 8], 32 * (to - 3), 1), rest)
+    return jnp.concatenate([top, rest], axis=0)
+
+
+def unpack_weights(blocks, b, g):
     c, y = b % 2, b // 2
-    block = jnp.concatenate([blocks[c * 16 + x * 4 + y, 32 * g : 32 * g + 32, :] for x in range(NX)], axis=0)
-    return halves(block)
-
-
-def forward_sweep(coarse, blocks, mine):
+    tiles = [unpack_tile(blocks[c * 16 + x * 4 + y, 24 * g : 24 * g + 24, :], x) for x in range(NX)]
+    return halves(jnp.concatenate(tiles, axis=0))
+
+
+def forward_sweep(coarse, weights, mine):
     group = lane_group()
     zero = jnp.zeros((8, 128), F32)
     s = [zero, zero, coarse[0], zero, zero]
@@ -197,7 +264,7 @@
             lhs = jnp.concatenate(
                 [jnp.where(group == 3, left, s[g]), s[g], s[g], jnp.where(group == 0, right, s[g])], axis=0
             )
-            hi, lo = weights(blocks, b, g)
+            hi, lo = weights(b, g)
             o = dot3(lhs, hi, lo, NT)
             carried = pick([o[8 * x : 8 * x + 8] for x in range(NX)])
             new.append(coarse[b] - carried if g == 2 else -carried)
@@ -206,7 +273,7 @@
     return out
 
 
-def backward_sweep(pivoted, blocks):
+def backward_sweep(pivoted, weights):
     group = lane_group()
     zero = jnp.zeros((8, 128), F32)
     s = pivoted[NB - 1]
@@ -216,7 +283,7 @@
         o = []
         for g in range(NG):
             lhs = jnp.concatenate([jnp.where(group == x, s[g], 0.0) for x in range(NX)], axis=0)
-            hi, lo = weights(blocks, b + 1, g)
+            hi, lo = weights(b + 1, g)
             o.append(dot3(lhs, hi, lo, NN))
         s = []
         for g in range(NG):
@@ -231,19 +298,30 @@
 
 
 def pack_window(s, extra, out):
-    upper = iota((8, 128), 0) >= 4
-    parts = list(s) + [extra]
-    for i in range(3):
-        out[8 * i : 8 * i + 8, :] = jnp.where(upper, roll(parts[2 * i + 1], 4, 0), parts[2 * i])
+    parts = [jnp.where(lane_group() == 0, extra, s[0])] + list(s[1:])
+    for g in range(NG):
+        rows = parts[g][:4]
+        for z in range(NZ):
+            out[z, g] = rows
+
+
+def to_plane(first, second, out):
+    rows = out.shape[1]
+    for i in range(NX * NB):
+        out[i, :, :128] = first[:rows]
+        out[i, :, 128:] = second[:rows]
 
 
 def unpack_swept(got):
+    reached = iota((4, 128), 1) >= 32
     out = []
     for z in range(NZ):
-        even = got[(z + 2) % NZ, 0:8, :] + got[z, 8:16, :] + got[(z - 2) % NZ, 16:24, :]
-        odd = got[(z + 1) % NZ, 0:8, :] + got[(z - 1) % NZ, 8:16, :]
-        out.append(even + roll(odd, 4, 0))
-    return jnp.concatenate(out, axis=1)
+        acc = jnp.where(reached, got[(z + 2) % NZ, 0], 0.0)
+        for g in range(1, NG):
+            acc = acc + got[(z + 2 - g) % NZ, g]
+        out.append(acc)
+    out = jnp.concatenate(out, axis=1)
+    return jnp.concatenate([out, jnp.zeros_like(out)], axis=0)
 
 
 def pivot_product(swept, pivots):
@@ -258,7 +336,10 @@
     half = field // 4 * 128
     out = None
     for x in range(NX):
-        piece = roll(got[64 * x : 64 * x + 64, half : half + 128], 32 * (x - field % 4), 1)
+        bands = [got[x * NB + b, :, half : half + 128] for b in range(NB)]
+        if got.shape[1] == 4:
+            bands = [jnp.concatenate([v, jnp.zeros_like(v)], axis=0) for v in bands]
+        piece = roll(jnp.concatenate(bands, axis=0), 32 * (x - field % 4), 1)
         out = piece if out is None else jnp.where(group == x, piece, out)
     return out
 
@@ -281,40 +362,51 @@
     return jnp.sum(acc, axis=1, keepdims=True)
 
 
-def forward_kernel(pos, blocks, act, out, coarse_out):
+def stored(w_hi, w_lo):
+    return lambda b, g: (w_hi[b * NG + g], w_lo[b * NG + g])
+
+
+def forward_kernel(pos, blocks, act, out, coarse_out, w_hi, w_lo):
     coarse = []
     for b in range(NB):
         c, y = b % 2, b // 2
-        acc = blocks[c * 16 + y, 160:168, :]
+        acc = blocks[c * 16 + y, 120:128, :]
         for x in range(1, NX):
-            acc = acc + blocks[c * 16 + x * 4 + y, 160:168, :]
+            acc = acc + blocks[c * 16 + x * 4 + y, 120:128, :]
         coarse.append(acc)
         coarse_out[8 * b : 8 * b + 8, :] = acc
-    s = forward_sweep(coarse, blocks, pos[2])
-    pack_window(s, jnp.broadcast_to(act[...], (8, 128)), out)
+
+    def weights(b, g):
+        hi, lo = unpack_weights(blocks, b, g)
+        w_hi[b * NG + g] = hi
+        w_lo[b * NG + g] = lo
+        return hi, lo
+
+    s = forward_sweep(coarse, weights, pos[2])
+    pack_window(s, act[...], out)
 
 
 def pivot_kernel(pos, got, early, p0, p1, p2, p3, p4, out):
     z = pos[0]
     first, last = pivot_product(unpack_swept(got), (p0, p1, p2, p3, p4))
-    act_before = jnp.broadcast_to(got[lax.rem(z + NZ - 1, NZ), 20:21, :], (8, 128))
-    act_after = jnp.broadcast_to(got[lax.rem(z + 1, NZ), 20:21, :], (8, 128))
+    act_before, act_after = (
+        jnp.broadcast_to(got[lax.rem(z + by, NZ), 0][:1], (8, 128)) for by in (NZ - 1, 1)
+    )
     group = lane_group()
     upper = iota((8, 128), 0) >= 4
     second = jnp.where(group == 0, last, early[0])
-    fourth = pick([act_before, act_after, early[2], jnp.zeros((8, 128), F32)])
-    out[:, :128] = jnp.where(upper, roll(early[1], 4, 0), first)
-    out[:, 128:] = jnp.where(upper, roll(fourth, 4, 0), second)
+    fourth = pick([act_before, roll(act_after, 32, 1), early[2], jnp.zeros((8, 128), F32)])
+    to_plane(jnp.where(upper, roll(early[1], 4, 0), first), jnp.where(upper, roll(fourth, 4, 0), second), out)
 
 
 def upper_half(value):
     return roll(value, -4, 0)
 
 
-def middle_kernel(pos, got, blocks, coarse_right, out, s_out, coarse_image_out, t_out):
+def middle_kernel(pos, got, w_hi, w_lo, coarse_right, out, s_out, coarse_image_out, t_out):
     windows = [unpack_plane(got, f) for f in range(8)]
     pivoted = [[windows[g][8 * b : 8 * b + 8] for g in range(NG)] for b in range(NB)]
-    settled = backward_sweep(pivoted, blocks)
+    settled = backward_sweep(pivoted, stored(w_hi, w_lo))
     act = upper_half(windows[3])
     s1, s2, s3 = (
         jnp.concatenate([settled[b][g] for b in range(NB)], axis=0) * a
@@ -338,7 +430,7 @@
         t_out[i] = v
     t_out[6] = upper_half(windows[4])
     t_out[7] = upper_half(windows[5])
-    s = forward_sweep([coarse_image[8 * b : 8 * b + 8] for b in range(NB)], blocks, pos[2])
+    s = forward_sweep([coarse_image[8 * b : 8 * b + 8] for b in range(NB)], stored(w_hi, w_lo), pos[2])
     pack_window(s, extra, out)
 
 
@@ -379,10 +471,10 @@
 
 def step_kernel(pos, got, ext, consts, image, p0, p1, p2, p3, p4, out, smooth_out, scalar_out):
     first, last = pivot_product(unpack_swept(got), (p0, p1, p2, p3, p4))
-    sums = got[0, 16:24, :]
+    sums = got[0, 0]
     for z in range(1, NZ):
-        sums = sums + got[z, 16:24, :]
-    sums = upper_half(sums)
+        sums = sums + got[z, 0]
+    sums = jnp.concatenate([sums, jnp.ones_like(sums)], axis=0)
     weight, energy = sums[:, 0:1], sums[:, 1:2]
     step = weight / energy
     fields = tuple(consts[i] for i in range(5))
@@ -404,16 +496,15 @@
     scalars = jnp.zeros((8, 128), F32)
     for i in range(3):
         scalars = jnp.where(lane == i, member_rows(dots[i]), scalars)
-    out[:, :128] = first
-    out[:, 128:] = pick([last, rows, scalars, jnp.zeros((8, 128), F32)])
+    to_plane(first, pick([last, rows, scalars, jnp.zeros((8, 128), F32)]), out)
     lane = iota((8, 128), 1)
     scalar_out[...] = jnp.where(lane == 0, weight, jnp.where(lane == 1, energy, jnp.where(lane == 2, step, 0.0)))
 
 
-def last_kernel(pos, got, blocks, s_ref, coarse_right, coarse_image, t_ref, scalar, out, s_out):
+def last_kernel(pos, got, w_hi, w_lo, s_ref, coarse_right, coarse_image, t_ref, scalar, out, s_out):
     windows = [unpack_plane(got, f) for f in range(7)]
     pivoted = [[windows[g][8 * b : 8 * b + 8] for g in range(NG)] for b in range(NB)]
-    settled = backward_sweep(pivoted, blocks)
+    settled = backward_sweep(pivoted, stored(w_hi, w_lo))
     t = tuple(t_ref[i] for i in range(5))
     step = jnp.concatenate([scalar[:, 2:3]] * NB, axis=0)
     s1, s2, s3 = (
@@ -433,21 +524,22 @@
     res = jnp.zeros((8, 128), F32)
     for i in range(3):
         res = jnp.where(lane == i, dots[i], res)
-    out[...] = res
-
-
-def finish_kernel(pos, got, scalar, pre, smooth, wet_ref, s_ref, out):
+    for z in range(NZ):
+        out[z] = res[:4]
+
+
+def finish_kernel(pos, got, scalar, pre, smooth, stack, s_ref, out):
     x, b = pos[1], pos[2]
     sums = got[0]
     for z in range(1, NZ):
         sums = sums + got[z]
     renewed, energy, cross = sums[:, 0:1], sums[:, 1:2], sums[:, 2:3]
-    weight, first_energy, step = scalar[:, 0:1], scalar[:, 1:2], scalar[:, 2:3]
+    weight, first_energy, step = scalar[:4, 0:1], scalar[:4, 1:2], scalar[:4, 2:3]
     ratio = renewed / weight
     second = renewed / (energy + 2.0 * ratio * cross + ratio * ratio * first_energy)
     own = s_ref[b]
     mains = [spread_rows(own, x, kr) for kr in range(4)]
-    mask = wet_ref[...]
+    mask = stack[7]
     for m in range(M):
         spread = jnp.concatenate([jnp.broadcast_to(v[m : m + 1], (8, 128)) for v in mains], axis=0)
         z1 = smooth[m] + mask * spread
@@ -467,49 +559,45 @@
     z, x = lax.axis_index("z"), lax.axis_index("x")
     b = 2 * lax.axis_index("y") + lax.axis_index("c")
     pos = jnp.stack([z, x, b, b]).astype(jnp.int32)
-    mask = wet.astype(F32)
-    act = jnp.tile(active[0].astype(F32), (1, 4))
-    run = functools.partial(call)
-
-    (coarse,) = run(coarse_kernel, [(8, 128)], pos, right_side, mask, act)
-    own = jnp.transpose(coupling[0, 0], (1, 0, 2)).reshape(32, 96)
-    own = jnp.roll(jnp.pad(own, ((0, 0), (0, 32))), 32 * (x - 1), axis=1)
-    window = [own if g == 2 else shift(own, "z", NZ, 2 - g) for g in range(NG)]
+    stack, act, tile, coarse = call(
+        start_kernel,
+        [(8, ROWS, COLS), (8, 128), (40, 128), (8, 128)],
+        pos, right_side, diagonal, east_face, north_face, wet, active[0], coupling[0, 0],
+    )
+    window = [tile if g == 2 else shift(tile if g in (1, 3) else tile[:24], "z", NZ, 2 - g) for g in range(NG)]
+    (plane,) = call(gather_kernel, [(NX * 4, 136, 128)], pos, *window, coarse)
+    plane = lax.all_to_all(plane, ("x", "y"), 0, 0)
+    blocks = to_all(plane, "c", 2).reshape(32, 136, 128)
+
     pivot_rows = [pivots[0] if g == 2 else shift(pivots[0], "z", NZ, 2 - g) for g in range(NG)]
-    plane = to_all(jnp.concatenate(window + [coarse], axis=0), ("x", "y"), NX * 4)
-    blocks = to_all(plane, "c", 2).reshape(32, 168, 128)
-
-    stack = jnp.concatenate([right_side, jnp.stack([diagonal, east_face, north_face, mask])], axis=0)
-    south = shift(stack[:, ROWS - HALO :], ("y", "c"), NB, 1)
-    north = shift(stack[:, :HALO], ("y", "c"), NB, -1)
-    gap = jnp.zeros((8, EXT_ROWS - ROWS - 2 * HALO, COLS), F32)
-    tall = jnp.concatenate([stack, north, gap, south], axis=1)
-    west = shift(tall[:, :, COLS - HALO :], ("z", "x"), NZ * NX, 1)
-    east = shift(tall[:, :, :HALO], ("z", "x"), NZ * NX, -1)
-    gap = jnp.zeros((8, EXT_ROWS, EXT_COLS - COLS - 2 * HALO), F32)
-    ext = jnp.concatenate([tall, east, gap, west], axis=2)
-
-    swept, coarse_right = run(forward_kernel, [(24, 128), (64, 128)], pos, blocks, act)
-    got = to_all(swept, "z", NZ)
-    consts, early = run(fields_kernel, [(7, EXT_ROWS, EXT_COLS), (3, 8, 128)], pos, ext, act)
-    (message,) = run(pivot_kernel, [(8, 256)], pos, got, early, *pivot_rows)
-    got = to_all(message, ("x", "y", "c"), 32).reshape(256, 256)
-    swept, s0, coarse_image, t = run(
-        middle_kernel, [(24, 128), (3, 64, 128), (64, 128), (8, 64, 128)], pos, got, blocks, coarse_right
-    )
-    got = to_all(swept, "z", NZ)
-    pre, image = run(
-        image_kernel, [(M, ROWS, COLS), (M, EXT_ROWS, EXT_COLS)], pos, ext, consts, s0.reshape(3, NB, 8, 128)
-    )
-    message, smooth, scalar = run(
-        step_kernel, [(8, 256), (M, ROWS, COLS), (8, 128)], pos, got, ext, consts, image, *pivot_rows
-    )
-    got = to_all(message, ("x", "y", "c"), 32).reshape(256, 256)
-    dots, s1 = run(last_kernel, [(8, 128), (64, 128)], pos, got, blocks, s0, coarse_right, coarse_image, t, scalar)
-    got = to_all(dots, "z", NZ)
-    (out,) = run(
-        finish_kernel, [(M, ROWS, COLS)], pos, got, scalar, pre, smooth, mask, s1.reshape(NB, 8, 128)
-    )
+    south = shift(stack[:, ROWS - 8 :], ("y", "c"), NB, 1)
+    north = shift(stack[:, :8], ("y", "c"), NB, -1)
+
+    ring, rim = (NZ, NG, 4, 128), (M, EXT_ROWS, EXT_COLS)
+    weights = ((NB * NG, 128, 128), BF16)
+    ext, consts, early = call(
+        fields_kernel, [rim, (7, EXT_ROWS, EXT_COLS), (3, 8, 128)], pos, stack, north, south, blocks, act
+    )
+    swept, coarse_right, w_hi, w_lo = call(forward_kernel, [ring, (64, 128), weights, weights], pos, blocks, act)
+    swept, early, pivot_rows = lax.optimization_barrier((swept, early, pivot_rows))
+    got = lax.all_to_all(swept, "z", 0, 0)
+    (message,) = call(pivot_kernel, [(32, 8, 256)], pos, got, early, *pivot_rows)
+    got = lax.all_to_all(message, ("x", "y", "c"), 0, 0)
+    swept, s0, coarse_image, t = call(
+        middle_kernel, [ring, (3, 64, 128), (64, 128), (8, 64, 128)], pos, got, w_hi, w_lo, coarse_right
+    )
+    pre, image = call(image_kernel, [(M, ROWS, COLS), rim], pos, ext, consts, s0.reshape(3, NB, 8, 128))
+    swept, pre, image = lax.optimization_barrier((swept, pre, image))
+    got = lax.all_to_all(swept, "z", 0, 0)
+    message, smooth, scalar = call(
+        step_kernel, [(32, 4, 256), (M, ROWS, COLS), (8, 128)], pos, got, ext, consts, image, *pivot_rows
+    )
+    got = lax.all_to_all(message, ("x", "y", "c"), 0, 0)
+    dots, s1 = call(
+        last_kernel, [(NZ, 4, 128), (64, 128)], pos, got, w_hi, w_lo, s0, coarse_right, coarse_image, t, scalar
+    )
+    got = lax.all_to_all(dots, "z", 0, 0)
+    (out,) = call(finish_kernel, [(M, ROWS, COLS)], pos, got, scalar, pre, smooth, stack, s1.reshape(NB, 8, 128))
     return out
 
 

time: 207 us -> 164 us (0.79)
  waiting for transfers between devices: 49.2 us -> 4.24 us
  blocking collectives: 54.4 us -> 93.1 us
  starting transfers between devices: 67.5 us -> 44.6 us
  local copies, waits for them, and re-layouts: 18.3 us -> 5.32 us
    all_to_all x0 -> x5, blocking collectives: none -> 87.4 us  [the longest x2 38.5 us: body(): got = lax.all_to_all(swept, 'z', 0, 0)]
    all_to_all x4 -> x1, blocking collectives: 54.4 us -> 5.66 us  [to_all(): lax.all_to_all(jnp.broadcast_to(value[None], (count,) + value.shape), axe...]
    all_to_all x3 -> x1, waiting for transfers between devices: 29.5 us -> 0.01 us  [body(): plane = lax.all_to_all(plane, ('x', 'y'), 0, 0)]
    all_to_all x3 -> x1, starting transfers between devices: 26.3 us -> 6.89 us  [body(): plane = lax.all_to_all(plane, ('x', 'y'), 0, 0)]
    ppermute x12 -> x10, waiting for transfers between devices: 19.7 us -> 4.24 us  [shift(): lax.ppermute(value, axes, [(i, (i + by) % count) for i in range(count)])]
    unnamed x56 -> x16, local copies, waits for them, and re-layouts: 14.2 us -> 5.16 us
    ppermute x12 -> x10, starting transfers between devices: 41.2 us -> 37.7 us  [shift(): lax.ppermute(value, axes, [(i, (i + by) % count) for i in range(count)])]
    broadcast_in_dim x7 -> x1, local copies, waits for them, and re-layouts: 2.85 us -> 0.14 us  [to_all(): jnp.broadcast_to(value[None], (count,) + value.shape)]
  transfers between devices with their start and end apart: 15 -> 11, of which waited for: 4 -> 2; matrix products, arithmetic and copies ran while one was open for 1% -> 0% of each run, Pallas kernels for 1% -> 2%
where the time goes in v2:
time: 164 us; the launch traced here: 163 us
  blocking collectives  93.1 us (57%)
  starting transfers between devices  44.6 us (27%)
  Pallas kernels  15.5 us (9%)
  local copies, waits for them, and re-layouts  5.32 us (3%)
  waiting for transfers between devices  4.24 us (3%)
    all_to_all x2, blocking collectives, body(): got = lax.all_to_all(swept, 'z', 0, 0)  38.5 us
    ppermute x10, starting transfers between devices, shift(): lax.ppermute(value, axes, [(i, (i + by) % count) for i in range(count)])  37.7 us
    all_to_all x2, blocking collectives, body(): got = lax.all_to_all(message, ('x', 'y', 'c'), 0, 0)  33.1 us
    all_to_all x1, blocking collectives, body(): got = lax.all_to_all(dots, 'z', 0, 0)  15.8 us
    pallas_call x10, Pallas kernels, call(): pl.pallas_call(kernel, out_shape=[jax.ShapeDtypeStruct(s, d) for s, d in...  15.5 us
    all_to_all x1, starting transfers between devices, body(): plane = lax.all_to_all(plane, ('x', 'y'), 0, 0)  6.89 us
    all_to_all x1, blocking collectives, to_all(): lax.all_to_all(jnp.broadcast_to(value[None], (count,) + value.shape), axe...  5.66 us
    unnamed x16, local copies, waits for them, and re-layouts  5.16 us
  transfers between devices with their start and end apart: 11, of which 2 were waited for; matrix products, arithmetic and copies ran while one was open for 0% of the time, Pallas kernels for 2%

profile of v2, /device:TPU:1, one launch (start us, length us, event | category | flops | bytes accessed | tf_op | source)
XLA Modules:
  0.0 163.1 jit_solution(1941851125118458775)
XLA Ops:
  0.0 0.1 pad_add_fusion.pos
  0.1 0.0 copy-start.1
  0.1 0.8 copy-done.1
  0.9 0.0 copy-start.2
  0.9 0.8 copy-done.2
  1.7 0.0 copy-start.3
  1.7 0.7 copy-done.3
  2.4 0.0 copy-start.4
  2.4 0.7 copy-done.4
  3.2 0.0 copy-start.5
  3.2 0.7 copy-done.5
  3.9 0.0 copy-start.6
  3.9 0.7 copy-done.6
  4.6 0.0 copy-start.7
  4.6 0.7 copy-done.7
  5.2 0.7 shard_map.82
  6.0 4.4 %collective-permute-start.1 = (f32[40,128]{1,0:T(8,128)S(1)}, f32[40,128]{1,0:T(8,128)S(1)}, u32[]{:S(2)}, u32[]{:S(2)}) collective-permute-start(f32[40,128]{1,0:T(8,128)S(1)} %get-tuple-element.37.t2), channel_id=1, source_target_pairs={{0,32},{32,64},{64,96},{96,128},{128,160},{160,192},{192,224},{224... | collective-permute-start | bytes 61448 | tf_op jit(solution)/shard_map/ppermute | solution.py:551
  10.4 9.5 %collective-permute-start.2 = (f32[40,128]{1,0:T(8,128)S(1)}, f32[40,128]{1,0:T(8,128)S(1)}, u32[]{:S(2)}, u32[]{:S(2)}) collective-permute-start(f32[40,128]{1,0:T(8,128)S(1)} %get-tuple-element.37.t2), channel_id=1, source_target_pairs={{0,480},{32,0},{64,32},{96,64},{128,96},{160,128},{192,160},{224,1... | collective-permute-start | bytes 61448 | tf_op jit(solution)/shard_map/ppermute | solution.py:551
  19.9 1.9 %collective-permute-start = (f32[24,128]{1,0:T(8,128)S(1)}, f32[24,128]{1,0:T(8,128)S(1)}, u32[]{:S(2)}, u32[]{:S(2)}) collective-permute-start(f32[24,128]{1,0:T(8,128)S(1)} %slice.10), channel_id=1, source_target_pairs={{0,64},{32,96},{64,128},{96,160},{128,192},{160,224},{192,256},{22... | collective-permute-start | bytes 36872 | tf_op jit(solution)/shard_map/ppermute | solution.py:551
  21.8 5.5 %collective-permute-start.3 = (f32[24,128]{1,0:T(8,128)S(1)}, f32[24,128]{1,0:T(8,128)S(1)}, u32[]{:S(2)}, u32[]{:S(2)}) collective-permute-start(f32[24,128]{1,0:T(8,128)S(1)} %slice.10), channel_id=1, source_target_pairs={{0,448},{32,480},{64,0},{96,32},{128,64},{160,96},{192,128},{224,1... | collective-permute-start | bytes 36872 | tf_op jit(solution)/shard_map/ppermute | solution.py:551
  27.3 0.0 collective-permute-done.t0
  27.3 0.8 collective-permute-done.3.t4
  28.1 0.0 collective-permute-done.1.t1
  28.1 0.0 collective-permute-done.2.t3
  28.1 1.6 shard_map.83
  29.7 0.0 copy-start
  29.7 6.9 %all-to-all-start = ((f32[16,136,128]{2,1,0:T(8,128)}), f32[16,136,128]{2,1,0:T(8,128)S(1)}, u32[]{:S(2)}, u32[]{:S(2)}) async-start(f32[16,136,128]{2,1,0:T(8,128)} %shard_map.83), calls=%async_computation | async-start | bytes 2228224 | tf_op jit(solution)/shard_map/all_to_all | solution.py:569
  36.6 0.0 copy-done
  36.6 2.8 %collective-permute-start.6 = (f32[32,2048]{1,0:T(8,128)S(1)}, f32[32,2048]{1,0:T(8,128)S(1)}, u32[]{:S(2)}, u32[]{:S(2)}) collective-permute-start(f32[32,2048]{1,0:T(8,128)S(1)} %bitcast.11), channel_id=1, source_target_pairs={{0,64},{32,96},{64,128},{96,160},{128,192},{160,224},{192,256},{22... | collective-permute-start | bytes 786440 | tf_op jit(solution)/shard_map/ppermute | solution.py:551
  39.4 3.2 %collective-permute-start.7 = (f32[32,2048]{1,0:T(8,128)S(1)}, f32[32,2048]{1,0:T(8,128)S(1)}, u32[]{:S(2)}, u32[]{:S(2)}) collective-permute-start(f32[32,2048]{1,0:T(8,128)S(1)} %bitcast.12), channel_id=1, source_target_pairs={{0,32},{32,64},{64,96},{96,128},{128,160},{160,192},{192,224},{224... | collective-permute-start | bytes 786440 | tf_op jit(solution)/shard_map/ppermute | solution.py:551
  42.6 3.3 %collective-permute-start.8 = (f32[32,2048]{1,0:T(8,128)S(1)}, f32[32,2048]{1,0:T(8,128)S(1)}, u32[]{:S(2)}, u32[]{:S(2)}) collective-permute-start(f32[32,2048]{1,0:T(8,128)S(1)} %bitcast.13), channel_id=1, source_target_pairs={{0,480},{32,0},{64,32},{96,64},{128,96},{160,128},{192,160},{224,1... | collective-permute-start | bytes 786440 | tf_op jit(solution)/shard_map/ppermute | solution.py:551
  46.0 3.6 %collective-permute-start.9 = (f32[32,2048]{1,0:T(8,128)S(1)}, f32[32,2048]{1,0:T(8,128)S(1)}, u32[]{:S(2)}, u32[]{:S(2)}) collective-permute-start(f32[32,2048]{1,0:T(8,128)S(1)} %bitcast.14), channel_id=1, source_target_pairs={{0,448},{32,480},{64,0},{96,32},{128,64},{160,96},{192,128},{224,1... | collective-permute-start | bytes 786440 | tf_op jit(solution)/shard_map/ppermute | solution.py:551
  49.6 3.5 %collective-permute-start.4 = (f32[8,8,128]{2,1,0:T(8,128)S(1)}, f32[8,8,128]{2,1,0:T(8,128)S(1)}, u32[]{:S(2)}, u32[]{:S(2)}) collective-permute-start(f32[8,8,128]{2,1,0:T(8,128)S(1)} %get-tuple-element.70), channel_id=1, source_target_pairs={{0,7},{1,0},{2,1},{3,2},{4,3},{5,4},{6,5},{7,6},{8,15},{9,8},{10,9... | collective-permute-start | bytes 98312 | tf_op jit(solution)/shard_map/ppermute | solution.py:551
  53.1 3.4 %collective-permute-done.4.north_rows = f32[8,8,128]{2,1,0:T(8,128)S(1)} collective-permute-done((f32[8,8,128]{2,1,0:T(8,128)S(1)}, f32[8,8,128]{2,1,0:T(8,128)S(1)}, u32[]{:S(2)}, u32[]{:S(2)}) %collective-permute-start.4) | collective-permute-done | bytes 32800 | tf_op jit(solution)/shard_map/ppermute | solution.py:551
  56.6 0.0 collective-permute-start.5
  56.6 0.0 all-to-all-done
  56.6 0.1 broadcast_in_dim.2
  56.7 5.7 %all_to_all.35 = f32[2,16,136,128]{3,2,1,0:T(8,128)S(1)} all-to-all(f32[2,16,136,128]{3,2,1,0:T(8,128)S(1)} %broadcast_in_dim.2), channel_id=1, replica_groups=mesh['z'=16,'x'=4,'y'=4,'c'=2] {'c'}, dimensions={0} | all-to-all | bytes 4456448 | tf_op jit(solution)/shard_map/all_to_all | solution.py:555
  62.4 2.2 %shard_map.84 = (f32[16,5,4,128]{3,2,1,0:T(4,128)S(1)}, f32[64,128]{1,0:T(8,128)S(1)}, bf16[40,128,128]{2,1,0:T(8,128)(2,1)S(1)}, bf16[40,128,128]{2,1,0:T(8,128)(2,1)S(1)}) custom-call(s32[4]{0:T(128)S(1)} %pad_add_fusion.pos, f32[32,136,128]{2,1,0:T(8,128)S(1)} %bitcast.9, f32[8,128]{1,0:T(8,128)S(1)} %get-tuple-element.39.act), custom_call_target="tpu_custom_call" | custom-call | tf_op jit(solution)/shard_map/pallas_call | solution.py:29
  64.6 0.0 collective-permute-done.5.south_rows
  64.6 1.2 shard_map.85
  65.8 0.0 collective-permute-done.6.p0
  65.8 0.0 collective-permute-done.7.p1
  65.8 0.0 collective-permute-done.8.p3
  65.8 0.0 collective-permute-done.9.p4
  65.8 21.4 %all_to_all.36.got = f32[16,5,4,128]{3,2,1,0:T(4,128)S(1)} all-to-all(f32[16,5,4,128]{3,2,1,0:T(4,128)S(1)} %get-tuple-element.43), channel_id=1, replica_groups=mesh['z'=16,'x'=4,'y'=4,'c'=2] {'z'}, dimensions={0} | all-to-all | bytes 327680 | tf_op jit(solution)/shard_map/all_to_all | solution.py:583
  87.2 1.1 shard_map.86
  88.3 18.9 %all_to_all.37.got = f32[32,8,256]{2,1,0:T(8,128)S(1)} all-to-all(f32[32,8,256]{2,1,0:T(8,128)S(1)} %shard_map.86), channel_id=1, replica_groups=mesh['z'=16,'x'=4,'y'=4,'c'=2] {'x','y','c'}, dimensions={0} | all-to-all | bytes 524288 | tf_op jit(solution)/shard_map/all_to_all | solution.py:585
  107.2 3.4 %shard_map.87 = (f32[16,5,4,128]{3,2,1,0:T(4,128)S(1)}, f32[3,64,128]{2,1,0:T(8,128)S(1)}, f32[64,128]{1,0:T(8,128)S(1)}, f32[8,64,128]{2,1,0:T(8,128)S(1)}) custom-call(s32[4]{0:T(128)S(1)} %pad_add_fusion.pos, f32[32,8,256]{2,1,0:T(8,128)S(1)} %all_to_all.37.got, bf16[40,128,128]{2,1,0:T(8,128)(2,1)S(1)} %get-tuple-element.50.w_hi, ...), custom_call_target="tpu_custom_call" | custom-call | tf_op jit(solution)/shard_map/pallas_call | solution.py:29
  110.6 0.8 shard_map.88
  111.4 17.1 %all_to_all.38.got = f32[16,5,4,128]{3,2,1,0:T(4,128)S(1)} all-to-all(f32[16,5,4,128]{3,2,1,0:T(4,128)S(1)} %get-tuple-element.59), channel_id=1, replica_groups=mesh['z'=16,'x'=4,'y'=4,'c'=2] {'z'}, dimensions={0} | all-to-all | bytes 327680 | tf_op jit(solution)/shard_map/all_to_all | solution.py:591
  128.6 1.1 shard_map.89
  129.7 14.2 %all_to_all.39.got = f32[32,4,256]{2,1,0:T(4,128)S(1)} all-to-all(f32[32,4,256]{2,1,0:T(4,128)S(1)} %get-tuple-element.61), channel_id=1, replica_groups=mesh['z'=16,'x'=4,'y'=4,'c'=2] {'x','y','c'}, dimensions={0} | all-to-all | bytes 262144 | tf_op jit(solution)/shard_map/all_to_all | solution.py:595
  143.9 1.9 %shard_map.90 = (f32[16,4,128]{2,1,0:T(4,128)S(1)}, f32[64,128]{1,0:T(8,128)S(1)}) custom-call(s32[4]{0:T(128)S(1)} %pad_add_fusion.pos, f32[32,4,256]{2,1,0:T(4,128)S(1)} %all_to_all.39.got, bf16[40,128,128]{2,1,0:T(8,128)(2,1)S(1)} %get-tuple-element.50.w_hi, bf16[40,128,128]{2,1,0:T(8,128)(2,1)S(1)} %get-tuple-element.51.w_lo, ...), custom_call_target="tpu_custom_call" | custom-call | tf_op jit(solution)/shard_map/pallas_call | solution.py:29
  145.8 15.8 %all_to_all.40.got = f32[16,4,128]{2,1,0:T(4,128)S(1)} all-to-all(f32[16,4,128]{2,1,0:T(4,128)S(1)} %get-tuple-element.65), channel_id=1, replica_groups=mesh['z'=16,'x'=4,'y'=4,'c'=2] {'z'}, dimensions={0} | all-to-all | bytes 65536 | tf_op jit(solution)/shard_map/all_to_all | solution.py:599
  161.6 1.4 shard_map.91
  (2 shorter events, 0.0 us)
Async XLA Ops:
  0.1 0.8 copy-start.1
  0.9 0.8 copy-start.2
  1.7 0.7 copy-start.3
  2.4 0.7 copy-start.4
  3.2 0.7 copy-start.5
  3.9 0.7 copy-start.6
  4.6 0.7 copy-start.7
  6.0 22.1 %collective-permute-start.1 = (f32[40,128]{1,0:T(8,128)S(1)}, f32[40,128]{1,0:T(8,128)S(1)}, u32[]{:S(2)}, u32[]{:S(2)}) collective-permute-start(f32[40,128]{1,0:T(8,128)S(1)} %get-tuple-element.37.t2), channel_id=1, source_target_pairs={{0,32},{32,64},{64,96},{96,128},{128,160},{160,192},{192,224},{224... | collective-permute-start | bytes 61448 | tf_op jit(solution)/shard_map/ppermute | solution.py:551
  10.4 17.7 %collective-permute-start.2 = (f32[40,128]{1,0:T(8,128)S(1)}, f32[40,128]{1,0:T(8,128)S(1)}, u32[]{:S(2)}, u32[]{:S(2)}) collective-permute-start(f32[40,128]{1,0:T(8,128)S(1)} %get-tuple-element.37.t2), channel_id=1, source_target_pairs={{0,480},{32,0},{64,32},{96,64},{128,96},{160,128},{192,160},{224,1... | collective-permute-start | bytes 61448 | tf_op jit(solution)/shard_map/ppermute | solution.py:551
  19.9 7.4 %collective-permute-start = (f32[24,128]{1,0:T(8,128)S(1)}, f32[24,128]{1,0:T(8,128)S(1)}, u32[]{:S(2)}, u32[]{:S(2)}) collective-permute-start(f32[24,128]{1,0:T(8,128)S(1)} %slice.10), channel_id=1, source_target_pairs={{0,64},{32,96},{64,128},{96,160},{128,192},{160,224},{192,256},{22... | collective-permute-start | bytes 36872 | tf_op jit(solution)/shard_map/ppermute | solution.py:551
  21.8 6.3 %collective-permute-start.3 = (f32[24,128]{1,0:T(8,128)S(1)}, f32[24,128]{1,0:T(8,128)S(1)}, u32[]{:S(2)}, u32[]{:S(2)}) collective-permute-start(f32[24,128]{1,0:T(8,128)S(1)} %slice.10), channel_id=1, source_target_pairs={{0,448},{32,480},{64,0},{96,32},{128,64},{160,96},{192,128},{224,1... | collective-permute-start | bytes 36872 | tf_op jit(solution)/shard_map/ppermute | solution.py:551
  29.7 6.9 %copy-start = (f32[1,32,2048]{2,1,0:T(8,128)S(1)}, f32[1,32,2048]{2,1,0:T(8,128)}, u32[]{:S(2)}) copy-start(f32[1,32,2048]{2,1,0:T(8,128)} %param.15) | copy-start | bytes 786436
  29.7 26.8 %all-to-all-start = ((f32[16,136,128]{2,1,0:T(8,128)}), f32[16,136,128]{2,1,0:T(8,128)S(1)}, u32[]{:S(2)}, u32[]{:S(2)}) async-start(f32[16,136,128]{2,1,0:T(8,128)} %shard_map.83), calls=%async_computation | async-start | bytes 2228224 | tf_op jit(solution)/shard_map/all_to_all | solution.py:569
  36.6 29.2 %collective-permute-start.6 = (f32[32,2048]{1,0:T(8,128)S(1)}, f32[32,2048]{1,0:T(8,128)S(1)}, u32[]{:S(2)}, u32[]{:S(2)}) collective-permute-start(f32[32,2048]{1,0:T(8,128)S(1)} %bitcast.11), channel_id=1, source_target_pairs={{0,64},{32,96},{64,128},{96,160},{128,192},{160,224},{192,256},{22... | collective-permute-start | bytes 786440 | tf_op jit(solution)/shard_map/ppermute | solution.py:551
  39.4 26.4 %collective-permute-start.7 = (f32[32,2048]{1,0:T(8,128)S(1)}, f32[32,2048]{1,0:T(8,128)S(1)}, u32[]{:S(2)}, u32[]{:S(2)}) collective-permute-start(f32[32,2048]{1,0:T(8,128)S(1)} %bitcast.12), channel_id=1, source_target_pairs={{0,32},{32,64},{64,96},{96,128},{128,160},{160,192},{192,224},{224... | collective-permute-start | bytes 786440 | tf_op jit(solution)/shard_map/ppermute | solution.py:551
  42.6 23.2 %collective-permute-start.8 = (f32[32,2048]{1,0:T(8,128)S(1)}, f32[32,2048]{1,0:T(8,128)S(1)}, u32[]{:S(2)}, u32[]{:S(2)}) collective-permute-start(f32[32,2048]{1,0:T(8,128)S(1)} %bitcast.13), channel_id=1, source_target_pairs={{0,480},{32,0},{64,32},{96,64},{128,96},{160,128},{192,160},{224,1... | collective-permute-start | bytes 786440 | tf_op jit(solution)/shard_map/ppermute | solution.py:551
  46.0 19.9 %collective-permute-start.9 = (f32[32,2048]{1,0:T(8,128)S(1)}, f32[32,2048]{1,0:T(8,128)S(1)}, u32[]{:S(2)}, u32[]{:S(2)}) collective-permute-start(f32[32,2048]{1,0:T(8,128)S(1)} %bitcast.14), channel_id=1, source_target_pairs={{0,448},{32,480},{64,0},{96,32},{128,64},{160,96},{192,128},{224,1... | collective-permute-start | bytes 786440 | tf_op jit(solution)/shard_map/ppermute | solution.py:551
  49.6 6.9 %collective-permute-start.4 = (f32[8,8,128]{2,1,0:T(8,128)S(1)}, f32[8,8,128]{2,1,0:T(8,128)S(1)}, u32[]{:S(2)}, u32[]{:S(2)}) collective-permute-start(f32[8,8,128]{2,1,0:T(8,128)S(1)} %get-tuple-element.70), channel_id=1, source_target_pairs={{0,7},{1,0},{2,1},{3,2},{4,3},{5,4},{6,5},{7,6},{8,15},{9,8},{10,9... | collective-permute-start | bytes 98312 | tf_op jit(solution)/shard_map/ppermute | solution.py:551
  56.6 8.1 %collective-permute-start.5 = (f32[8,8,128]{2,1,0:T(8,128)S(1)}, f32[8,8,128]{2,1,0:T(8,128)S(1)}, u32[]{:S(2)}, u32[]{:S(2)}) collective-permute-start(f32[8,8,128]{2,1,0:T(8,128)S(1)} %get-tuple-element.69), channel_id=1, source_target_pairs={{0,1},{1,2},{2,3},{3,4},{4,5},{5,6},{6,7},{7,0},{8,9},{9,10},{10,1... | collective-permute-start | bytes 98312 | tf_op jit(solution)/shard_map/ppermute | solution.py:551

commit v3 on v2

--- a/solution.py
+++ b/solution.py
@@ -23,14 +23,19 @@
 VMEM_BYTES = 12 * 1024 * 1024
 
 
-def call(kernel, outs, pos, *arrays):
+def call(kernel, outs, pos, *arrays, fetch=False):
     outs = [o if o[1] == BF16 else (o, F32) for o in outs]
     vmem = pl.BlockSpec(memory_space=pltpu.VMEM)
+    scratch = []
+    if fetch:
+        scratch = [pltpu.VMEM(a.shape, a.dtype) for a in arrays] + [pltpu.SemaphoreType.DMA((len(arrays),))]
+    given = pl.BlockSpec(memory_space=pl.ANY) if fetch else vmem
     return pl.pallas_call(
         kernel,
         out_shape=[jax.ShapeDtypeStruct(s, d) for s, d in outs],
-        in_specs=[pl.BlockSpec(memory_space=pltpu.SMEM)] + [vmem] * len(arrays),
+        in_specs=[pl.BlockSpec(memory_space=pltpu.SMEM)] + [given] * len(arrays),
         out_specs=[vmem] * len(outs),
+        scratch_shapes=scratch,
         compiler_params=pltpu.CompilerParams(vmem_limit_bytes=VMEM_BYTES),
     )(pos, *arrays)
 
@@ -129,10 +134,16 @@
     return value[:ROWS, :COLS]
 
 
-def start_kernel(pos, right, diag, east, north, wet, active, coupling, stack, act_out, tile, coarse):
+def start_kernel(pos, *refs):
+    given, (stack, tile), held, sems = refs[:7], refs[7:9], refs[9:16], refs[16]
+    copies = [pltpu.make_async_copy(a, h, sems.at[i]) for i, (a, h) in enumerate(zip(given, held))]
+    for copy in copies:
+        copy.start()
+    for copy in copies:
+        copy.wait()
+    right, diag, east, north, wet, active, coupling = held
     mask = wet[...].astype(F32)
     act = jnp.concatenate([jnp.broadcast_to(active[...].astype(F32), (8, 32))] * 4, axis=1)
-    act_out[...] = act
     fields = [right[m] for m in range(M)] + [diag[...], east[...], north[...], mask]
     for f, v in enumerate(fields):
         stack[f] = v
@@ -150,17 +161,20 @@
     upper = iota((8, 128), 0) >= 4
     for i in range(2):
         part = columns[8 * i : 8 * i + 8]
-        tile[24 + 8 * i : 32 + 8 * i, :] = jnp.where(upper, roll(part[:, 128:], 4, 0), part[:, :128])
+        tile[32 + 8 * i : 40 + 8 * i, :] = jnp.where(upper, roll(part[:, 128:], 4, 0), part[:, :128])
     rows = block_sums([fields[m] * mask for m in range(M)])
-    coarse[...] = jnp.where(lane_group() == pos[1], member_rows(rows) * act, 0.0)
-
-
-def gather_kernel(pos, t0, t1, t2, t3, t4, coarse, out):
+    packed = pick([jnp.broadcast_to(r, (8, 128)) for r in rows]) * act
+    row = iota((8, 128), 0)
+    tile[24:32, :] = jnp.where(row == 0, packed, jnp.where(row == 1, act, 0.0))
+
+
+def gather_kernel(pos, t0, t1, t2, t3, t4, out):
     x = pos[1]
-    onward = jnp.where(x == NX - 1, t1[32:40, :], t2[32:40, :])
-    back = jnp.where(x == 0, t3[24:32, :], t2[24:32, :])
-    tiles = [t[:24, :] for t in (t0, t1, t2, t3, t4)]
-    rows = jnp.concatenate(tiles + [coarse[...]], axis=0)
+    onward = jnp.where(x == NX - 1, t1[40:48, :], t2[40:48, :])
+    back = jnp.where(x == 0, t3[32:40, :], t2[32:40, :])
+    tiles = (t0, t1, t2, t3, t4)
+    rows = [t[:24, :] for t in tiles] + [t[24:25, :] for t in tiles] + [t[25:26, :] for t in (t1, t2, t3)]
+    rows = jnp.concatenate(rows, axis=0)
     for d in range(NX * 4):
         out[d, :128, :] = rows
         out[d, 128:, :] = jnp.where(lax.rem(x + 1, NX) == d // 4, onward, back)
@@ -170,7 +184,7 @@
     return blocks[lax.rem(band, 2) * 16 + sender * 4 + lax.div(band, 2), 128:136, :]
 
 
-def fields_kernel(pos, stack, north_rows, south_rows, blocks, act, ext, consts, early):
+def fields_kernel(pos, stack, north_rows, south_rows, blocks, ext, consts, early):
     x, b = pos[1], pos[2]
     after, before = lax.rem(x + 1, NX), lax.rem(x + NX - 1, NX)
     sides = []
@@ -230,8 +244,7 @@
     lane = iota((8, 128), 1) % 32
     scalars = jnp.where(lane == 0, member_rows(energy), jnp.where(lane == 1, member_rows(smooth), 0.0))
     early[0] = pick([member_rows(rows[5:])] * 2 + [jnp.broadcast_to(rows[0], (8, 128)), jnp.broadcast_to(rows[1], (8, 128))])
-    early[1] = pick([jnp.broadcast_to(rows[i], (8, 128)) for i in (2, 3, 4)] + [act[...]])
-    early[2] = scalars
+    early[1] = pick([jnp.broadcast_to(rows[i], (8, 128)) for i in (2, 3, 4)] + [scalars])
 
 
 def unpack_tile(tile, x):
@@ -254,7 +267,7 @@
 def forward_sweep(coarse, weights, mine):
     group = lane_group()
     zero = jnp.zeros((8, 128), F32)
-    s = [zero, zero, coarse[0], zero, zero]
+    s = [zero if v is None else v for v in coarse[0]]
     out = s
     for b in range(1, NB):
         new = []
@@ -267,7 +280,7 @@
             hi, lo = weights(b, g)
             o = dot3(lhs, hi, lo, NT)
             carried = pick([o[8 * x : 8 * x + 8] for x in range(NX)])
-            new.append(coarse[b] - carried if g == 2 else -carried)
+            new.append(-carried if coarse[b][g] is None else coarse[b][g] - carried)
         s = new
         out = [jnp.where(mine == b, s[g], out[g]) for g in range(NG)]
     return out
@@ -305,21 +318,23 @@
             out[z, g] = rows
 
 
-def to_plane(first, second, out):
-    rows = out.shape[1]
-    for i in range(NX * NB):
-        out[i, :, :128] = first[:rows]
-        out[i, :, 128:] = second[:rows]
+def to_plane(values, out):
+    for d in range(NX * NB):
+        for i, v in enumerate(values):
+            out[d, :, 128 * i : 128 * i + 128] = v[:4]
 
 
 def unpack_swept(got):
-    reached = iota((4, 128), 1) >= 32
-    out = []
-    for z in range(NZ):
-        acc = jnp.where(reached, got[(z + 2) % NZ, 0], 0.0)
-        for g in range(1, NG):
-            acc = acc + got[(z + 2 - g) % NZ, g]
-        out.append(acc)
+    if len(got.shape) == 3:
+        out = [got[z] for z in range(NZ)]
+    else:
+        reached = iota((4, 128), 1) >= 32
+        out = []
+        for z in range(NZ):
+            acc = jnp.where(reached, got[(z + 2) % NZ, 0], 0.0)
+            for g in range(1, NG):
+                acc = acc + got[(z + 2 - g) % NZ, g]
+            out.append(acc)
     out = jnp.concatenate(out, axis=1)
     return jnp.concatenate([out, jnp.zeros_like(out)], axis=0)
 
@@ -337,8 +352,7 @@
     out = None
     for x in range(NX):
         bands = [got[x * NB + b, :, half : half + 128] for b in range(NB)]
-        if got.shape[1] == 4:
-            bands = [jnp.concatenate([v, jnp.zeros_like(v)], axis=0) for v in bands]
+        bands = [jnp.concatenate([v, jnp.zeros_like(v)], axis=0) for v in bands]
         piece = roll(jnp.concatenate(bands, axis=0), 32 * (x - field % 4), 1)
         out = piece if out is None else jnp.where(group == x, piece, out)
     return out
@@ -366,15 +380,25 @@
     return lambda b, g: (w_hi[b * NG + g], w_lo[b * NG + g])
 
 
-def forward_kernel(pos, blocks, act, out, coarse_out, w_hi, w_lo):
-    coarse = []
+def plane_rows(blocks, at):
+    return [
+        jnp.concatenate([blocks[b % 2 * 16 + x * 4 + b // 2, at : at + 1, :] for b in range(NB)], axis=0) for x in range(NX)
+    ]
+
+
+def forward_kernel(pos, blocks, out, coarse_out, acts_out, w_hi, w_lo):
+    coarse = [[] for _ in range(NB)]
+    for g in range(NG):
+        rows = plane_rows(blocks, 120 + g)
+        members = [pick([roll(rows[x], 32 * (x - m), 1) for x in range(NX)]) for m in range(M)]
+        for b in range(NB):
+            coarse[b].append(member_rows([v[b : b + 1] for v in members]))
     for b in range(NB):
-        c, y = b % 2, b // 2
-        acc = blocks[c * 16 + y, 120:128, :]
-        for x in range(1, NX):
-            acc = acc + blocks[c * 16 + x * 4 + y, 120:128, :]
-        coarse.append(acc)
-        coarse_out[8 * b : 8 * b + 8, :] = acc
+        coarse_out[8 * b : 8 * b + 8, :] = coarse[b][2]
+    for i in range(3):
+        act = pick(plane_rows(blocks, 125 + i))
+        for b in range(NB):
+            acts_out[i, 8 * b : 8 * b + 8, :] = jnp.broadcast_to(act[b : b + 1], (8, 128))
 
     def weights(b, g):
         hi, lo = unpack_weights(blocks, b, g)
@@ -382,56 +406,38 @@
         w_lo[b * NG + g] = lo
         return hi, lo
 
-    s = forward_sweep(coarse, weights, pos[2])
-    pack_window(s, act[...], out)
+    own = forward_sweep(coarse, weights, pos[2])[2][:4]
+    for z in range(NZ):
+        out[z] = own
 
 
 def pivot_kernel(pos, got, early, p0, p1, p2, p3, p4, out):
-    z = pos[0]
     first, last = pivot_product(unpack_swept(got), (p0, p1, p2, p3, p4))
-    act_before, act_after = (
-        jnp.broadcast_to(got[lax.rem(z + by, NZ), 0][:1], (8, 128)) for by in (NZ - 1, 1)
-    )
-    group = lane_group()
-    upper = iota((8, 128), 0) >= 4
-    second = jnp.where(group == 0, last, early[0])
-    fourth = pick([act_before, roll(act_after, 32, 1), early[2], jnp.zeros((8, 128), F32)])
-    to_plane(jnp.where(upper, roll(early[1], 4, 0), first), jnp.where(upper, roll(fourth, 4, 0), second), out)
-
-
-def upper_half(value):
-    return roll(value, -4, 0)
-
-
-def middle_kernel(pos, got, w_hi, w_lo, coarse_right, out, s_out, coarse_image_out, t_out):
-    windows = [unpack_plane(got, f) for f in range(8)]
+    to_plane([first, jnp.where(lane_group() == 0, last, early[0]), early[1]], out)
+
+
+def middle_kernel(pos, got, w_hi, w_lo, coarse_right, acts, out, s_out, coarse_image_out, t_out):
+    windows = [unpack_plane(got, f) for f in range(12)]
     pivoted = [[windows[g][8 * b : 8 * b + 8] for g in range(NG)] for b in range(NB)]
     settled = backward_sweep(pivoted, stored(w_hi, w_lo))
-    act = upper_half(windows[3])
     s1, s2, s3 = (
-        jnp.concatenate([settled[b][g] for b in range(NB)], axis=0) * a
-        for g, a in ((1, upper_half(windows[4])), (2, act), (3, upper_half(windows[5])))
-    )
-    t = (windows[6], windows[7], upper_half(windows[0]), upper_half(windows[1]), upper_half(windows[2]))
+        jnp.concatenate([settled[b][g] for b in range(NB)], axis=0) * acts[g - 1] for g in (1, 2, 3)
+    )
+    smooth, t, scalars = windows[5], windows[6:11], windows[11]
     t_s = coarse_operate(s2, s1, s3, t)
-    smooth = windows[5]
-    coarse_image = act * (smooth + t_s)
-    scalars = upper_half(windows[6])
+    coarse_image = acts[1] * (smooth + t_s)
     lane = iota((64, 128), 1) % 32
-    c_r = coarse_right[...]
-    weight = band_sum(c_r * s2 + jnp.where(lane == 1, scalars, 0.0))
+    weight = band_sum(coarse_right[...] * s2 + jnp.where(lane == 1, scalars, 0.0))
     energy = band_sum((2.0 * smooth + t_s) * s2 + jnp.where(lane == 0, scalars, 0.0))
-    lane8 = iota((8, 128), 1)
-    extra = jnp.where(lane8 == 0, weight, jnp.where(lane8 == 1, energy, 0.0))
+    lane = iota((8, 128), 1)
+    extra = jnp.where(lane == 0, weight, jnp.where(lane == 1, energy, 0.0))
     for i, v in enumerate((s1, s2, s3)):
         s_out[i] = v
     coarse_image_out[...] = coarse_image
-    for i, v in enumerate(t + (act, windows[4], windows[5])):
+    for i, v in enumerate(t):
         t_out[i] = v
-    t_out[6] = upper_half(windows[4])
-    t_out[7] = upper_half(windows[5])
-    s = forward_sweep([coarse_image[8 * b : 8 * b + 8] for b in range(NB)], stored(w_hi, w_lo), pos[2])
-    pack_window(s, extra, out)
+    coarse = [[None, None, coarse_image[8 * b : 8 * b + 8], None, None] for b in range(NB)]
+    pack_window(forward_sweep(coarse, stored(w_hi, w_lo), pos[2]), extra, out)
 
 
 def spread_rows(s, x, kr):
@@ -496,20 +502,20 @@
     scalars = jnp.zeros((8, 128), F32)
     for i in range(3):
         scalars = jnp.where(lane == i, member_rows(dots[i]), scalars)
-    to_plane(first, pick([last, rows, scalars, jnp.zeros((8, 128), F32)]), out)
+    to_plane([first, pick([last, rows, scalars, jnp.zeros((8, 128), F32)])], out)
     lane = iota((8, 128), 1)
     scalar_out[...] = jnp.where(lane == 0, weight, jnp.where(lane == 1, energy, jnp.where(lane == 2, step, 0.0)))
 
 
-def last_kernel(pos, got, w_hi, w_lo, s_ref, coarse_right, coarse_image, t_ref, scalar, out, s_out):
+def last_kernel(pos, got, w_hi, w_lo, s_ref, coarse_right, coarse_image, t_ref, acts, scalar, out, s_out):
     windows = [unpack_plane(got, f) for f in range(7)]
     pivoted = [[windows[g][8 * b : 8 * b + 8] for g in range(NG)] for b in range(NB)]
     settled = backward_sweep(pivoted, stored(w_hi, w_lo))
     t = tuple(t_ref[i] for i in range(5))
     step = jnp.concatenate([scalar[:, 2:3]] * NB, axis=0)
     s1, s2, s3 = (
-        s_ref[g - 1] - step * (jnp.concatenate([settled[b][g] for b in range(NB)], axis=0) * t_ref[a])
-        for g, a in ((1, 6), (2, 5), (3, 7))
+        s_ref[g - 1] - step * (jnp.concatenate([settled[b][g] for b in range(NB)], axis=0) * acts[g - 1])
+        for g in (1, 2, 3)
     )
     s_out[...] = s2
     t_s = coarse_operate(s2, s1, s3, t)
@@ -559,13 +565,14 @@
     z, x = lax.axis_index("z"), lax.axis_index("x")
     b = 2 * lax.axis_index("y") + lax.axis_index("c")
     pos = jnp.stack([z, x, b, b]).astype(jnp.int32)
-    stack, act, tile, coarse = call(
+    stack, tile = call(
         start_kernel,
-        [(8, ROWS, COLS), (8, 128), (40, 128), (8, 128)],
+        [(8, ROWS, COLS), (48, 128)],
         pos, right_side, diagonal, east_face, north_face, wet, active[0], coupling[0, 0],
-    )
-    window = [tile if g == 2 else shift(tile if g in (1, 3) else tile[:24], "z", NZ, 2 - g) for g in range(NG)]
-    (plane,) = call(gather_kernel, [(NX * 4, 136, 128)], pos, *window, coarse)
+        fetch=True,
+    )
+    window = [tile if g == 2 else shift(tile if g in (1, 3) else tile[:32], "z", NZ, 2 - g) for g in range(NG)]
+    (plane,) = call(gather_kernel, [(NX * 4, 136, 128)], pos, *window)
     plane = lax.all_to_all(plane, ("x", "y"), 0, 0)
     blocks = to_all(plane, "c", 2).reshape(32, 136, 128)
 
@@ -576,15 +583,17 @@
     ring, rim = (NZ, NG, 4, 128), (M, EXT_ROWS, EXT_COLS)
     weights = ((NB * NG, 128, 128), BF16)
     ext, consts, early = call(
-        fields_kernel, [rim, (7, EXT_ROWS, EXT_COLS), (3, 8, 128)], pos, stack, north, south, blocks, act
-    )
-    swept, coarse_right, w_hi, w_lo = call(forward_kernel, [ring, (64, 128), weights, weights], pos, blocks, act)
+        fields_kernel, [rim, (7, EXT_ROWS, EXT_COLS), (2, 8, 128)], pos, stack, north, south, blocks
+    )
+    swept, coarse_right, acts, w_hi, w_lo = call(
+        forward_kernel, [(NZ, 4, 128), (64, 128), (3, 64, 128), weights, weights], pos, blocks
+    )
     swept, early, pivot_rows = lax.optimization_barrier((swept, early, pivot_rows))
     got = lax.all_to_all(swept, "z", 0, 0)
-    (message,) = call(pivot_kernel, [(32, 8, 256)], pos, got, early, *pivot_rows)
+    (message,) = call(pivot_kernel, [(32, 4, 384)], pos, got, early, *pivot_rows)
     got = lax.all_to_all(message, ("x", "y", "c"), 0, 0)
     swept, s0, coarse_image, t = call(
-        middle_kernel, [ring, (3, 64, 128), (64, 128), (8, 64, 128)], pos, got, w_hi, w_lo, coarse_right
+        middle_kernel, [ring, (3, 64, 128), (64, 128), (5, 64, 128)], pos, got, w_hi, w_lo, coarse_right, acts
     )
     pre, image = call(image_kernel, [(M, ROWS, COLS), rim], pos, ext, consts, s0.reshape(3, NB, 8, 128))
     swept, pre, image = lax.optimization_barrier((swept, pre, image))
@@ -594,7 +603,7 @@
     )
     got = lax.all_to_all(message, ("x", "y", "c"), 0, 0)
     dots, s1 = call(
-        last_kernel, [(NZ, 4, 128), (64, 128)], pos, got, w_hi, w_lo, s0, coarse_right, coarse_image, t, scalar
+        last_kernel, [(NZ, 4, 128), (64, 128)], pos, got, w_hi, w_lo, s0, coarse_right, coarse_image, t, acts, scalar
     )
     got = lax.all_to_all(dots, "z", 0, 0)
     (out,) = call(finish_kernel, [(M, ROWS, COLS)], pos, got, scalar, pre, smooth, stack, s1.reshape(NB, 8, 128))

time: 164 us -> 159 us (0.970)
  blocking collectives: 93.1 us -> 87.7 us
    all_to_all x2, blocking collectives: 33.1 us -> 30.2 us  [body(): got = lax.all_to_all(message, ('x', 'y', 'c'), 0, 0)]
    all_to_all x2, blocking collectives: 38.5 us -> 35.8 us  [body(): got = lax.all_to_all(swept, 'z', 0, 0)]
where the time goes in v3:
time: 159 us; the launch traced here: 158 us
  blocking collectives  87.7 us (55%)
  starting transfers between devices  44.6 us (28%)
  Pallas kernels  15.8 us (10%)
  local copies, waits for them, and re-layouts  5.32 us (3%)
  waiting for transfers between devices  4.28 us (3%)
    ppermute x10, starting transfers between devices, shift(): lax.ppermute(value, axes, [(i, (i + by) % count) for i in range(count)])  37.7 us
    all_to_all x2, blocking collectives, body(): got = lax.all_to_all(swept, 'z', 0, 0)  35.8 us
    all_to_all x2, blocking collectives, body(): got = lax.all_to_all(message, ('x', 'y', 'c'), 0, 0)  30.2 us
    all_to_all x1, blocking collectives, body(): got = lax.all_to_all(dots, 'z', 0, 0)  16.1 us
    pallas_call x10, Pallas kernels, call(): pl.pallas_call(kernel, out_shape=[jax.ShapeDtypeStruct(s, d) for s, d in...  15.8 us
    all_to_all x1, starting transfers between devices, body(): plane = lax.all_to_all(plane, ('x', 'y'), 0, 0)  6.89 us
    all_to_all x1, blocking collectives, to_all(): lax.all_to_all(jnp.broadcast_to(value[None], (count,) + value.shape), axe...  5.66 us
    unnamed x16, local copies, waits for them, and re-layouts  5.16 us
  transfers between devices with their start and end apart: 11, of which 2 were waited for; matrix products, arithmetic and copies ran while one was open for 0% of the time, Pallas kernels for 2%

profile of v3, /device:TPU:1, one launch (start us, length us, event | category | flops | bytes accessed | tf_op | source)
XLA Modules:
  0.0 158.0 jit_solution(6973555287392868709)
XLA Ops:
  0.0 0.1 pad_add_fusion.pos
  0.1 0.0 copy-start.1
  0.1 0.8 copy-done.1
  0.9 0.0 copy-start.2
  0.9 0.8 copy-done.2
  1.7 0.0 copy-start.3
  1.7 0.7 copy-done.3
  2.4 0.0 copy-start.4
  2.4 0.7 copy-done.4
  3.2 0.0 copy-start.5
  3.2 0.7 copy-done.5
  3.9 0.0 copy-start.6
  3.9 0.7 copy-done.6
  4.6 0.0 copy-start.7
  4.6 0.7 copy-done.7
  5.2 1.0 shard_map.82
  6.3 4.4 %collective-permute-start.1 = (f32[48,128]{1,0:T(8,128)S(1)}, f32[48,128]{1,0:T(8,128)S(1)}, u32[]{:S(2)}, u32[]{:S(2)}) collective-permute-start(f32[48,128]{1,0:T(8,128)S(1)} %get-tuple-element.36.t2), channel_id=1, source_target_pairs={{0,32},{32,64},{64,96},{96,128},{128,160},{160,192},{192,224},{224... | collective-permute-start | bytes 73736 | tf_op jit(solution)/shard_map/ppermute | solution.py:557
  10.7 9.5 %collective-permute-start.2 = (f32[48,128]{1,0:T(8,128)S(1)}, f32[48,128]{1,0:T(8,128)S(1)}, u32[]{:S(2)}, u32[]{:S(2)}) collective-permute-start(f32[48,128]{1,0:T(8,128)S(1)} %get-tuple-element.36.t2), channel_id=1, source_target_pairs={{0,480},{32,0},{64,32},{96,64},{128,96},{160,128},{192,160},{224,1... | collective-permute-start | bytes 73736 | tf_op jit(solution)/shard_map/ppermute | solution.py:557
  20.2 1.9 %collective-permute-start = (f32[32,128]{1,0:T(8,128)S(1)}, f32[32,128]{1,0:T(8,128)S(1)}, u32[]{:S(2)}, u32[]{:S(2)}) collective-permute-start(f32[32,128]{1,0:T(8,128)S(1)} %slice.10), channel_id=1, source_target_pairs={{0,64},{32,96},{64,128},{96,160},{128,192},{160,224},{192,256},{22... | collective-permute-start | bytes 49160 | tf_op jit(solution)/shard_map/ppermute | solution.py:557
  22.1 5.5 %collective-permute-start.3 = (f32[32,128]{1,0:T(8,128)S(1)}, f32[32,128]{1,0:T(8,128)S(1)}, u32[]{:S(2)}, u32[]{:S(2)}) collective-permute-start(f32[32,128]{1,0:T(8,128)S(1)} %slice.10), channel_id=1, source_target_pairs={{0,448},{32,480},{64,0},{96,32},{128,64},{160,96},{192,128},{224,1... | collective-permute-start | bytes 49160 | tf_op jit(solution)/shard_map/ppermute | solution.py:557
  27.6 0.0 collective-permute-done.t0
  27.6 0.8 collective-permute-done.3.t4
  28.4 0.0 collective-permute-done.1.t1
  28.4 0.0 collective-permute-done.2.t3
  28.4 1.6 %shard_map.83 = f32[16,136,128]{2,1,0:T(8,128)} custom-call(s32[4]{0:T(128)S(1)} %pad_add_fusion.pos, f32[32,128]{1,0:T(8,128)S(1)} %collective-permute-done.t0, f32[48,128]{1,0:T(8,128)S(1)} %collective-permute-done.1.t1, f32[48,128]{1,0:T(8,128)S(1)} %get-tuple-element.36.t2, f32[48,128]{1,0:T(8,128)S(1)} %collective-permute-done.2.t3, ...), custom_call_target="tpu_custom_call" | custom-call | tf_op jit(solution)/shard_map/pallas_call | solution.py:33
  30.1 0.0 copy-start
  30.1 6.9 %all-to-all-start = ((f32[16,136,128]{2,1,0:T(8,128)}), f32[16,136,128]{2,1,0:T(8,128)S(1)}, u32[]{:S(2)}, u32[]{:S(2)}) async-start(f32[16,136,128]{2,1,0:T(8,128)} %shard_map.83), calls=%async_computation | async-start | bytes 2228224 | tf_op jit(solution)/shard_map/all_to_all | solution.py:576
  37.0 0.0 copy-done
  37.0 2.8 %collective-permute-start.6 = (f32[32,2048]{1,0:T(8,128)S(1)}, f32[32,2048]{1,0:T(8,128)S(1)}, u32[]{:S(2)}, u32[]{:S(2)}) collective-permute-start(f32[32,2048]{1,0:T(8,128)S(1)} %bitcast.11), channel_id=1, source_target_pairs={{0,64},{32,96},{64,128},{96,160},{128,192},{160,224},{192,256},{22... | collective-permute-start | bytes 786440 | tf_op jit(solution)/shard_map/ppermute | solution.py:557
  39.8 3.2 %collective-permute-start.7 = (f32[32,2048]{1,0:T(8,128)S(1)}, f32[32,2048]{1,0:T(8,128)S(1)}, u32[]{:S(2)}, u32[]{:S(2)}) collective-permute-start(f32[32,2048]{1,0:T(8,128)S(1)} %bitcast.12), channel_id=1, source_target_pairs={{0,32},{32,64},{64,96},{96,128},{128,160},{160,192},{192,224},{224... | collective-permute-start | bytes 786440 | tf_op jit(solution)/shard_map/ppermute | solution.py:557
  43.0 3.3 %collective-permute-start.8 = (f32[32,2048]{1,0:T(8,128)S(1)}, f32[32,2048]{1,0:T(8,128)S(1)}, u32[]{:S(2)}, u32[]{:S(2)}) collective-permute-start(f32[32,2048]{1,0:T(8,128)S(1)} %bitcast.13), channel_id=1, source_target_pairs={{0,480},{32,0},{64,32},{96,64},{128,96},{160,128},{192,160},{224,1... | collective-permute-start | bytes 786440 | tf_op jit(solution)/shard_map/ppermute | solution.py:557
  46.3 3.6 %collective-permute-start.9 = (f32[32,2048]{1,0:T(8,128)S(1)}, f32[32,2048]{1,0:T(8,128)S(1)}, u32[]{:S(2)}, u32[]{:S(2)}) collective-permute-start(f32[32,2048]{1,0:T(8,128)S(1)} %bitcast.14), channel_id=1, source_target_pairs={{0,448},{32,480},{64,0},{96,32},{128,64},{160,96},{192,128},{224,1... | collective-permute-start | bytes 786440 | tf_op jit(solution)/shard_map/ppermute | solution.py:557
  50.0 3.5 %collective-permute-start.4 = (f32[8,8,128]{2,1,0:T(8,128)S(1)}, f32[8,8,128]{2,1,0:T(8,128)S(1)}, u32[]{:S(2)}, u32[]{:S(2)}) collective-permute-start(f32[8,8,128]{2,1,0:T(8,128)S(1)} %get-tuple-element.68), channel_id=1, source_target_pairs={{0,7},{1,0},{2,1},{3,2},{4,3},{5,4},{6,5},{7,6},{8,15},{9,8},{10,9... | collective-permute-start | bytes 98312 | tf_op jit(solution)/shard_map/ppermute | solution.py:557
  53.5 3.4 %collective-permute-done.4.north_rows = f32[8,8,128]{2,1,0:T(8,128)S(1)} collective-permute-done((f32[8,8,128]{2,1,0:T(8,128)S(1)}, f32[8,8,128]{2,1,0:T(8,128)S(1)}, u32[]{:S(2)}, u32[]{:S(2)}) %collective-permute-start.4) | collective-permute-done | bytes 32800 | tf_op jit(solution)/shard_map/ppermute | solution.py:557
  56.9 0.0 collective-permute-start.5
  56.9 0.0 all-to-all-done
  56.9 0.1 broadcast_in_dim.2
  57.1 5.7 %all_to_all.35 = f32[2,16,136,128]{3,2,1,0:T(8,128)S(1)} all-to-all(f32[2,16,136,128]{3,2,1,0:T(8,128)S(1)} %broadcast_in_dim.2), channel_id=1, replica_groups=mesh['z'=16,'x'=4,'y'=4,'c'=2] {'c'}, dimensions={0} | all-to-all | bytes 4456448 | tf_op jit(solution)/shard_map/all_to_all | solution.py:561
  62.7 2.2 %shard_map.84 = (f32[16,4,128]{2,1,0:T(4,128)S(1)}, f32[64,128]{1,0:T(8,128)S(1)}, f32[3,64,128]{2,1,0:T(8,128)S(1)}, bf16[40,128,128]{2,1,0:T(8,128)(2,1)S(1)}, bf16[40,128,128]{2,1,0:T(8,128)(2,1)S(1)}) custom-call(s32[4]{0:T(128)S(1)} %pad_add_fusion.pos, f32[32,136,128]{2,1,0:T(8,128)S(1)} %bitcast.9), custom_call_target="tpu_custom_call" | custom-call | tf_op jit(solution)/shard_map/pallas_call | solution.py:33
  64.9 0.0 collective-permute-done.5.south_rows
  64.9 1.2 shard_map.85
  66.1 0.0 collective-permute-done.6.p0
  66.1 0.0 collective-permute-done.7.p1
  66.1 0.0 collective-permute-done.8.p3
  66.1 0.0 collective-permute-done.9.p4
  66.2 20.5 %all_to_all.36.got = f32[16,4,128]{2,1,0:T(4,128)S(1)} all-to-all(f32[16,4,128]{2,1,0:T(4,128)S(1)} %get-tuple-element.40), channel_id=1, replica_groups=mesh['z'=16,'x'=4,'y'=4,'c'=2] {'z'}, dimensions={0} | all-to-all | bytes 65536 | tf_op jit(solution)/shard_map/all_to_all | solution.py:592
  86.6 1.1 shard_map.86
  87.7 16.4 %all_to_all.37.got = f32[32,4,384]{2,1,0:T(4,128)S(1)} all-to-all(f32[32,4,384]{2,1,0:T(4,128)S(1)} %shard_map.86), channel_id=1, replica_groups=mesh['z'=16,'x'=4,'y'=4,'c'=2] {'x','y','c'}, dimensions={0} | all-to-all | bytes 393216 | tf_op jit(solution)/shard_map/all_to_all | solution.py:594
  104.1 3.4 %shard_map.87 = (f32[16,5,4,128]{3,2,1,0:T(4,128)S(1)}, f32[3,64,128]{2,1,0:T(8,128)S(1)}, f32[64,128]{1,0:T(8,128)S(1)}, f32[5,64,128]{2,1,0:T(8,128)S(1)}) custom-call(s32[4]{0:T(128)S(1)} %pad_add_fusion.pos, f32[32,4,384]{2,1,0:T(4,128)S(1)} %all_to_all.37.got, bf16[40,128,128]{2,1,0:T(8,128)(2,1)S(1)} %get-tuple-element.47.w_hi, ...), custom_call_target="tpu_custom_call" | custom-call | tf_op jit(solution)/shard_map/pallas_call | solution.py:33
  107.5 0.8 shard_map.88
  108.3 15.3 %all_to_all.38.got = f32[16,5,4,128]{3,2,1,0:T(4,128)S(1)} all-to-all(f32[16,5,4,128]{3,2,1,0:T(4,128)S(1)} %get-tuple-element.57), channel_id=1, replica_groups=mesh['z'=16,'x'=4,'y'=4,'c'=2] {'z'}, dimensions={0} | all-to-all | bytes 327680 | tf_op jit(solution)/shard_map/all_to_all | solution.py:600
  123.6 1.1 shard_map.89
  124.7 13.8 %all_to_all.39.got = f32[32,4,256]{2,1,0:T(4,128)S(1)} all-to-all(f32[32,4,256]{2,1,0:T(4,128)S(1)} %get-tuple-element.59), channel_id=1, replica_groups=mesh['z'=16,'x'=4,'y'=4,'c'=2] {'x','y','c'}, dimensions={0} | all-to-all | bytes 262144 | tf_op jit(solution)/shard_map/all_to_all | solution.py:604
  138.6 1.9 %shard_map.90 = (f32[16,4,128]{2,1,0:T(4,128)S(1)}, f32[64,128]{1,0:T(8,128)S(1)}) custom-call(s32[4]{0:T(128)S(1)} %pad_add_fusion.pos, f32[32,4,256]{2,1,0:T(4,128)S(1)} %all_to_all.39.got, bf16[40,128,128]{2,1,0:T(8,128)(2,1)S(1)} %get-tuple-element.47.w_hi, bf16[40,128,128]{2,1,0:T(8,128)(2,1)S(1)} %get-tuple-element.48.w_lo, ...), custom_call_target="tpu_custom_call" | custom-call | tf_op jit(solution)/shard_map/pallas_call | solution.py:33
  140.5 16.1 %all_to_all.40.got = f32[16,4,128]{2,1,0:T(4,128)S(1)} all-to-all(f32[16,4,128]{2,1,0:T(4,128)S(1)} %get-tuple-element.63), channel_id=1, replica_groups=mesh['z'=16,'x'=4,'y'=4,'c'=2] {'z'}, dimensions={0} | all-to-all | bytes 65536 | tf_op jit(solution)/shard_map/all_to_all | solution.py:608
  156.6 1.4 shard_map.91
  (2 shorter events, 0.0 us)
Async XLA Ops:
  0.1 0.8 copy-start.1
  0.9 0.8 copy-start.2
  1.7 0.7 copy-start.3
  2.4 0.7 copy-start.4
  3.2 0.7 copy-start.5
  3.9 0.7 copy-start.6
  4.6 0.7 copy-start.7
  6.3 22.2 %collective-permute-start.1 = (f32[48,128]{1,0:T(8,128)S(1)}, f32[48,128]{1,0:T(8,128)S(1)}, u32[]{:S(2)}, u32[]{:S(2)}) collective-permute-start(f32[48,128]{1,0:T(8,128)S(1)} %get-tuple-element.36.t2), channel_id=1, source_target_pairs={{0,32},{32,64},{64,96},{96,128},{128,160},{160,192},{192,224},{224... | collective-permute-start | bytes 73736 | tf_op jit(solution)/shard_map/ppermute | solution.py:557
  10.7 17.8 %collective-permute-start.2 = (f32[48,128]{1,0:T(8,128)S(1)}, f32[48,128]{1,0:T(8,128)S(1)}, u32[]{:S(2)}, u32[]{:S(2)}) collective-permute-start(f32[48,128]{1,0:T(8,128)S(1)} %get-tuple-element.36.t2), channel_id=1, source_target_pairs={{0,480},{32,0},{64,32},{96,64},{128,96},{160,128},{192,160},{224,1... | collective-permute-start | bytes 73736 | tf_op jit(solution)/shard_map/ppermute | solution.py:557
  20.2 7.4 %collective-permute-start = (f32[32,128]{1,0:T(8,128)S(1)}, f32[32,128]{1,0:T(8,128)S(1)}, u32[]{:S(2)}, u32[]{:S(2)}) collective-permute-start(f32[32,128]{1,0:T(8,128)S(1)} %slice.10), channel_id=1, source_target_pairs={{0,64},{32,96},{64,128},{96,160},{128,192},{160,224},{192,256},{22... | collective-permute-start | bytes 49160 | tf_op jit(solution)/shard_map/ppermute | solution.py:557
  22.1 6.3 %collective-permute-start.3 = (f32[32,128]{1,0:T(8,128)S(1)}, f32[32,128]{1,0:T(8,128)S(1)}, u32[]{:S(2)}, u32[]{:S(2)}) collective-permute-start(f32[32,128]{1,0:T(8,128)S(1)} %slice.10), channel_id=1, source_target_pairs={{0,448},{32,480},{64,0},{96,32},{128,64},{160,96},{192,128},{224,1... | collective-permute-start | bytes 49160 | tf_op jit(solution)/shard_map/ppermute | solution.py:557
  30.1 6.9 %copy-start = (f32[1,32,2048]{2,1,0:T(8,128)S(1)}, f32[1,32,2048]{2,1,0:T(8,128)}, u32[]{:S(2)}) copy-start(f32[1,32,2048]{2,1,0:T(8,128)} %param.15) | copy-start | bytes 786436
  30.1 26.8 %all-to-all-start = ((f32[16,136,128]{2,1,0:T(8,128)}), f32[16,136,128]{2,1,0:T(8,128)S(1)}, u32[]{:S(2)}, u32[]{:S(2)}) async-start(f32[16,136,128]{2,1,0:T(8,128)} %shard_map.83), calls=%async_computation | async-start | bytes 2228224 | tf_op jit(solution)/shard_map/all_to_all | solution.py:576
  37.0 29.1 %collective-permute-start.6 = (f32[32,2048]{1,0:T(8,128)S(1)}, f32[32,2048]{1,0:T(8,128)S(1)}, u32[]{:S(2)}, u32[]{:S(2)}) collective-permute-start(f32[32,2048]{1,0:T(8,128)S(1)} %bitcast.11), channel_id=1, source_target_pairs={{0,64},{32,96},{64,128},{96,160},{128,192},{160,224},{192,256},{22... | collective-permute-start | bytes 786440 | tf_op jit(solution)/shard_map/ppermute | solution.py:557
  39.8 26.3 %collective-permute-start.7 = (f32[32,2048]{1,0:T(8,128)S(1)}, f32[32,2048]{1,0:T(8,128)S(1)}, u32[]{:S(2)}, u32[]{:S(2)}) collective-permute-start(f32[32,2048]{1,0:T(8,128)S(1)} %bitcast.12), channel_id=1, source_target_pairs={{0,32},{32,64},{64,96},{96,128},{128,160},{160,192},{192,224},{224... | collective-permute-start | bytes 786440 | tf_op jit(solution)/shard_map/ppermute | solution.py:557
  43.0 23.2 %collective-permute-start.8 = (f32[32,2048]{1,0:T(8,128)S(1)}, f32[32,2048]{1,0:T(8,128)S(1)}, u32[]{:S(2)}, u32[]{:S(2)}) collective-permute-start(f32[32,2048]{1,0:T(8,128)S(1)} %bitcast.13), channel_id=1, source_target_pairs={{0,480},{32,0},{64,32},{96,64},{128,96},{160,128},{192,160},{224,1... | collective-permute-start | bytes 786440 | tf_op jit(solution)/shard_map/ppermute | solution.py:557
  46.3 19.8 %collective-permute-start.9 = (f32[32,2048]{1,0:T(8,128)S(1)}, f32[32,2048]{1,0:T(8,128)S(1)}, u32[]{:S(2)}, u32[]{:S(2)}) collective-permute-start(f32[32,2048]{1,0:T(8,128)S(1)} %bitcast.14), channel_id=1, source_target_pairs={{0,448},{32,480},{64,0},{96,32},{128,64},{160,96},{192,128},{224,1... | collective-permute-start | bytes 786440 | tf_op jit(solution)/shard_map/ppermute | solution.py:557
  50.0 6.9 %collective-permute-start.4 = (f32[8,8,128]{2,1,0:T(8,128)S(1)}, f32[8,8,128]{2,1,0:T(8,128)S(1)}, u32[]{:S(2)}, u32[]{:S(2)}) collective-permute-start(f32[8,8,128]{2,1,0:T(8,128)S(1)} %get-tuple-element.68), channel_id=1, source_target_pairs={{0,7},{1,0},{2,1},{3,2},{4,3},{5,4},{6,5},{7,6},{8,15},{9,8},{10,9... | collective-permute-start | bytes 98312 | tf_op jit(solution)/shard_map/ppermute | solution.py:557
  56.9 8.0 %collective-permute-start.5 = (f32[8,8,128]{2,1,0:T(8,128)S(1)}, f32[8,8,128]{2,1,0:T(8,128)S(1)}, u32[]{:S(2)}, u32[]{:S(2)}) collective-permute-start(f32[8,8,128]{2,1,0:T(8,128)S(1)} %get-tuple-element.67), channel_id=1, source_target_pairs={{0,1},{1,2},{2,3},{3,4},{4,5},{5,6},{6,7},{7,0},{8,9},{9,10},{10,1... | collective-permute-start | bytes 98312 | tf_op jit(solution)/shard_map/ppermute | solution.py:557

commit v4 on v3

--- a/solution.py
+++ b/solution.py
@@ -21,23 +21,38 @@
 NT = (((1,), (1,)), ((), ()))
 NN = (((1,), (0,)), ((), ()))
 VMEM_BYTES = 12 * 1024 * 1024
-
-
-def call(kernel, outs, pos, *arrays, fetch=False):
+FETCH_BYTES = 63 * 1024 * 1024
+
+
+def call(kernel, outs, *arrays, fetch=(), room=VMEM_BYTES):
     outs = [o if o[1] == BF16 else (o, F32) for o in outs]
-    vmem = pl.BlockSpec(memory_space=pltpu.VMEM)
-    scratch = []
+    vmem, hbm = pl.BlockSpec(memory_space=pltpu.VMEM), pl.BlockSpec(memory_space=pltpu.HBM)
+    n, count = len(arrays), len(fetch)
+
+    def whole(*refs):
+        given, rest, held = list(refs[:n]), refs[n : n + len(outs)], refs[n + len(outs) :]
+        copies = [pltpu.make_async_copy(given[i], held[j], held[count].at[j]) for j, i in enumerate(fetch)]
+        for copy in copies:
+            copy.start()
+        for copy in copies:
+            copy.wait()
+        for j, i in enumerate(fetch):
+            given[i] = held[j]
+        z, x = lax.axis_index("z"), lax.axis_index("x")
+        b = 2 * lax.axis_index("y") + lax.axis_index("c")
+        kernel((z, x, b), *given, *rest)
+
+    scratch = [pltpu.VMEM(arrays[i].shape, arrays[i].dtype) for i in fetch]
     if fetch:
-        scratch = [pltpu.VMEM(a.shape, a.dtype) for a in arrays] + [pltpu.SemaphoreType.DMA((len(arrays),))]
-    given = pl.BlockSpec(memory_space=pl.ANY) if fetch else vmem
+        scratch.append(pltpu.SemaphoreType.DMA((count,)))
     return pl.pallas_call(
-        kernel,
+        whole,
         out_shape=[jax.ShapeDtypeStruct(s, d) for s, d in outs],
-        in_specs=[pl.BlockSpec(memory_space=pltpu.SMEM)] + [given] * len(arrays),
+        in_specs=[hbm if i in fetch else vmem for i in range(n)],
         out_specs=[vmem] * len(outs),
         scratch_shapes=scratch,
-        compiler_params=pltpu.CompilerParams(vmem_limit_bytes=VMEM_BYTES),
-    )(pos, *arrays)
+        compiler_params=pltpu.CompilerParams(vmem_limit_bytes=room),
+    )(*arrays)
 
 
 def iota(shape, dim):
@@ -134,14 +149,7 @@
     return value[:ROWS, :COLS]
 
 
-def start_kernel(pos, *refs):
-    given, (stack, tile), held, sems = refs[:7], refs[7:9], refs[9:16], refs[16]
-    copies = [pltpu.make_async_copy(a, h, sems.at[i]) for i, (a, h) in enumerate(zip(given, held))]
-    for copy in copies:
-        copy.start()
-    for copy in copies:
-        copy.wait()
-    right, diag, east, north, wet, active, coupling = held
+def start_kernel(pos, right, diag, east, north, wet, active, coupling, stack, tile, small, rims):
     mask = wet[...].astype(F32)
     act = jnp.concatenate([jnp.broadcast_to(active[...].astype(F32), (8, 32))] * 4, axis=1)
     fields = [right[m] for m in range(M)] + [diag[...], east[...], north[...], mask]
@@ -162,33 +170,44 @@
     for i in range(2):
         part = columns[8 * i : 8 * i + 8]
         tile[32 + 8 * i : 40 + 8 * i, :] = jnp.where(upper, roll(part[:, 128:], 4, 0), part[:, :128])
+    for i, start in enumerate((0, ROWS - HALO)):
+        rims[i] = jnp.concatenate([v[start + j : start + j + 1] for j in range(HALO) for v in fields], axis=0)
     rows = block_sums([fields[m] * mask for m in range(M)])
     packed = pick([jnp.broadcast_to(r, (8, 128)) for r in rows]) * act
     row = iota((8, 128), 0)
     tile[24:32, :] = jnp.where(row == 0, packed, jnp.where(row == 1, act, 0.0))
-
-
-def gather_kernel(pos, t0, t1, t2, t3, t4, out):
-    x = pos[1]
+    small[...] = tile[:32, :]
+
+
+def gather_kernel(pos, t0, t1, t2, t3, t4, rims, out):
+    x, y, c = pos[1], lax.div(pos[2], 2), lax.rem(pos[2], 2)
     onward = jnp.where(x == NX - 1, t1[40:48, :], t2[40:48, :])
     back = jnp.where(x == 0, t3[32:40, :], t2[32:40, :])
     tiles = (t0, t1, t2, t3, t4)
     rows = [t[:24, :] for t in tiles] + [t[24:25, :] for t in tiles] + [t[25:26, :] for t in (t1, t2, t3)]
     rows = jnp.concatenate(rows, axis=0)
+    far = jnp.where(c == 0, rims[0], rims[1])
+    near = jnp.where(c == 0, rims[1], rims[0])
     for d in range(NX * 4):
         out[d, :128, :] = rows
-        out[d, 128:, :] = jnp.where(lax.rem(x + 1, NX) == d // 4, onward, back)
-
-
-def side(blocks, band, sender):
-    return blocks[lax.rem(band, 2) * 16 + sender * 4 + lax.div(band, 2), 128:136, :]
-
-
-def fields_kernel(pos, stack, north_rows, south_rows, blocks, ext, consts, early):
+        rim = jnp.where(y == d % 4, near, far)
+        out[d, 136:, :] = rim[8:]
+        columns = jnp.where(lax.rem(x + 1, NX) == d // 4, onward, back)
+        out[d, 128:136, :] = jnp.where(x == d // 4, rim[:8], columns)
+
+
+def side(blocks, band, sender, rows=8):
+    return blocks[lax.rem(band, 2) * 16 + sender * 4 + lax.div(band, 2), 128 : 128 + rows, :]
+
+
+def fields_kernel(pos, stack, blocks, ext, consts, early):
     x, b = pos[1], pos[2]
     after, before = lax.rem(x + 1, NX), lax.rem(x + NX - 1, NX)
+    up, down = lax.rem(b + 1, NB), lax.rem(b + NB - 1, NB)
+    north_rows, south_rows = side(blocks, up, x, 24), side(blocks, down, x, 24)
+    sub = iota((8, 128), 0)
     sides = []
-    for band in (b, lax.rem(b + 1, NB), lax.rem(b + NB - 1, NB)):
+    for band in (b, up, down):
         sides += [side(blocks, band, after), side(blocks, band, before)]
     turned = jnp.transpose(jnp.concatenate(sides + [jnp.zeros((80, 128), F32)], axis=0))
     first = iota((8, 128), 0) < 4
@@ -204,7 +223,12 @@
         rows = turned[32 * (f % 4) : 32 * (f % 4) + 32]
         h = f // 4
         corner = jnp.where(first, columns(rows[:8], 1, h), columns(rows[24:], 2, h))
-        left = jnp.concatenate([stack[f], jnp.where(first, north_rows[f], south_rows[f])], axis=0)
+        beyond = jnp.zeros((8, 128), F32)
+        for j in range(HALO):
+            at = 8 * j + f
+            beyond = jnp.where(sub == j, north_rows[at : at + 1], beyond)
+            beyond = jnp.where(sub == 8 - HALO + j, south_rows[at : at + 1], beyond)
+        left = jnp.concatenate([stack[f], beyond], axis=0)
         right = jnp.concatenate([columns(rows, 0, h), corner], axis=0)
         fields.append(jnp.concatenate([left, right], axis=1))
     for m in range(M):
@@ -264,7 +288,7 @@
     return halves(jnp.concatenate(tiles, axis=0))
 
 
-def forward_sweep(coarse, weights, mine):
+def forward_sweep(coarse, weights, mine, live):
     group = lane_group()
     zero = jnp.zeros((8, 128), F32)
     s = [zero if v is None else v for v in coarse[0]]
@@ -272,6 +296,9 @@
     for b in range(1, NB):
         new = []
         for g in range(NG):
+            if not live(b, g):
+                new.append(zero)
+                continue
             left = s[g - 1] if g > 0 else zero
             right = s[g + 1] if g < NG - 1 else zero
             lhs = jnp.concatenate(
@@ -286,6 +313,22 @@
     return out
 
 
+def distance(g):
+    return max(0, 4 * abs(g - 2) - 4) if g != 2 else -1
+
+
+def inward(b, g):
+    return distance(g) < NB - 1 - b
+
+
+def outward(b, g):
+    return distance(g) < b
+
+
+def rimward(b, g):
+    return distance(g) < b + 1
+
+
 def backward_sweep(pivoted, weights):
     group = lane_group()
     zero = jnp.zeros((8, 128), F32)
@@ -295,15 +338,21 @@
     for b in range(NB - 2, -1, -1):
         o = []
         for g in range(NG):
+            if not rimward(b + 1, g):
+                o.append(None)
+                continue
             lhs = jnp.concatenate([jnp.where(group == x, s[g], 0.0) for x in range(NX)], axis=0)
             hi, lo = weights(b + 1, g)
             o.append(dot3(lhs, hi, lo, NN))
         s = []
         for g in range(NG):
+            if o[g] is None or not rimward(b, g):
+                s.append(zero)
+                continue
             own = o[g][8:16] + o[g][16:24]
             own = own + jnp.where(group == 3, 0.0, o[g][0:8]) + jnp.where(group == 0, 0.0, o[g][24:32])
-            after = o[g + 1][0:8] if g < NG - 1 else zero
-            before = o[g - 1][24:32] if g > 0 else zero
+            after = o[g + 1][0:8] if g < NG - 1 and o[g + 1] is not None else zero
+            before = o[g - 1][24:32] if g > 0 and o[g - 1] is not None else zero
             own = own + jnp.where(group == 3, after, 0.0) + jnp.where(group == 0, before, 0.0)
             s.append(pivoted[b][g] - own)
         out[b] = s
@@ -406,7 +455,11 @@
         w_lo[b * NG + g] = lo
         return hi, lo
 
-    own = forward_sweep(coarse, weights, pos[2])[2][:4]
+    for b in range(1, NB):
+        for g in range(NG):
+            if not inward(b, g) and (rimward(b, g) or outward(b, g)):
+                weights(b, g)
+    own = forward_sweep(coarse, weights, pos[2], inward)[2][:4]
     for z in range(NZ):
         out[z] = own
 
@@ -437,7 +490,7 @@
     for i, v in enumerate(t):
         t_out[i] = v
     coarse = [[None, None, coarse_image[8 * b : 8 * b + 8], None, None] for b in range(NB)]
-    pack_window(forward_sweep(coarse, stored(w_hi, w_lo), pos[2]), extra, out)
+    pack_window(forward_sweep(coarse, stored(w_hi, w_lo), pos[2], outward), extra, out)
 
 
 def spread_rows(s, x, kr):
@@ -562,51 +615,47 @@
 
 
 def body(right_side, diagonal, east_face, north_face, wet, active, coupling, pivots):
-    z, x = lax.axis_index("z"), lax.axis_index("x")
-    b = 2 * lax.axis_index("y") + lax.axis_index("c")
-    pos = jnp.stack([z, x, b, b]).astype(jnp.int32)
-    stack, tile = call(
+    stack, tile, part, rims = call(
         start_kernel,
-        [(8, ROWS, COLS), (48, 128)],
-        pos, right_side, diagonal, east_face, north_face, wet, active[0], coupling[0, 0],
-        fetch=True,
-    )
-    window = [tile if g == 2 else shift(tile if g in (1, 3) else tile[:32], "z", NZ, 2 - g) for g in range(NG)]
-    (plane,) = call(gather_kernel, [(NX * 4, 136, 128)], pos, *window)
+        [(8, ROWS, COLS), (48, 128), (32, 128), (2, 24, 128)],
+        right_side, diagonal, east_face, north_face, wet, active[0], coupling[0, 0],
+        fetch=range(7),
+        room=FETCH_BYTES,
+    )
+    window = [tile if g == 2 else shift(tile if g in (1, 3) else part, "z", NZ, 2 - g) for g in range(NG)]
+    (plane,) = call(gather_kernel, [(NX * 4, 152, 128)], *window, rims, fetch=(2, 5))
     plane = lax.all_to_all(plane, ("x", "y"), 0, 0)
-    blocks = to_all(plane, "c", 2).reshape(32, 136, 128)
+    blocks = to_all(plane, "c", 2).reshape(32, 152, 128)
 
     pivot_rows = [pivots[0] if g == 2 else shift(pivots[0], "z", NZ, 2 - g) for g in range(NG)]
-    south = shift(stack[:, ROWS - 8 :], ("y", "c"), NB, 1)
-    north = shift(stack[:, :8], ("y", "c"), NB, -1)
 
     ring, rim = (NZ, NG, 4, 128), (M, EXT_ROWS, EXT_COLS)
     weights = ((NB * NG, 128, 128), BF16)
     ext, consts, early = call(
-        fields_kernel, [rim, (7, EXT_ROWS, EXT_COLS), (2, 8, 128)], pos, stack, north, south, blocks
+        fields_kernel, [rim, (7, EXT_ROWS, EXT_COLS), (2, 8, 128)], stack, blocks
     )
     swept, coarse_right, acts, w_hi, w_lo = call(
-        forward_kernel, [(NZ, 4, 128), (64, 128), (3, 64, 128), weights, weights], pos, blocks
+        forward_kernel, [(NZ, 4, 128), (64, 128), (3, 64, 128), weights, weights], blocks
     )
     swept, early, pivot_rows = lax.optimization_barrier((swept, early, pivot_rows))
     got = lax.all_to_all(swept, "z", 0, 0)
-    (message,) = call(pivot_kernel, [(32, 4, 384)], pos, got, early, *pivot_rows)
+    (message,) = call(pivot_kernel, [(32, 4, 384)], got, early, *pivot_rows)
     got = lax.all_to_all(message, ("x", "y", "c"), 0, 0)
     swept, s0, coarse_image, t = call(
-        middle_kernel, [ring, (3, 64, 128), (64, 128), (5, 64, 128)], pos, got, w_hi, w_lo, coarse_right, acts
-    )
-    pre, image = call(image_kernel, [(M, ROWS, COLS), rim], pos, ext, consts, s0.reshape(3, NB, 8, 128))
+        middle_kernel, [ring, (3, 64, 128), (64, 128), (5, 64, 128)], got, w_hi, w_lo, coarse_right, acts
+    )
+    pre, image = call(image_kernel, [(M, ROWS, COLS), rim], ext, consts, s0.reshape(3, NB, 8, 128))
     swept, pre, image = lax.optimization_barrier((swept, pre, image))
     got = lax.all_to_all(swept, "z", 0, 0)
     message, smooth, scalar = call(
-        step_kernel, [(32, 4, 256), (M, ROWS, COLS), (8, 128)], pos, got, ext, consts, image, *pivot_rows
+        step_kernel, [(32, 4, 256), (M, ROWS, COLS), (8, 128)], got, ext, consts, image, *pivot_rows
     )
     got = lax.all_to_all(message, ("x", "y", "c"), 0, 0)
     dots, s1 = call(
-        last_kernel, [(NZ, 4, 128), (64, 128)], pos, got, w_hi, w_lo, s0, coarse_right, coarse_image, t, acts, scalar
+        last_kernel, [(NZ, 4, 128), (64, 128)], got, w_hi, w_lo, s0, coarse_right, coarse_image, t, acts, scalar
     )
     got = lax.all_to_all(dots, "z", 0, 0)
-    (out,) = call(finish_kernel, [(M, ROWS, COLS)], pos, got, scalar, pre, smooth, stack, s1.reshape(NB, 8, 128))
+    (out,) = call(finish_kernel, [(M, ROWS, COLS)], got, scalar, pre, smooth, stack, s1.reshape(NB, 8, 128))
     return out
 
 

time: 159 us -> 152 us (0.956)
  blocking collectives: 87.7 us -> 92 us
  Pallas kernels: 15.8 us -> 11.6 us
  local copies, waits for them, and re-layouts: 5.32 us -> 1.65 us
  starting transfers between devices: 44.6 us -> 41.1 us
    pallas_call x10, Pallas kernels: 15.8 us -> 11.6 us  [call(): pl.pallas_call(whole, out_shape=[jax.ShapeDtypeStruct(s, d) for s, d in o...]
    all_to_all x1, waiting for transfers between devices: 0.01 us -> 3.69 us  [body(): plane = lax.all_to_all(plane, ('x', 'y'), 0, 0)]
    unnamed x16 -> x8, local copies, waits for them, and re-layouts: 5.16 us -> 1.49 us
    ppermute x10 -> x8, starting transfers between devices: 37.7 us -> 34.2 us  [shift(): lax.ppermute(value, axes, [(i, (i + by) % count) for i in range(count)])]
    all_to_all x1, blocking collectives: 5.66 us -> 8.98 us  [to_all(): lax.all_to_all(jnp.broadcast_to(value[None], (count,) + value.shape), axe...]
    ppermute x10 -> x8, waiting for transfers between devices: 4.28 us -> 1.07 us  [shift(): lax.ppermute(value, axes, [(i, (i + by) % count) for i in range(count)])]
  transfers between devices with their start and end apart: 11 -> 9, of which waited for: 2 -> 2; matrix products, arithmetic and copies ran while one was open for 0% -> 0% of each run, Pallas kernels for 2% -> 1%
where the time goes in v4:
time: 152 us; the launch traced here: 151 us
  blocking collectives  92 us (61%)
  starting transfers between devices  41.1 us (27%)
  Pallas kernels  11.6 us (8%)
  waiting for transfers between devices  4.75 us (3%)
  local copies, waits for them, and re-layouts  1.65 us (1%)
    all_to_all x2, blocking collectives, body(): got = lax.all_to_all(swept, 'z', 0, 0)  35.6 us
    ppermute x8, starting transfers between devices, shift(): lax.ppermute(value, axes, [(i, (i + by) % count) for i in range(count)])  34.2 us
    all_to_all x2, blocking collectives, body(): got = lax.all_to_all(message, ('x', 'y', 'c'), 0, 0)  31.4 us
    all_to_all x1, blocking collectives, body(): got = lax.all_to_all(dots, 'z', 0, 0)  16.1 us
    pallas_call x10, Pallas kernels, call(): pl.pallas_call(whole, out_shape=[jax.ShapeDtypeStruct(s, d) for s, d in o...  11.6 us
    all_to_all x1, blocking collectives, to_all(): lax.all_to_all(jnp.broadcast_to(value[None], (count,) + value.shape), axe...  8.98 us
    all_to_all x1, starting transfers between devices, body(): plane = lax.all_to_all(plane, ('x', 'y'), 0, 0)  6.9 us
    all_to_all x1, waiting for transfers between devices, body(): plane = lax.all_to_all(plane, ('x', 'y'), 0, 0)  3.69 us
  transfers between devices with their start and end apart: 9, of which 2 were waited for; matrix products, arithmetic and copies ran while one was open for 0% of the time, Pallas kernels for 1%

profile of v4, /device:TPU:1, one launch (start us, length us, event | category | flops | bytes accessed | tf_op | source)
XLA Modules:
  0.0 151.4 jit_solution(9100545788344388959)
XLA Ops:
  0.0 1.8 %shard_map.82 = (f32[8,32,128]{2,1,0:T(8,128)}, f32[48,128]{1,0:T(8,128)}, f32[32,128]{1,0:T(8,128)}, f32[2,24,128]{2,1,0:T(8,128)}) custom-call(f32[4,32,128]{2,1,0:T(8,128)} %refs_0_.1, f32[32,128]{1,0:T(8,128)} %refs_1_.1, f32[32,128]{1,0:T(8,128)} %refs_2_.1, f32[32,128]{1,0:T(8,128)} %refs_3_.1, s32[32,128]{1,0:T(8,128)} %refs_4_.1, s32[1,32]{1,0:T(1,128)} %bitcast.17, ...), custom_call_target="tpu_custom_call" | custom-call | tf_op jit(solution)/shard_map/pallas_call | solution.py:48
  1.8 4.4 %collective-permute-start.1 = (f32[48,128]{1,0:T(8,128)}, f32[48,128]{1,0:T(8,128)S(1)}, u32[]{:S(2)}, u32[]{:S(2)}) collective-permute-start(f32[48,128]{1,0:T(8,128)} %get-tuple-element.39.refs_2_), channel_id=1, source_target_pairs={{0,32},{32,64},{64,96},{96,128},{128,160},{160,192},{192,224},{224... | collective-permute-start | bytes 73736 | tf_op jit(solution)/shard_map/ppermute | solution.py:610
  6.2 9.5 %collective-permute-start.2 = (f32[48,128]{1,0:T(8,128)}, f32[48,128]{1,0:T(8,128)S(1)}, u32[]{:S(2)}, u32[]{:S(2)}) collective-permute-start(f32[48,128]{1,0:T(8,128)} %get-tuple-element.39.refs_2_), channel_id=1, source_target_pairs={{0,480},{32,0},{64,32},{96,64},{128,96},{160,128},{192,160},{224,1... | collective-permute-start | bytes 73736 | tf_op jit(solution)/shard_map/ppermute | solution.py:610
  15.7 1.9 %collective-permute-start = (f32[32,128]{1,0:T(8,128)}, f32[32,128]{1,0:T(8,128)S(1)}, u32[]{:S(2)}, u32[]{:S(2)}) collective-permute-start(f32[32,128]{1,0:T(8,128)} %get-tuple-element.38), channel_id=1, source_target_pairs={{0,64},{32,96},{64,128},{96,160},{128,192},{160,224},{192,256},{22... | collective-permute-start | bytes 49160 | tf_op jit(solution)/shard_map/ppermute | solution.py:610
  17.6 5.5 %collective-permute-start.3 = (f32[32,128]{1,0:T(8,128)}, f32[32,128]{1,0:T(8,128)S(1)}, u32[]{:S(2)}, u32[]{:S(2)}) collective-permute-start(f32[32,128]{1,0:T(8,128)} %get-tuple-element.38), channel_id=1, source_target_pairs={{0,448},{32,480},{64,0},{96,32},{128,64},{160,96},{192,128},{224,1... | collective-permute-start | bytes 49160 | tf_op jit(solution)/shard_map/ppermute | solution.py:610
  23.1 0.0 collective-permute-done.refs_0_
  23.1 1.0 collective-permute-done.3.refs_4_
  24.1 0.0 collective-permute-done.1.refs_1_
  24.1 0.0 collective-permute-done.2.refs_3_
  24.1 0.0 copy-start.2
  24.1 0.7 copy-done.2
  24.9 0.0 copy-start.3
  24.9 0.7 copy-done.3
  25.6 1.2 shard_map.83
  26.8 0.0 copy-start
  26.8 6.9 %all-to-all-start = ((f32[16,152,128]{2,1,0:T(8,128)}), f32[16,152,128]{2,1,0:T(8,128)S(1)}, u32[]{:S(2)}, u32[]{:S(2)}) async-start(f32[16,152,128]{2,1,0:T(8,128)} %shard_map.83), calls=%async_computation | async-start | bytes 2490368 | tf_op jit(solution)/shard_map/all_to_all | solution.py:627
  33.7 0.0 copy-done
  33.7 2.8 %collective-permute-start.4 = (f32[32,2048]{1,0:T(8,128)S(1)}, f32[32,2048]{1,0:T(8,128)S(1)}, u32[]{:S(2)}, u32[]{:S(2)}) collective-permute-start(f32[32,2048]{1,0:T(8,128)S(1)} %bitcast.8), channel_id=1, source_target_pairs={{0,64},{32,96},{64,128},{96,160},{128,192},{160,224},{192,256},{22... | collective-permute-start | bytes 786440 | tf_op jit(solution)/shard_map/ppermute | solution.py:610
  36.5 3.2 %collective-permute-start.5 = (f32[32,2048]{1,0:T(8,128)S(1)}, f32[32,2048]{1,0:T(8,128)S(1)}, u32[]{:S(2)}, u32[]{:S(2)}) collective-permute-start(f32[32,2048]{1,0:T(8,128)S(1)} %bitcast.9), channel_id=1, source_target_pairs={{0,32},{32,64},{64,96},{96,128},{128,160},{160,192},{192,224},{224... | collective-permute-start | bytes 786440 | tf_op jit(solution)/shard_map/ppermute | solution.py:610
  39.7 3.3 %collective-permute-start.6 = (f32[32,2048]{1,0:T(8,128)S(1)}, f32[32,2048]{1,0:T(8,128)S(1)}, u32[]{:S(2)}, u32[]{:S(2)}) collective-permute-start(f32[32,2048]{1,0:T(8,128)S(1)} %bitcast.10), channel_id=1, source_target_pairs={{0,480},{32,0},{64,32},{96,64},{128,96},{160,128},{192,160},{224,1... | collective-permute-start | bytes 786440 | tf_op jit(solution)/shard_map/ppermute | solution.py:610
  43.1 3.6 %collective-permute-start.7 = (f32[32,2048]{1,0:T(8,128)S(1)}, f32[32,2048]{1,0:T(8,128)S(1)}, u32[]{:S(2)}, u32[]{:S(2)}) collective-permute-start(f32[32,2048]{1,0:T(8,128)S(1)} %bitcast.11), channel_id=1, source_target_pairs={{0,448},{32,480},{64,0},{96,32},{128,64},{160,96},{192,128},{224,1... | collective-permute-start | bytes 786440 | tf_op jit(solution)/shard_map/ppermute | solution.py:610
  46.7 3.7 %all-to-all-done = f32[16,152,128]{2,1,0:T(8,128)S(1)} async-done(((f32[16,152,128]{2,1,0:T(8,128)}), f32[16,152,128]{2,1,0:T(8,128)S(1)}, u32[]{:S(2)}, u32[]{:S(2)}) %all-to-all-start) | async-done | bytes 1245216 | tf_op jit(solution)/shard_map/all_to_all | solution.py:627
  50.4 0.2 broadcast_in_dim.2
  50.6 9.0 %all_to_all.35 = f32[2,16,152,128]{3,2,1,0:T(8,128)S(1)} all-to-all(f32[2,16,152,128]{3,2,1,0:T(8,128)S(1)} %broadcast_in_dim.2), channel_id=1, replica_groups=mesh['z'=16,'x'=4,'y'=4,'c'=2] {'c'}, dimensions={0} | all-to-all | bytes 4980736 | tf_op jit(solution)/shard_map/all_to_all | solution.py:614
  59.5 0.0 copy-start.1
  59.5 1.6 %shard_map.84 = (f32[16,4,128]{2,1,0:T(4,128)S(1)}, f32[64,128]{1,0:T(8,128)S(1)}, f32[3,64,128]{2,1,0:T(8,128)S(1)}, bf16[40,128,128]{2,1,0:T(8,128)(2,1)S(1)}, bf16[40,128,128]{2,1,0:T(8,128)(2,1)S(1)}) custom-call(f32[32,152,128]{2,1,0:T(8,128)S(1)} %bitcast.6), custom_call_target="tpu_custom_call" | custom-call | tf_op jit(solution)/shard_map/pallas_call | solution.py:48
  61.1 0.0 copy-done.1
  61.2 0.6 shard_map.85
  61.8 0.0 collective-permute-done.4.refs_2_.refs_4_
  61.8 0.0 collective-permute-done.5.refs_3_.refs_5_
  61.8 0.0 collective-permute-done.6.refs_5_.refs_7_
  61.8 0.0 collective-permute-done.7.refs_6_.refs_8_
  61.8 20.3 %all_to_all.36.refs_0_ = f32[16,4,128]{2,1,0:T(4,128)S(1)} all-to-all(f32[16,4,128]{2,1,0:T(4,128)S(1)} %get-tuple-element.44), channel_id=1, replica_groups=mesh['z'=16,'x'=4,'y'=4,'c'=2] {'z'}, dimensions={0} | all-to-all | bytes 65536 | tf_op jit(solution)/shard_map/all_to_all | solution.py:641
  82.1 0.5 shard_map.86
  82.7 17.6 %all_to_all.37.refs_0_ = f32[32,4,384]{2,1,0:T(4,128)S(1)} all-to-all(f32[32,4,384]{2,1,0:T(4,128)S(1)} %shard_map.86), channel_id=1, replica_groups=mesh['z'=16,'x'=4,'y'=4,'c'=2] {'x','y','c'}, dimensions={0} | all-to-all | bytes 393216 | tf_op jit(solution)/shard_map/all_to_all | solution.py:643
  100.3 2.7 %shard_map.87 = (f32[16,5,4,128]{3,2,1,0:T(4,128)S(1)}, f32[3,64,128]{2,1,0:T(8,128)S(1)}, f32[64,128]{1,0:T(8,128)S(1)}, f32[5,64,128]{2,1,0:T(8,128)S(1)}) custom-call(f32[32,4,384]{2,1,0:T(4,128)S(1)} %all_to_all.37.refs_0_, bf16[40,128,128]{2,1,0:T(8,128)(2,1)S(1)} %get-tuple-element.51.refs_1_, bf16[40,128,128]{2,1,0:T(8,128)(2,1)S(1)} %get-tuple-element.52.refs_2_, ...), custom_call_target="tpu_custom_call" | custom-call | tf_op jit(solution)/shard_map/pallas_call | solution.py:48
  103.0 0.3 shard_map.88
  103.3 15.3 %all_to_all.38.refs_0_ = f32[16,5,4,128]{3,2,1,0:T(4,128)S(1)} all-to-all(f32[16,5,4,128]{3,2,1,0:T(4,128)S(1)} %get-tuple-element.61), channel_id=1, replica_groups=mesh['z'=16,'x'=4,'y'=4,'c'=2] {'z'}, dimensions={0} | all-to-all | bytes 327680 | tf_op jit(solution)/shard_map/all_to_all | solution.py:649
  118.6 0.6 shard_map.89
  119.2 13.8 %all_to_all.39.refs_0_ = f32[32,4,256]{2,1,0:T(4,128)S(1)} all-to-all(f32[32,4,256]{2,1,0:T(4,128)S(1)} %get-tuple-element.63), channel_id=1, replica_groups=mesh['z'=16,'x'=4,'y'=4,'c'=2] {'x','y','c'}, dimensions={0} | all-to-all | bytes 262144 | tf_op jit(solution)/shard_map/all_to_all | solution.py:653
  133.0 1.4 shard_map.90
  134.4 16.1 %all_to_all.40.refs_0_ = f32[16,4,128]{2,1,0:T(4,128)S(1)} all-to-all(f32[16,4,128]{2,1,0:T(4,128)S(1)} %get-tuple-element.67), channel_id=1, replica_groups=mesh['z'=16,'x'=4,'y'=4,'c'=2] {'z'}, dimensions={0} | all-to-all | bytes 65536 | tf_op jit(solution)/shard_map/all_to_all | solution.py:657
  150.5 0.9 shard_map.91
Async XLA Ops:
  1.8 22.4 %collective-permute-start.1 = (f32[48,128]{1,0:T(8,128)}, f32[48,128]{1,0:T(8,128)S(1)}, u32[]{:S(2)}, u32[]{:S(2)}) collective-permute-start(f32[48,128]{1,0:T(8,128)} %get-tuple-element.39.refs_2_), channel_id=1, source_target_pairs={{0,32},{32,64},{64,96},{96,128},{128,160},{160,192},{192,224},{224... | collective-permute-start | bytes 73736 | tf_op jit(solution)/shard_map/ppermute | solution.py:610
  6.2 18.0 %collective-permute-start.2 = (f32[48,128]{1,0:T(8,128)}, f32[48,128]{1,0:T(8,128)S(1)}, u32[]{:S(2)}, u32[]{:S(2)}) collective-permute-start(f32[48,128]{1,0:T(8,128)} %get-tuple-element.39.refs_2_), channel_id=1, source_target_pairs={{0,480},{32,0},{64,32},{96,64},{128,96},{160,128},{192,160},{224,1... | collective-permute-start | bytes 73736 | tf_op jit(solution)/shard_map/ppermute | solution.py:610
  15.7 7.4 %collective-permute-start = (f32[32,128]{1,0:T(8,128)}, f32[32,128]{1,0:T(8,128)S(1)}, u32[]{:S(2)}, u32[]{:S(2)}) collective-permute-start(f32[32,128]{1,0:T(8,128)} %get-tuple-element.38), channel_id=1, source_target_pairs={{0,64},{32,96},{64,128},{96,160},{128,192},{160,224},{192,256},{22... | collective-permute-start | bytes 49160 | tf_op jit(solution)/shard_map/ppermute | solution.py:610
  17.6 6.5 %collective-permute-start.3 = (f32[32,128]{1,0:T(8,128)}, f32[32,128]{1,0:T(8,128)S(1)}, u32[]{:S(2)}, u32[]{:S(2)}) collective-permute-start(f32[32,128]{1,0:T(8,128)} %get-tuple-element.38), channel_id=1, source_target_pairs={{0,448},{32,480},{64,0},{96,32},{128,64},{160,96},{192,128},{224,1... | collective-permute-start | bytes 49160 | tf_op jit(solution)/shard_map/ppermute | solution.py:610
  24.1 0.7 copy-start.2
  24.9 0.7 copy-start.3
  26.8 6.9 %copy-start = (f32[1,32,2048]{2,1,0:T(8,128)S(1)}, f32[1,32,2048]{2,1,0:T(8,128)}, u32[]{:S(2)}) copy-start(f32[1,32,2048]{2,1,0:T(8,128)} %param.15) | copy-start | bytes 786436
  26.8 23.6 %all-to-all-start = ((f32[16,152,128]{2,1,0:T(8,128)}), f32[16,152,128]{2,1,0:T(8,128)S(1)}, u32[]{:S(2)}, u32[]{:S(2)}) async-start(f32[16,152,128]{2,1,0:T(8,128)} %shard_map.83), calls=%async_computation | async-start | bytes 2490368 | tf_op jit(solution)/shard_map/all_to_all | solution.py:627
  33.7 28.1 %collective-permute-start.4 = (f32[32,2048]{1,0:T(8,128)S(1)}, f32[32,2048]{1,0:T(8,128)S(1)}, u32[]{:S(2)}, u32[]{:S(2)}) collective-permute-start(f32[32,2048]{1,0:T(8,128)S(1)} %bitcast.8), channel_id=1, source_target_pairs={{0,64},{32,96},{64,128},{96,160},{128,192},{160,224},{192,256},{22... | collective-permute-start | bytes 786440 | tf_op jit(solution)/shard_map/ppermute | solution.py:610
  36.5 25.3 %collective-permute-start.5 = (f32[32,2048]{1,0:T(8,128)S(1)}, f32[32,2048]{1,0:T(8,128)S(1)}, u32[]{:S(2)}, u32[]{:S(2)}) collective-permute-start(f32[32,2048]{1,0:T(8,128)S(1)} %bitcast.9), channel_id=1, source_target_pairs={{0,32},{32,64},{64,96},{96,128},{128,160},{160,192},{192,224},{224... | collective-permute-start | bytes 786440 | tf_op jit(solution)/shard_map/ppermute | solution.py:610
  39.7 22.1 %collective-permute-start.6 = (f32[32,2048]{1,0:T(8,128)S(1)}, f32[32,2048]{1,0:T(8,128)S(1)}, u32[]{:S(2)}, u32[]{:S(2)}) collective-permute-start(f32[32,2048]{1,0:T(8,128)S(1)} %bitcast.10), channel_id=1, source_target_pairs={{0,480},{32,0},{64,32},{96,64},{128,96},{160,128},{192,160},{224,1... | collective-permute-start | bytes 786440 | tf_op jit(solution)/shard_map/ppermute | solution.py:610
  43.1 18.8 %collective-permute-start.7 = (f32[32,2048]{1,0:T(8,128)S(1)}, f32[32,2048]{1,0:T(8,128)S(1)}, u32[]{:S(2)}, u32[]{:S(2)}) collective-permute-start(f32[32,2048]{1,0:T(8,128)S(1)} %bitcast.11), channel_id=1, source_target_pairs={{0,448},{32,480},{64,0},{96,32},{128,64},{160,96},{192,128},{224,1... | collective-permute-start | bytes 786440 | tf_op jit(solution)/shard_map/ppermute | solution.py:610
  59.5 1.6 %copy-start.1 = (f32[8,32,128]{2,1,0:T(8,128)S(1)}, f32[8,32,128]{2,1,0:T(8,128)}, u32[]{:S(2)}) copy-start(f32[8,32,128]{2,1,0:T(8,128)} %get-tuple-element.42.refs_0_.refs_4_) | copy-start | bytes 393220

commit v5 on v4

--- a/solution.py
+++ b/solution.py
@@ -149,7 +149,7 @@
     return value[:ROWS, :COLS]
 
 
-def start_kernel(pos, right, diag, east, north, wet, active, coupling, stack, tile, small, rims):
+def start_kernel(pos, right, diag, east, north, wet, active, coupling, stack, tile, rims):
     mask = wet[...].astype(F32)
     act = jnp.concatenate([jnp.broadcast_to(active[...].astype(F32), (8, 32))] * 4, axis=1)
     fields = [right[m] for m in range(M)] + [diag[...], east[...], north[...], mask]
@@ -176,7 +176,6 @@
     packed = pick([jnp.broadcast_to(r, (8, 128)) for r in rows]) * act
     row = iota((8, 128), 0)
     tile[24:32, :] = jnp.where(row == 0, packed, jnp.where(row == 1, act, 0.0))
-    small[...] = tile[:32, :]
 
 
 def gather_kernel(pos, t0, t1, t2, t3, t4, rims, out):
@@ -610,24 +609,29 @@
     return lax.ppermute(value, axes, [(i, (i + by) % count) for i in range(count)])
 
 
+def ring_window(value):
+    before, after = shift(value, "z", NZ, 1), shift(value, "z", NZ, -1)
+    return [shift(before, "z", NZ, 1), before, value, after, shift(after, "z", NZ, -1)]
+
+
 def to_all(value, axes, count):
     return lax.all_to_all(jnp.broadcast_to(value[None], (count,) + value.shape), axes, 0, 0)
 
 
 def body(right_side, diagonal, east_face, north_face, wet, active, coupling, pivots):
-    stack, tile, part, rims = call(
+    stack, tile, rims = call(
         start_kernel,
-        [(8, ROWS, COLS), (48, 128), (32, 128), (2, 24, 128)],
+        [(8, ROWS, COLS), (48, 128), (2, 24, 128)],
         right_side, diagonal, east_face, north_face, wet, active[0], coupling[0, 0],
         fetch=range(7),
         room=FETCH_BYTES,
     )
-    window = [tile if g == 2 else shift(tile if g in (1, 3) else part, "z", NZ, 2 - g) for g in range(NG)]
+    window = ring_window(tile)
     (plane,) = call(gather_kernel, [(NX * 4, 152, 128)], *window, rims, fetch=(2, 5))
     plane = lax.all_to_all(plane, ("x", "y"), 0, 0)
     blocks = to_all(plane, "c", 2).reshape(32, 152, 128)
 
-    pivot_rows = [pivots[0] if g == 2 else shift(pivots[0], "z", NZ, 2 - g) for g in range(NG)]
+    pivot_rows = ring_window(pivots[0])
 
     ring, rim = (NZ, NG, 4, 128), (M, EXT_ROWS, EXT_COLS)
     weights = ((NB * NG, 128, 128), BF16)

time: 152 us -> 149 us (0.980)
  blocking collectives: 92 us -> 90.3 us
    all_to_all x1, waiting for transfers between devices: 3.69 us -> 1.2 us  [body(): plane = lax.all_to_all(plane, ('x', 'y'), 0, 0)]
    ppermute x8, waiting for transfers between devices: 1.07 us -> 3.04 us  [shift(): lax.ppermute(value, axes, [(i, (i + by) % count) for i in range(count)])]
    all_to_all x2, blocking collectives: 31.4 us -> 29.7 us  [body(): got = lax.all_to_all(message, ('x', 'y', 'c'), 0, 0)]
  transfers between devices with their start and end apart: 9 -> 9, of which waited for: 2 -> 3; matrix products, arithmetic and copies ran while one was open for 0% -> 0% of each run, Pallas kernels for 1% -> 2%
where the time goes in v5:
time: 149 us; the launch traced here: 148 us
  blocking collectives  90.3 us (61%)
  starting transfers between devices  40.5 us (27%)
  Pallas kernels  11.6 us (8%)
  waiting for transfers between devices  4.24 us (3%)
  local copies, waits for them, and re-layouts  1.65 us (1%)
    all_to_all x2, blocking collectives, body(): got = lax.all_to_all(swept, 'z', 0, 0)  35.6 us
    ppermute x8, starting transfers between devices, shift(): lax.ppermute(value, axes, [(i, (i + by) % count) for i in range(count)])  33.6 us
    all_to_all x2, blocking collectives, body(): got = lax.all_to_all(message, ('x', 'y', 'c'), 0, 0)  29.7 us
    all_to_all x1, blocking collectives, body(): got = lax.all_to_all(dots, 'z', 0, 0)  16.1 us
    pallas_call x10, Pallas kernels, call(): pl.pallas_call(whole, out_shape=[jax.ShapeDtypeStruct(s, d) for s, d in o...  11.6 us
    all_to_all x1, blocking collectives, to_all(): lax.all_to_all(jnp.broadcast_to(value[None], (count,) + value.shape), axe...  8.98 us
    all_to_all x1, starting transfers between devices, body(): plane = lax.all_to_all(plane, ('x', 'y'), 0, 0)  6.9 us
    ppermute x8, waiting for transfers between devices, shift(): lax.ppermute(value, axes, [(i, (i + by) % count) for i in range(count)])  3.04 us
  transfers between devices with their start and end apart: 9, of which 3 were waited for; matrix products, arithmetic and copies ran while one was open for 0% of the time, Pallas kernels for 2%

profile of v5, /device:TPU:1, one launch (start us, length us, event | category | flops | bytes accessed | tf_op | source)
XLA Modules:
  0.0 148.5 jit_solution(17207748688188368829)
XLA Ops:
  0.0 1.8 %shard_map.82 = (f32[8,32,128]{2,1,0:T(8,128)}, f32[48,128]{1,0:T(8,128)}, f32[2,24,128]{2,1,0:T(8,128)}) custom-call(f32[4,32,128]{2,1,0:T(8,128)} %refs_0_.1, f32[32,128]{1,0:T(8,128)} %refs_1_.1, f32[32,128]{1,0:T(8,128)} %refs_2_.1, f32[32,128]{1,0:T(8,128)} %refs_3_.1, s32[32,128]{1,0:T(8,128)} %refs_4_.1, s32[1,32]{1,0:T(1,128)} %bitcast.15, ...), custom_call_target="tpu_custom_call" | custom-call | tf_op jit(solution)/shard_map/pallas_call | solution.py:48
  1.8 4.4 %collective-permute-start = (f32[48,128]{1,0:T(8,128)}, f32[48,128]{1,0:T(8,128)S(1)}, u32[]{:S(2)}, u32[]{:S(2)}) collective-permute-start(f32[48,128]{1,0:T(8,128)} %get-tuple-element.37.refs_2_), channel_id=1, source_target_pairs={{0,32},{32,64},{64,96},{96,128},{128,160},{160,192},{192,224},{224... | collective-permute-start | bytes 73736 | tf_op jit(solution)/shard_map/ppermute | solution.py:609
  6.2 9.5 %collective-permute-start.2 = (f32[48,128]{1,0:T(8,128)}, f32[48,128]{1,0:T(8,128)S(1)}, u32[]{:S(2)}, u32[]{:S(2)}) collective-permute-start(f32[48,128]{1,0:T(8,128)} %get-tuple-element.37.refs_2_), channel_id=1, source_target_pairs={{0,480},{32,0},{64,32},{96,64},{128,96},{160,128},{192,160},{224,1... | collective-permute-start | bytes 73736 | tf_op jit(solution)/shard_map/ppermute | solution.py:609
  15.7 0.0 collective-permute-done.refs_1_
  15.7 1.9 %collective-permute-start.1 = (f32[48,128]{1,0:T(8,128)S(1)}, f32[48,128]{1,0:T(8,128)S(1)}, u32[]{:S(2)}, u32[]{:S(2)}) collective-permute-start(f32[48,128]{1,0:T(8,128)S(1)} %collective-permute-done.refs_1_), channel_id=1, source_target_pairs={{0,32},{32,64},{64,96},{96,128},{128,160},{160,192},{192,224},{224... | collective-permute-start | bytes 73736 | tf_op jit(solution)/shard_map/ppermute | solution.py:609
  17.6 0.0 collective-permute-done.2.refs_3_
  17.6 4.6 %collective-permute-start.3 = (f32[48,128]{1,0:T(8,128)S(1)}, f32[48,128]{1,0:T(8,128)S(1)}, u32[]{:S(2)}, u32[]{:S(2)}) collective-permute-start(f32[48,128]{1,0:T(8,128)S(1)} %collective-permute-done.2.refs_3_), channel_id=1, source_target_pairs={{0,480},{32,0},{64,32},{96,64},{128,96},{160,128},{192,160},{224,1... | collective-permute-start | bytes 73736 | tf_op jit(solution)/shard_map/ppermute | solution.py:609
  22.2 0.0 collective-permute-done.1.refs_0_
  22.2 0.9 collective-permute-done.3.refs_4_
  23.1 0.0 copy-start.2
  23.1 0.7 copy-done.2
  23.9 0.0 copy-start.3
  23.9 0.7 copy-done.3
  24.6 1.2 shard_map.83
  25.8 0.0 copy-start
  25.8 6.9 %all-to-all-start = ((f32[16,152,128]{2,1,0:T(8,128)}), f32[16,152,128]{2,1,0:T(8,128)S(1)}, u32[]{:S(2)}, u32[]{:S(2)}) async-start(f32[16,152,128]{2,1,0:T(8,128)} %shard_map.83), calls=%async_computation | async-start | bytes 2490368 | tf_op jit(solution)/shard_map/all_to_all | solution.py:631
  32.7 0.0 copy-done
  32.7 1.9 %collective-permute-start.4 = (f32[32,2048]{1,0:T(8,128)S(1)}, f32[32,2048]{1,0:T(8,128)S(1)}, u32[]{:S(2)}, u32[]{:S(2)}) collective-permute-start(f32[32,2048]{1,0:T(8,128)S(1)} %bitcast.8), channel_id=1, source_target_pairs={{0,32},{32,64},{64,96},{96,128},{128,160},{160,192},{192,224},{224... | collective-permute-start | bytes 786440 | tf_op jit(solution)/shard_map/ppermute | solution.py:609
  34.7 4.8 %collective-permute-start.6 = (f32[32,2048]{1,0:T(8,128)S(1)}, f32[32,2048]{1,0:T(8,128)S(1)}, u32[]{:S(2)}, u32[]{:S(2)}) collective-permute-start(f32[32,2048]{1,0:T(8,128)S(1)} %bitcast.9), channel_id=1, source_target_pairs={{0,480},{32,0},{64,32},{96,64},{128,96},{160,128},{192,160},{224,1... | collective-permute-start | bytes 786440 | tf_op jit(solution)/shard_map/ppermute | solution.py:609
  39.5 2.1 %collective-permute-done.4.refs_3_.refs_5_ = f32[32,2048]{1,0:T(8,128)S(1)} collective-permute-done((f32[32,2048]{1,0:T(8,128)S(1)}, f32[32,2048]{1,0:T(8,128)S(1)}, u32[]{:S(2)}, u32[]{:S(2)}) %collective-permute-start.4) | collective-permute-done | bytes 262176 | tf_op jit(solution)/shard_map/ppermute | solution.py:609
  41.6 1.9 %collective-permute-start.5 = (f32[32,2048]{1,0:T(8,128)S(1)}, f32[32,2048]{1,0:T(8,128)S(1)}, u32[]{:S(2)}, u32[]{:S(2)}) collective-permute-start(f32[32,2048]{1,0:T(8,128)S(1)} %collective-permute-done.4.refs_3_.refs_5_), channel_id=1, source_target_pairs={{0,32},{32,64},{64,96},{96,128},{128,160},{160,192},{192,224},{224... | collective-permute-start | bytes 786440 | tf_op jit(solution)/shard_map/ppermute | solution.py:609
  43.5 0.0 collective-permute-done.6.refs_5_.refs_7_
  43.5 4.6 %collective-permute-start.7 = (f32[32,2048]{1,0:T(8,128)S(1)}, f32[32,2048]{1,0:T(8,128)S(1)}, u32[]{:S(2)}, u32[]{:S(2)}) collective-permute-start(f32[32,2048]{1,0:T(8,128)S(1)} %collective-permute-done.6.refs_5_.refs_7_), channel_id=1, source_target_pairs={{0,480},{32,0},{64,32},{96,64},{128,96},{160,128},{192,160},{224,1... | collective-permute-start | bytes 786440 | tf_op jit(solution)/shard_map/ppermute | solution.py:609
  48.1 1.2 all-to-all-done
  49.3 0.2 broadcast_in_dim.2
  49.5 9.0 %all_to_all.35 = f32[2,16,152,128]{3,2,1,0:T(8,128)S(1)} all-to-all(f32[2,16,152,128]{3,2,1,0:T(8,128)S(1)} %broadcast_in_dim.2), channel_id=1, replica_groups=mesh['z'=16,'x'=4,'y'=4,'c'=2] {'c'}, dimensions={0} | all-to-all | bytes 4980736 | tf_op jit(solution)/shard_map/all_to_all | solution.py:618
  58.5 0.0 copy-start.1
  58.5 1.6 %shard_map.84 = (f32[16,4,128]{2,1,0:T(4,128)S(1)}, f32[64,128]{1,0:T(8,128)S(1)}, f32[3,64,128]{2,1,0:T(8,128)S(1)}, bf16[40,128,128]{2,1,0:T(8,128)(2,1)S(1)}, bf16[40,128,128]{2,1,0:T(8,128)(2,1)S(1)}) custom-call(f32[32,152,128]{2,1,0:T(8,128)S(1)} %bitcast.6), custom_call_target="tpu_custom_call" | custom-call | tf_op jit(solution)/shard_map/pallas_call | solution.py:48
  60.1 0.0 copy-done.1
  60.1 0.6 shard_map.85
  60.7 0.0 collective-permute-done.5.refs_2_.refs_4_
  60.7 0.0 collective-permute-done.7.refs_6_.refs_8_
  60.8 20.2 %all_to_all.36.refs_0_ = f32[16,4,128]{2,1,0:T(4,128)S(1)} all-to-all(f32[16,4,128]{2,1,0:T(4,128)S(1)} %get-tuple-element.42), channel_id=1, replica_groups=mesh['z'=16,'x'=4,'y'=4,'c'=2] {'z'}, dimensions={0} | all-to-all | bytes 65536 | tf_op jit(solution)/shard_map/all_to_all | solution.py:645
  81.0 0.5 shard_map.86
  81.6 15.9 %all_to_all.37.refs_0_ = f32[32,4,384]{2,1,0:T(4,128)S(1)} all-to-all(f32[32,4,384]{2,1,0:T(4,128)S(1)} %shard_map.86), channel_id=1, replica_groups=mesh['z'=16,'x'=4,'y'=4,'c'=2] {'x','y','c'}, dimensions={0} | all-to-all | bytes 393216 | tf_op jit(solution)/shard_map/all_to_all | solution.py:647
  97.4 2.7 %shard_map.87 = (f32[16,5,4,128]{3,2,1,0:T(4,128)S(1)}, f32[3,64,128]{2,1,0:T(8,128)S(1)}, f32[64,128]{1,0:T(8,128)S(1)}, f32[5,64,128]{2,1,0:T(8,128)S(1)}) custom-call(f32[32,4,384]{2,1,0:T(4,128)S(1)} %all_to_all.37.refs_0_, bf16[40,128,128]{2,1,0:T(8,128)(2,1)S(1)} %get-tuple-element.49.refs_1_, bf16[40,128,128]{2,1,0:T(8,128)(2,1)S(1)} %get-tuple-element.50.refs_2_, ...), custom_call_target="tpu_custom_call" | custom-call | tf_op jit(solution)/shard_map/pallas_call | solution.py:48
  100.2 0.3 shard_map.88
  100.4 15.3 %all_to_all.38.refs_0_ = f32[16,5,4,128]{3,2,1,0:T(4,128)S(1)} all-to-all(f32[16,5,4,128]{3,2,1,0:T(4,128)S(1)} %get-tuple-element.59), channel_id=1, replica_groups=mesh['z'=16,'x'=4,'y'=4,'c'=2] {'z'}, dimensions={0} | all-to-all | bytes 327680 | tf_op jit(solution)/shard_map/all_to_all | solution.py:653
  115.7 0.6 shard_map.89
  116.3 13.8 %all_to_all.39.refs_0_ = f32[32,4,256]{2,1,0:T(4,128)S(1)} all-to-all(f32[32,4,256]{2,1,0:T(4,128)S(1)} %get-tuple-element.61), channel_id=1, replica_groups=mesh['z'=16,'x'=4,'y'=4,'c'=2] {'x','y','c'}, dimensions={0} | all-to-all | bytes 262144 | tf_op jit(solution)/shard_map/all_to_all | solution.py:657
  130.1 1.4 shard_map.90
  131.5 16.1 %all_to_all.40.refs_0_ = f32[16,4,128]{2,1,0:T(4,128)S(1)} all-to-all(f32[16,4,128]{2,1,0:T(4,128)S(1)} %get-tuple-element.65), channel_id=1, replica_groups=mesh['z'=16,'x'=4,'y'=4,'c'=2] {'z'}, dimensions={0} | all-to-all | bytes 65536 | tf_op jit(solution)/shard_map/all_to_all | solution.py:661
  147.6 0.9 shard_map.91
Async XLA Ops:
  1.8 13.9 %collective-permute-start = (f32[48,128]{1,0:T(8,128)}, f32[48,128]{1,0:T(8,128)S(1)}, u32[]{:S(2)}, u32[]{:S(2)}) collective-permute-start(f32[48,128]{1,0:T(8,128)} %get-tuple-element.37.refs_2_), channel_id=1, source_target_pairs={{0,32},{32,64},{64,96},{96,128},{128,160},{160,192},{192,224},{224... | collective-permute-start | bytes 73736 | tf_op jit(solution)/shard_map/ppermute | solution.py:609
  6.2 11.4 %collective-permute-start.2 = (f32[48,128]{1,0:T(8,128)}, f32[48,128]{1,0:T(8,128)S(1)}, u32[]{:S(2)}, u32[]{:S(2)}) collective-permute-start(f32[48,128]{1,0:T(8,128)} %get-tuple-element.37.refs_2_), channel_id=1, source_target_pairs={{0,480},{32,0},{64,32},{96,64},{128,96},{160,128},{192,160},{224,1... | collective-permute-start | bytes 73736 | tf_op jit(solution)/shard_map/ppermute | solution.py:609
  15.7 6.5 %collective-permute-start.1 = (f32[48,128]{1,0:T(8,128)S(1)}, f32[48,128]{1,0:T(8,128)S(1)}, u32[]{:S(2)}, u32[]{:S(2)}) collective-permute-start(f32[48,128]{1,0:T(8,128)S(1)} %collective-permute-done.refs_1_), channel_id=1, source_target_pairs={{0,32},{32,64},{64,96},{96,128},{128,160},{160,192},{192,224},{224... | collective-permute-start | bytes 73736 | tf_op jit(solution)/shard_map/ppermute | solution.py:609
  17.6 5.5 %collective-permute-start.3 = (f32[48,128]{1,0:T(8,128)S(1)}, f32[48,128]{1,0:T(8,128)S(1)}, u32[]{:S(2)}, u32[]{:S(2)}) collective-permute-start(f32[48,128]{1,0:T(8,128)S(1)} %collective-permute-done.2.refs_3_), channel_id=1, source_target_pairs={{0,480},{32,0},{64,32},{96,64},{128,96},{160,128},{192,160},{224,1... | collective-permute-start | bytes 73736 | tf_op jit(solution)/shard_map/ppermute | solution.py:609
  23.1 0.7 copy-start.2
  23.9 0.7 copy-start.3
  25.8 6.9 %copy-start = (f32[1,32,2048]{2,1,0:T(8,128)S(1)}, f32[1,32,2048]{2,1,0:T(8,128)}, u32[]{:S(2)}) copy-start(f32[1,32,2048]{2,1,0:T(8,128)} %param.15) | copy-start | bytes 786436
  25.8 23.5 %all-to-all-start = ((f32[16,152,128]{2,1,0:T(8,128)}), f32[16,152,128]{2,1,0:T(8,128)S(1)}, u32[]{:S(2)}, u32[]{:S(2)}) async-start(f32[16,152,128]{2,1,0:T(8,128)} %shard_map.83), calls=%async_computation | async-start | bytes 2490368 | tf_op jit(solution)/shard_map/all_to_all | solution.py:631
  32.7 8.9 %collective-permute-start.4 = (f32[32,2048]{1,0:T(8,128)S(1)}, f32[32,2048]{1,0:T(8,128)S(1)}, u32[]{:S(2)}, u32[]{:S(2)}) collective-permute-start(f32[32,2048]{1,0:T(8,128)S(1)} %bitcast.8), channel_id=1, source_target_pairs={{0,32},{32,64},{64,96},{96,128},{128,160},{160,192},{192,224},{224... | collective-permute-start | bytes 786440 | tf_op jit(solution)/shard_map/ppermute | solution.py:609
  34.7 8.9 %collective-permute-start.6 = (f32[32,2048]{1,0:T(8,128)S(1)}, f32[32,2048]{1,0:T(8,128)S(1)}, u32[]{:S(2)}, u32[]{:S(2)}) collective-permute-start(f32[32,2048]{1,0:T(8,128)S(1)} %bitcast.9), channel_id=1, source_target_pairs={{0,480},{32,0},{64,32},{96,64},{128,96},{160,128},{192,160},{224,1... | collective-permute-start | bytes 786440 | tf_op jit(solution)/shard_map/ppermute | solution.py:609
  41.6 19.1 %collective-permute-start.5 = (f32[32,2048]{1,0:T(8,128)S(1)}, f32[32,2048]{1,0:T(8,128)S(1)}, u32[]{:S(2)}, u32[]{:S(2)}) collective-permute-start(f32[32,2048]{1,0:T(8,128)S(1)} %collective-permute-done.4.refs_3_.refs_5_), channel_id=1, source_target_pairs={{0,32},{32,64},{64,96},{96,128},{128,160},{160,192},{192,224},{224... | collective-permute-start | bytes 786440 | tf_op jit(solution)/shard_map/ppermute | solution.py:609
  43.5 17.2 %collective-permute-start.7 = (f32[32,2048]{1,0:T(8,128)S(1)}, f32[32,2048]{1,0:T(8,128)S(1)}, u32[]{:S(2)}, u32[]{:S(2)}) collective-permute-start(f32[32,2048]{1,0:T(8,128)S(1)} %collective-permute-done.6.refs_5_.refs_7_), channel_id=1, source_target_pairs={{0,480},{32,0},{64,32},{96,64},{128,96},{160,128},{192,160},{224,1... | collective-permute-start | bytes 786440 | tf_op jit(solution)/shard_map/ppermute | solution.py:609
  58.5 1.6 %copy-start.1 = (f32[8,32,128]{2,1,0:T(8,128)S(1)}, f32[8,32,128]{2,1,0:T(8,128)}, u32[]{:S(2)}) copy-start(f32[8,32,128]{2,1,0:T(8,128)} %get-tuple-element.40.refs_0_.refs_4_) | copy-start | bytes 393220

commit v6 on v5

--- a/solution.py
+++ b/solution.py
@@ -176,6 +176,11 @@
     packed = pick([jnp.broadcast_to(r, (8, 128)) for r in rows]) * act
     row = iota((8, 128), 0)
     tile[24:32, :] = jnp.where(row == 0, packed, jnp.where(row == 1, act, 0.0))
+
+
+def own_kernel(pos, tile, rims, tile_out, rims_out):
+    tile_out[...] = tile[...]
+    rims_out[...] = rims[...]
 
 
 def gather_kernel(pos, t0, t1, t2, t3, t4, rims, out):
@@ -627,7 +632,8 @@
         room=FETCH_BYTES,
     )
     window = ring_window(tile)
-    (plane,) = call(gather_kernel, [(NX * 4, 152, 128)], *window, rims, fetch=(2, 5))
+    window[2], rims = call(own_kernel, [(48, 128), (2, 24, 128)], tile, rims)
+    (plane,) = call(gather_kernel, [(NX * 4, 152, 128)], *window, rims)
     plane = lax.all_to_all(plane, ("x", "y"), 0, 0)
     blocks = to_all(plane, "c", 2).reshape(32, 152, 128)
 

time: 149 us -> 148 us (level)
    pallas_call x10 -> x11, Pallas kernels: 11.6 us -> 11.6 us  [call(): pl.pallas_call(whole, out_shape=[jax.ShapeDtypeStruct(s, d) for s, d in o...]
  transfers between devices with their start and end apart: 9 -> 9, of which waited for: 3 -> 2; matrix products, arithmetic and copies ran while one was open for 0% -> 0% of each run, Pallas kernels for 2% -> 2%
where the time goes in v6:
time: 148 us; the launch traced here: 147 us
  blocking collectives  89.2 us (60%)
  starting transfers between devices  40.2 us (27%)
  Pallas kernels  11.6 us (8%)
  waiting for transfers between devices  4.07 us (3%)
  local copies, waits for them, and re-layouts  1.64 us (1%)
    all_to_all x2, blocking collectives, body(): got = lax.all_to_all(swept, 'z', 0, 0)  34.8 us
    ppermute x8, starting transfers between devices, shift(): lax.ppermute(value, axes, [(i, (i + by) % count) for i in range(count)])  33.3 us
    all_to_all x2, blocking collectives, body(): got = lax.all_to_all(message, ('x', 'y', 'c'), 0, 0)  29.4 us
    all_to_all x1, blocking collectives, body(): got = lax.all_to_all(dots, 'z', 0, 0)  16.1 us
    pallas_call x11, Pallas kernels, call(): pl.pallas_call(whole, out_shape=[jax.ShapeDtypeStruct(s, d) for s, d in o...  11.6 us
    all_to_all x1, blocking collectives, to_all(): lax.all_to_all(jnp.broadcast_to(value[None], (count,) + value.shape), axe...  8.95 us
    all_to_all x1, starting transfers between devices, body(): plane = lax.all_to_all(plane, ('x', 'y'), 0, 0)  6.89 us
  transfers between devices with their start and end apart: 9, of which 2 were waited for; matrix products, arithmetic and copies ran while one was open for 0% of the time, Pallas kernels for 2%

profile of v6, /device:TPU:1, one launch (start us, length us, event | category | flops | bytes accessed | tf_op | source)
XLA Modules:
  0.0 147.0 jit_solution(7214205737643962485)
XLA Ops:
  0.0 1.8 %shard_map.82 = (f32[8,32,128]{2,1,0:T(8,128)}, f32[48,128]{1,0:T(8,128)}, f32[2,24,128]{2,1,0:T(8,128)}) custom-call(f32[4,32,128]{2,1,0:T(8,128)} %refs_0_.1, f32[32,128]{1,0:T(8,128)} %refs_1_.1, f32[32,128]{1,0:T(8,128)} %refs_2_.1, f32[32,128]{1,0:T(8,128)} %refs_3_.1, s32[32,128]{1,0:T(8,128)} %refs_4_.1, s32[1,32]{1,0:T(1,128)} %bitcast.15, ...), custom_call_target="tpu_custom_call" | custom-call | tf_op jit(solution)/shard_map/pallas_call | solution.py:48
  1.8 4.4 %collective-permute-start = (f32[48,128]{1,0:T(8,128)}, f32[48,128]{1,0:T(8,128)S(1)}, u32[]{:S(2)}, u32[]{:S(2)}) collective-permute-start(f32[48,128]{1,0:T(8,128)} %get-tuple-element.39.refs_0_), channel_id=1, source_target_pairs={{0,32},{32,64},{64,96},{96,128},{128,160},{160,192},{192,224},{224... | collective-permute-start | bytes 73736 | tf_op jit(solution)/shard_map/ppermute | solution.py:614
  6.2 9.5 %collective-permute-start.2 = (f32[48,128]{1,0:T(8,128)}, f32[48,128]{1,0:T(8,128)S(1)}, u32[]{:S(2)}, u32[]{:S(2)}) collective-permute-start(f32[48,128]{1,0:T(8,128)} %get-tuple-element.39.refs_0_), channel_id=1, source_target_pairs={{0,480},{32,0},{64,32},{96,64},{128,96},{160,128},{192,160},{224,1... | collective-permute-start | bytes 73736 | tf_op jit(solution)/shard_map/ppermute | solution.py:614
  15.7 0.0 collective-permute-done.refs_1_
  15.7 1.9 %collective-permute-start.1 = (f32[48,128]{1,0:T(8,128)S(1)}, f32[48,128]{1,0:T(8,128)S(1)}, u32[]{:S(2)}, u32[]{:S(2)}) collective-permute-start(f32[48,128]{1,0:T(8,128)S(1)} %collective-permute-done.refs_1_), channel_id=1, source_target_pairs={{0,32},{32,64},{64,96},{96,128},{128,160},{160,192},{192,224},{224... | collective-permute-start | bytes 73736 | tf_op jit(solution)/shard_map/ppermute | solution.py:614
  17.6 0.0 collective-permute-done.2.refs_3_
  17.6 4.6 %collective-permute-start.3 = (f32[48,128]{1,0:T(8,128)S(1)}, f32[48,128]{1,0:T(8,128)S(1)}, u32[]{:S(2)}, u32[]{:S(2)}) collective-permute-start(f32[48,128]{1,0:T(8,128)S(1)} %collective-permute-done.2.refs_3_), channel_id=1, source_target_pairs={{0,480},{32,0},{64,32},{96,64},{128,96},{160,128},{192,160},{224,1... | collective-permute-start | bytes 73736 | tf_op jit(solution)/shard_map/ppermute | solution.py:614
  22.2 0.0 copy-start.2
  22.2 0.7 copy-done.2
  22.9 0.0 copy-start.3
  22.9 0.7 copy-done.3
  23.7 0.0 collective-permute-done.1.refs_0_
  23.7 0.0 collective-permute-done.3.refs_4_
  23.7 1.2 shard_map.84
  24.8 0.0 copy-start
  24.9 6.9 %all-to-all-start = ((f32[16,152,128]{2,1,0:T(8,128)}), f32[16,152,128]{2,1,0:T(8,128)S(1)}, u32[]{:S(2)}, u32[]{:S(2)}) async-start(f32[16,152,128]{2,1,0:T(8,128)} %shard_map.84), calls=%async_computation | async-start | bytes 2490368 | tf_op jit(solution)/shard_map/all_to_all | solution.py:637
  31.7 0.0 copy-done
  31.8 1.9 %collective-permute-start.4 = (f32[32,2048]{1,0:T(8,128)S(1)}, f32[32,2048]{1,0:T(8,128)S(1)}, u32[]{:S(2)}, u32[]{:S(2)}) collective-permute-start(f32[32,2048]{1,0:T(8,128)S(1)} %bitcast.8), channel_id=1, source_target_pairs={{0,32},{32,64},{64,96},{96,128},{128,160},{160,192},{192,224},{224... | collective-permute-start | bytes 786440 | tf_op jit(solution)/shard_map/ppermute | solution.py:614
  33.7 4.6 %collective-permute-start.6 = (f32[32,2048]{1,0:T(8,128)S(1)}, f32[32,2048]{1,0:T(8,128)S(1)}, u32[]{:S(2)}, u32[]{:S(2)}) collective-permute-start(f32[32,2048]{1,0:T(8,128)S(1)} %bitcast.9), channel_id=1, source_target_pairs={{0,480},{32,0},{64,32},{96,64},{128,96},{160,128},{192,160},{224,1... | collective-permute-start | bytes 786440 | tf_op jit(solution)/shard_map/ppermute | solution.py:614
  38.3 2.3 %collective-permute-done.4.refs_3_.refs_5_ = f32[32,2048]{1,0:T(8,128)S(1)} collective-permute-done((f32[32,2048]{1,0:T(8,128)S(1)}, f32[32,2048]{1,0:T(8,128)S(1)}, u32[]{:S(2)}, u32[]{:S(2)}) %collective-permute-start.4) | collective-permute-done | bytes 262176 | tf_op jit(solution)/shard_map/ppermute | solution.py:614
  40.5 1.9 %collective-permute-start.5 = (f32[32,2048]{1,0:T(8,128)S(1)}, f32[32,2048]{1,0:T(8,128)S(1)}, u32[]{:S(2)}, u32[]{:S(2)}) collective-permute-start(f32[32,2048]{1,0:T(8,128)S(1)} %collective-permute-done.4.refs_3_.refs_5_), channel_id=1, source_target_pairs={{0,32},{32,64},{64,96},{96,128},{128,160},{160,192},{192,224},{224... | collective-permute-start | bytes 786440 | tf_op jit(solution)/shard_map/ppermute | solution.py:614
  42.4 0.0 collective-permute-done.6.refs_5_.refs_7_
  42.4 4.6 %collective-permute-start.7 = (f32[32,2048]{1,0:T(8,128)S(1)}, f32[32,2048]{1,0:T(8,128)S(1)}, u32[]{:S(2)}, u32[]{:S(2)}) collective-permute-start(f32[32,2048]{1,0:T(8,128)S(1)} %collective-permute-done.6.refs_5_.refs_7_), channel_id=1, source_target_pairs={{0,480},{32,0},{64,32},{96,64},{128,96},{160,128},{192,160},{224,1... | collective-permute-start | bytes 786440 | tf_op jit(solution)/shard_map/ppermute | solution.py:614
  47.0 1.8 %all-to-all-done = f32[16,152,128]{2,1,0:T(8,128)S(1)} async-done(((f32[16,152,128]{2,1,0:T(8,128)}), f32[16,152,128]{2,1,0:T(8,128)S(1)}, u32[]{:S(2)}, u32[]{:S(2)}) %all-to-all-start) | async-done | bytes 1245216 | tf_op jit(solution)/shard_map/all_to_all | solution.py:637
  48.8 0.2 broadcast_in_dim.2
  49.0 9.0 %all_to_all.35 = f32[2,16,152,128]{3,2,1,0:T(8,128)S(1)} all-to-all(f32[2,16,152,128]{3,2,1,0:T(8,128)S(1)} %broadcast_in_dim.2), channel_id=1, replica_groups=mesh['z'=16,'x'=4,'y'=4,'c'=2] {'c'}, dimensions={0} | all-to-all | bytes 4980736 | tf_op jit(solution)/shard_map/all_to_all | solution.py:623
  57.9 0.0 copy-start.1
  57.9 1.6 %shard_map.85 = (f32[16,4,128]{2,1,0:T(4,128)S(1)}, f32[64,128]{1,0:T(8,128)S(1)}, f32[3,64,128]{2,1,0:T(8,128)S(1)}, bf16[40,128,128]{2,1,0:T(8,128)(2,1)S(1)}, bf16[40,128,128]{2,1,0:T(8,128)(2,1)S(1)}) custom-call(f32[32,152,128]{2,1,0:T(8,128)S(1)} %bitcast.6), custom_call_target="tpu_custom_call" | custom-call | tf_op jit(solution)/shard_map/pallas_call | solution.py:48
  59.5 0.0 copy-done.1
  59.6 0.6 shard_map.86
  60.2 0.0 collective-permute-done.5.refs_2_.refs_4_
  60.2 0.0 collective-permute-done.7.refs_6_.refs_8_
  60.2 19.5 %all_to_all.36.refs_0_ = f32[16,4,128]{2,1,0:T(4,128)S(1)} all-to-all(f32[16,4,128]{2,1,0:T(4,128)S(1)} %get-tuple-element.46), channel_id=1, replica_groups=mesh['z'=16,'x'=4,'y'=4,'c'=2] {'z'}, dimensions={0} | all-to-all | bytes 65536 | tf_op jit(solution)/shard_map/all_to_all | solution.py:651
  79.7 0.5 shard_map.87
  80.2 15.6 %all_to_all.37.refs_0_ = f32[32,4,384]{2,1,0:T(4,128)S(1)} all-to-all(f32[32,4,384]{2,1,0:T(4,128)S(1)} %shard_map.87), channel_id=1, replica_groups=mesh['z'=16,'x'=4,'y'=4,'c'=2] {'x','y','c'}, dimensions={0} | all-to-all | bytes 393216 | tf_op jit(solution)/shard_map/all_to_all | solution.py:653
  95.9 2.7 %shard_map.88 = (f32[16,5,4,128]{3,2,1,0:T(4,128)S(1)}, f32[3,64,128]{2,1,0:T(8,128)S(1)}, f32[64,128]{1,0:T(8,128)S(1)}, f32[5,64,128]{2,1,0:T(8,128)S(1)}) custom-call(f32[32,4,384]{2,1,0:T(4,128)S(1)} %all_to_all.37.refs_0_, bf16[40,128,128]{2,1,0:T(8,128)(2,1)S(1)} %get-tuple-element.53.refs_1_, bf16[40,128,128]{2,1,0:T(8,128)(2,1)S(1)} %get-tuple-element.54.refs_2_, ...), custom_call_target="tpu_custom_call" | custom-call | tf_op jit(solution)/shard_map/pallas_call | solution.py:48
  98.6 0.3 shard_map.89
  98.9 15.3 %all_to_all.38.refs_0_ = f32[16,5,4,128]{3,2,1,0:T(4,128)S(1)} all-to-all(f32[16,5,4,128]{3,2,1,0:T(4,128)S(1)} %get-tuple-element.63), channel_id=1, replica_groups=mesh['z'=16,'x'=4,'y'=4,'c'=2] {'z'}, dimensions={0} | all-to-all | bytes 327680 | tf_op jit(solution)/shard_map/all_to_all | solution.py:659
  114.2 0.6 shard_map.90
  114.8 13.8 %all_to_all.39.refs_0_ = f32[32,4,256]{2,1,0:T(4,128)S(1)} all-to-all(f32[32,4,256]{2,1,0:T(4,128)S(1)} %get-tuple-element.65), channel_id=1, replica_groups=mesh['z'=16,'x'=4,'y'=4,'c'=2] {'x','y','c'}, dimensions={0} | all-to-all | bytes 262144 | tf_op jit(solution)/shard_map/all_to_all | solution.py:663
  128.6 1.4 shard_map.91
  130.0 16.1 %all_to_all.40.refs_0_ = f32[16,4,128]{2,1,0:T(4,128)S(1)} all-to-all(f32[16,4,128]{2,1,0:T(4,128)S(1)} %get-tuple-element.69), channel_id=1, replica_groups=mesh['z'=16,'x'=4,'y'=4,'c'=2] {'z'}, dimensions={0} | all-to-all | bytes 65536 | tf_op jit(solution)/shard_map/all_to_all | solution.py:667
  146.0 0.9 shard_map.92
  (1 shorter events, 0.0 us)
Async XLA Ops:
  1.8 13.9 %collective-permute-start = (f32[48,128]{1,0:T(8,128)}, f32[48,128]{1,0:T(8,128)S(1)}, u32[]{:S(2)}, u32[]{:S(2)}) collective-permute-start(f32[48,128]{1,0:T(8,128)} %get-tuple-element.39.refs_0_), channel_id=1, source_target_pairs={{0,32},{32,64},{64,96},{96,128},{128,160},{160,192},{192,224},{224... | collective-permute-start | bytes 73736 | tf_op jit(solution)/shard_map/ppermute | solution.py:614
  6.2 11.4 %collective-permute-start.2 = (f32[48,128]{1,0:T(8,128)}, f32[48,128]{1,0:T(8,128)S(1)}, u32[]{:S(2)}, u32[]{:S(2)}) collective-permute-start(f32[48,128]{1,0:T(8,128)} %get-tuple-element.39.refs_0_), channel_id=1, source_target_pairs={{0,480},{32,0},{64,32},{96,64},{128,96},{160,128},{192,160},{224,1... | collective-permute-start | bytes 73736 | tf_op jit(solution)/shard_map/ppermute | solution.py:614
  15.7 8.0 %collective-permute-start.1 = (f32[48,128]{1,0:T(8,128)S(1)}, f32[48,128]{1,0:T(8,128)S(1)}, u32[]{:S(2)}, u32[]{:S(2)}) collective-permute-start(f32[48,128]{1,0:T(8,128)S(1)} %collective-permute-done.refs_1_), channel_id=1, source_target_pairs={{0,32},{32,64},{64,96},{96,128},{128,160},{160,192},{192,224},{224... | collective-permute-start | bytes 73736 | tf_op jit(solution)/shard_map/ppermute | solution.py:614
  17.6 6.1 %collective-permute-start.3 = (f32[48,128]{1,0:T(8,128)S(1)}, f32[48,128]{1,0:T(8,128)S(1)}, u32[]{:S(2)}, u32[]{:S(2)}) collective-permute-start(f32[48,128]{1,0:T(8,128)S(1)} %collective-permute-done.2.refs_3_), channel_id=1, source_target_pairs={{0,480},{32,0},{64,32},{96,64},{128,96},{160,128},{192,160},{224,1... | collective-permute-start | bytes 73736 | tf_op jit(solution)/shard_map/ppermute | solution.py:614
  22.2 0.7 copy-start.2
  22.9 0.7 copy-start.3
  24.8 6.9 %copy-start = (f32[1,32,2048]{2,1,0:T(8,128)S(1)}, f32[1,32,2048]{2,1,0:T(8,128)}, u32[]{:S(2)}) copy-start(f32[1,32,2048]{2,1,0:T(8,128)} %param.15) | copy-start | bytes 786436
  24.9 24.0 %all-to-all-start = ((f32[16,152,128]{2,1,0:T(8,128)}), f32[16,152,128]{2,1,0:T(8,128)S(1)}, u32[]{:S(2)}, u32[]{:S(2)}) async-start(f32[16,152,128]{2,1,0:T(8,128)} %shard_map.84), calls=%async_computation | async-start | bytes 2490368 | tf_op jit(solution)/shard_map/all_to_all | solution.py:637
  31.8 8.8 %collective-permute-start.4 = (f32[32,2048]{1,0:T(8,128)S(1)}, f32[32,2048]{1,0:T(8,128)S(1)}, u32[]{:S(2)}, u32[]{:S(2)}) collective-permute-start(f32[32,2048]{1,0:T(8,128)S(1)} %bitcast.8), channel_id=1, source_target_pairs={{0,32},{32,64},{64,96},{96,128},{128,160},{160,192},{192,224},{224... | collective-permute-start | bytes 786440 | tf_op jit(solution)/shard_map/ppermute | solution.py:614
  33.7 8.8 %collective-permute-start.6 = (f32[32,2048]{1,0:T(8,128)S(1)}, f32[32,2048]{1,0:T(8,128)S(1)}, u32[]{:S(2)}, u32[]{:S(2)}) collective-permute-start(f32[32,2048]{1,0:T(8,128)S(1)} %bitcast.9), channel_id=1, source_target_pairs={{0,480},{32,0},{64,32},{96,64},{128,96},{160,128},{192,160},{224,1... | collective-permute-start | bytes 786440 | tf_op jit(solution)/shard_map/ppermute | solution.py:614
  40.5 19.7 %collective-permute-start.5 = (f32[32,2048]{1,0:T(8,128)S(1)}, f32[32,2048]{1,0:T(8,128)S(1)}, u32[]{:S(2)}, u32[]{:S(2)}) collective-permute-start(f32[32,2048]{1,0:T(8,128)S(1)} %collective-permute-done.4.refs_3_.refs_5_), channel_id=1, source_target_pairs={{0,32},{32,64},{64,96},{96,128},{128,160},{160,192},{192,224},{224... | collective-permute-start | bytes 786440 | tf_op jit(solution)/shard_map/ppermute | solution.py:614
  42.4 17.8 %collective-permute-start.7 = (f32[32,2048]{1,0:T(8,128)S(1)}, f32[32,2048]{1,0:T(8,128)S(1)}, u32[]{:S(2)}, u32[]{:S(2)}) collective-permute-start(f32[32,2048]{1,0:T(8,128)S(1)} %collective-permute-done.6.refs_5_.refs_7_), channel_id=1, source_target_pairs={{0,480},{32,0},{64,32},{96,64},{128,96},{160,128},{192,160},{224,1... | collective-permute-start | bytes 786440 | tf_op jit(solution)/shard_map/ppermute | solution.py:614
  57.9 1.6 %copy-start.1 = (f32[8,32,128]{2,1,0:T(8,128)S(1)}, f32[8,32,128]{2,1,0:T(8,128)}, u32[]{:S(2)}) copy-start(f32[8,32,128]{2,1,0:T(8,128)} %get-tuple-element.44.refs_0_.refs_4_) | copy-start | bytes 393220

commit v7 on v6

--- a/solution.py
+++ b/solution.py
@@ -583,12 +583,13 @@
         band_sum((2.0 * smooth + t_s) * s2 + jnp.where(lane == 1, scalars, 0.0)),
         band_sum(coarse_image[...] * s2 + jnp.where(lane == 2, scalars, 0.0)),
     )
-    lane = iota((8, 128), 1)
-    res = jnp.zeros((8, 128), F32)
-    for i in range(3):
-        res = jnp.where(lane == i, dots[i], res)
+    lane = iota((1, 128), 1)
+    res = jnp.zeros((1, 128), F32)
+    for m in range(M):
+        for i in range(3):
+            res = jnp.where(lane == 32 * m + i, dots[i][m : m + 1], res)
     for z in range(NZ):
-        out[z] = res[:4]
+        out[z] = res
 
 
 def finish_kernel(pos, got, scalar, pre, smooth, stack, s_ref, out):
@@ -596,7 +597,9 @@
     sums = got[0]
     for z in range(1, NZ):
         sums = sums + got[z]
-    renewed, energy, cross = sums[:, 0:1], sums[:, 1:2], sums[:, 2:3]
+    renewed, energy, cross = (
+        jnp.concatenate([sums[:, 32 * m + i : 32 * m + i + 1] for m in range(M)], axis=0) for i in range(3)
+    )
     weight, first_energy, step = scalar[:4, 0:1], scalar[:4, 1:2], scalar[:4, 2:3]
     ratio = renewed / weight
     second = renewed / (energy + 2.0 * ratio * cross + ratio * ratio * first_energy)
@@ -662,7 +665,7 @@
     )
     got = lax.all_to_all(message, ("x", "y", "c"), 0, 0)
     dots, s1 = call(
-        last_kernel, [(NZ, 4, 128), (64, 128)], got, w_hi, w_lo, s0, coarse_right, coarse_image, t, acts, scalar
+        last_kernel, [(NZ, 1, 128), (64, 128)], got, w_hi, w_lo, s0, coarse_right, coarse_image, t, acts, scalar
     )
     got = lax.all_to_all(dots, "z", 0, 0)
     (out,) = call(finish_kernel, [(M, ROWS, COLS)], got, scalar, pre, smooth, stack, s1.reshape(NB, 8, 128))

time: 148 us -> 148 us (level)
  no operation moved by 1% of the time
where the time goes in v7:
time: 148 us; the launch traced here: 147 us
  blocking collectives  89.1 us (60%)
  starting transfers between devices  40.2 us (27%)
  Pallas kernels  11.7 us (8%)
  waiting for transfers between devices  4.07 us (3%)
  local copies, waits for them, and re-layouts  1.64 us (1%)
    all_to_all x2, blocking collectives, body(): got = lax.all_to_all(swept, 'z', 0, 0)  34.8 us
    ppermute x8, starting transfers between devices, shift(): lax.ppermute(value, axes, [(i, (i + by) % count) for i in range(count)])  33.3 us
    all_to_all x2, blocking collectives, body(): got = lax.all_to_all(message, ('x', 'y', 'c'), 0, 0)  29.4 us
    all_to_all x1, blocking collectives, body(): got = lax.all_to_all(dots, 'z', 0, 0)  15.9 us
    pallas_call x11, Pallas kernels, call(): pl.pallas_call(whole, out_shape=[jax.ShapeDtypeStruct(s, d) for s, d in o...  11.7 us
    all_to_all x1, blocking collectives, to_all(): lax.all_to_all(jnp.broadcast_to(value[None], (count,) + value.shape), axe...  8.95 us
    all_to_all x1, starting transfers between devices, body(): plane = lax.all_to_all(plane, ('x', 'y'), 0, 0)  6.89 us
  transfers between devices with their start and end apart: 9, of which 2 were waited for; matrix products, arithmetic and copies ran while one was open for 0% of the time, Pallas kernels for 2%

profile of v7, /device:TPU:1, one launch (start us, length us, event | category | flops | bytes accessed | tf_op | source)
XLA Modules:
  0.0 146.9 jit_solution(17825778642293793387)
XLA Ops:
  0.0 1.8 %shard_map.82 = (f32[8,32,128]{2,1,0:T(8,128)}, f32[48,128]{1,0:T(8,128)}, f32[2,24,128]{2,1,0:T(8,128)}) custom-call(f32[4,32,128]{2,1,0:T(8,128)} %refs_0_.1, f32[32,128]{1,0:T(8,128)} %refs_1_.1, f32[32,128]{1,0:T(8,128)} %refs_2_.1, f32[32,128]{1,0:T(8,128)} %refs_3_.1, s32[32,128]{1,0:T(8,128)} %refs_4_.1, s32[1,32]{1,0:T(1,128)} %bitcast.15, ...), custom_call_target="tpu_custom_call" | custom-call | tf_op jit(solution)/shard_map/pallas_call | solution.py:48
  1.8 4.4 %collective-permute-start = (f32[48,128]{1,0:T(8,128)}, f32[48,128]{1,0:T(8,128)S(1)}, u32[]{:S(2)}, u32[]{:S(2)}) collective-permute-start(f32[48,128]{1,0:T(8,128)} %get-tuple-element.39.refs_0_), channel_id=1, source_target_pairs={{0,32},{32,64},{64,96},{96,128},{128,160},{160,192},{192,224},{224... | collective-permute-start | bytes 73736 | tf_op jit(solution)/shard_map/ppermute | solution.py:617
  6.2 9.5 %collective-permute-start.2 = (f32[48,128]{1,0:T(8,128)}, f32[48,128]{1,0:T(8,128)S(1)}, u32[]{:S(2)}, u32[]{:S(2)}) collective-permute-start(f32[48,128]{1,0:T(8,128)} %get-tuple-element.39.refs_0_), channel_id=1, source_target_pairs={{0,480},{32,0},{64,32},{96,64},{128,96},{160,128},{192,160},{224,1... | collective-permute-start | bytes 73736 | tf_op jit(solution)/shard_map/ppermute | solution.py:617
  15.7 0.0 collective-permute-done.refs_1_
  15.7 1.9 %collective-permute-start.1 = (f32[48,128]{1,0:T(8,128)S(1)}, f32[48,128]{1,0:T(8,128)S(1)}, u32[]{:S(2)}, u32[]{:S(2)}) collective-permute-start(f32[48,128]{1,0:T(8,128)S(1)} %collective-permute-done.refs_1_), channel_id=1, source_target_pairs={{0,32},{32,64},{64,96},{96,128},{128,160},{160,192},{192,224},{224... | collective-permute-start | bytes 73736 | tf_op jit(solution)/shard_map/ppermute | solution.py:617
  17.6 0.0 collective-permute-done.2.refs_3_
  17.6 4.6 %collective-permute-start.3 = (f32[48,128]{1,0:T(8,128)S(1)}, f32[48,128]{1,0:T(8,128)S(1)}, u32[]{:S(2)}, u32[]{:S(2)}) collective-permute-start(f32[48,128]{1,0:T(8,128)S(1)} %collective-permute-done.2.refs_3_), channel_id=1, source_target_pairs={{0,480},{32,0},{64,32},{96,64},{128,96},{160,128},{192,160},{224,1... | collective-permute-start | bytes 73736 | tf_op jit(solution)/shard_map/ppermute | solution.py:617
  22.2 0.0 copy-start.2
  22.2 0.7 copy-done.2
  22.9 0.0 copy-start.3
  22.9 0.7 copy-done.3
  23.7 0.0 collective-permute-done.1.refs_0_
  23.7 0.0 collective-permute-done.3.refs_4_
  23.7 1.2 shard_map.84
  24.8 0.0 copy-start
  24.9 6.9 %all-to-all-start = ((f32[16,152,128]{2,1,0:T(8,128)}), f32[16,152,128]{2,1,0:T(8,128)S(1)}, u32[]{:S(2)}, u32[]{:S(2)}) async-start(f32[16,152,128]{2,1,0:T(8,128)} %shard_map.84), calls=%async_computation | async-start | bytes 2490368 | tf_op jit(solution)/shard_map/all_to_all | solution.py:640
  31.7 0.0 copy-done
  31.8 1.9 %collective-permute-start.4 = (f32[32,2048]{1,0:T(8,128)S(1)}, f32[32,2048]{1,0:T(8,128)S(1)}, u32[]{:S(2)}, u32[]{:S(2)}) collective-permute-start(f32[32,2048]{1,0:T(8,128)S(1)} %bitcast.8), channel_id=1, source_target_pairs={{0,32},{32,64},{64,96},{96,128},{128,160},{160,192},{192,224},{224... | collective-permute-start | bytes 786440 | tf_op jit(solution)/shard_map/ppermute | solution.py:617
  33.7 4.6 %collective-permute-start.6 = (f32[32,2048]{1,0:T(8,128)S(1)}, f32[32,2048]{1,0:T(8,128)S(1)}, u32[]{:S(2)}, u32[]{:S(2)}) collective-permute-start(f32[32,2048]{1,0:T(8,128)S(1)} %bitcast.9), channel_id=1, source_target_pairs={{0,480},{32,0},{64,32},{96,64},{128,96},{160,128},{192,160},{224,1... | collective-permute-start | bytes 786440 | tf_op jit(solution)/shard_map/ppermute | solution.py:617
  38.3 2.3 %collective-permute-done.4.refs_3_.refs_5_ = f32[32,2048]{1,0:T(8,128)S(1)} collective-permute-done((f32[32,2048]{1,0:T(8,128)S(1)}, f32[32,2048]{1,0:T(8,128)S(1)}, u32[]{:S(2)}, u32[]{:S(2)}) %collective-permute-start.4) | collective-permute-done | bytes 262176 | tf_op jit(solution)/shard_map/ppermute | solution.py:617
  40.5 1.9 %collective-permute-start.5 = (f32[32,2048]{1,0:T(8,128)S(1)}, f32[32,2048]{1,0:T(8,128)S(1)}, u32[]{:S(2)}, u32[]{:S(2)}) collective-permute-start(f32[32,2048]{1,0:T(8,128)S(1)} %collective-permute-done.4.refs_3_.refs_5_), channel_id=1, source_target_pairs={{0,32},{32,64},{64,96},{96,128},{128,160},{160,192},{192,224},{224... | collective-permute-start | bytes 786440 | tf_op jit(solution)/shard_map/ppermute | solution.py:617
  42.4 0.0 collective-permute-done.6.refs_5_.refs_7_
  42.4 4.6 %collective-permute-start.7 = (f32[32,2048]{1,0:T(8,128)S(1)}, f32[32,2048]{1,0:T(8,128)S(1)}, u32[]{:S(2)}, u32[]{:S(2)}) collective-permute-start(f32[32,2048]{1,0:T(8,128)S(1)} %collective-permute-done.6.refs_5_.refs_7_), channel_id=1, source_target_pairs={{0,480},{32,0},{64,32},{96,64},{128,96},{160,128},{192,160},{224,1... | collective-permute-start | bytes 786440 | tf_op jit(solution)/shard_map/ppermute | solution.py:617
  47.0 1.8 %all-to-all-done = f32[16,152,128]{2,1,0:T(8,128)S(1)} async-done(((f32[16,152,128]{2,1,0:T(8,128)}), f32[16,152,128]{2,1,0:T(8,128)S(1)}, u32[]{:S(2)}, u32[]{:S(2)}) %all-to-all-start) | async-done | bytes 1245216 | tf_op jit(solution)/shard_map/all_to_all | solution.py:640
  48.8 0.2 broadcast_in_dim.2
  49.0 9.0 %all_to_all.35 = f32[2,16,152,128]{3,2,1,0:T(8,128)S(1)} all-to-all(f32[2,16,152,128]{3,2,1,0:T(8,128)S(1)} %broadcast_in_dim.2), channel_id=1, replica_groups=mesh['z'=16,'x'=4,'y'=4,'c'=2] {'c'}, dimensions={0} | all-to-all | bytes 4980736 | tf_op jit(solution)/shard_map/all_to_all | solution.py:626
  57.9 0.0 copy-start.1
  57.9 1.6 %shard_map.85 = (f32[16,4,128]{2,1,0:T(4,128)S(1)}, f32[64,128]{1,0:T(8,128)S(1)}, f32[3,64,128]{2,1,0:T(8,128)S(1)}, bf16[40,128,128]{2,1,0:T(8,128)(2,1)S(1)}, bf16[40,128,128]{2,1,0:T(8,128)(2,1)S(1)}) custom-call(f32[32,152,128]{2,1,0:T(8,128)S(1)} %bitcast.6), custom_call_target="tpu_custom_call" | custom-call | tf_op jit(solution)/shard_map/pallas_call | solution.py:48
  59.5 0.0 copy-done.1
  59.6 0.6 shard_map.86
  60.2 0.0 collective-permute-done.5.refs_2_.refs_4_
  60.2 0.0 collective-permute-done.7.refs_6_.refs_8_
  60.2 19.5 %all_to_all.36.refs_0_ = f32[16,4,128]{2,1,0:T(4,128)S(1)} all-to-all(f32[16,4,128]{2,1,0:T(4,128)S(1)} %get-tuple-element.46), channel_id=1, replica_groups=mesh['z'=16,'x'=4,'y'=4,'c'=2] {'z'}, dimensions={0} | all-to-all | bytes 65536 | tf_op jit(solution)/shard_map/all_to_all | solution.py:654
  79.7 0.5 shard_map.87
  80.2 15.6 %all_to_all.37.refs_0_ = f32[32,4,384]{2,1,0:T(4,128)S(1)} all-to-all(f32[32,4,384]{2,1,0:T(4,128)S(1)} %shard_map.87), channel_id=1, replica_groups=mesh['z'=16,'x'=4,'y'=4,'c'=2] {'x','y','c'}, dimensions={0} | all-to-all | bytes 393216 | tf_op jit(solution)/shard_map/all_to_all | solution.py:656
  95.9 2.7 %shard_map.88 = (f32[16,5,4,128]{3,2,1,0:T(4,128)S(1)}, f32[3,64,128]{2,1,0:T(8,128)S(1)}, f32[64,128]{1,0:T(8,128)S(1)}, f32[5,64,128]{2,1,0:T(8,128)S(1)}) custom-call(f32[32,4,384]{2,1,0:T(4,128)S(1)} %all_to_all.37.refs_0_, bf16[40,128,128]{2,1,0:T(8,128)(2,1)S(1)} %get-tuple-element.53.refs_1_, bf16[40,128,128]{2,1,0:T(8,128)(2,1)S(1)} %get-tuple-element.54.refs_2_, ...), custom_call_target="tpu_custom_call" | custom-call | tf_op jit(solution)/shard_map/pallas_call | solution.py:48
  98.6 0.3 shard_map.89
  98.9 15.3 %all_to_all.38.refs_0_ = f32[16,5,4,128]{3,2,1,0:T(4,128)S(1)} all-to-all(f32[16,5,4,128]{3,2,1,0:T(4,128)S(1)} %get-tuple-element.63), channel_id=1, replica_groups=mesh['z'=16,'x'=4,'y'=4,'c'=2] {'z'}, dimensions={0} | all-to-all | bytes 327680 | tf_op jit(solution)/shard_map/all_to_all | solution.py:662
  114.2 0.6 shard_map.90
  114.8 13.8 %all_to_all.39.refs_0_ = f32[32,4,256]{2,1,0:T(4,128)S(1)} all-to-all(f32[32,4,256]{2,1,0:T(4,128)S(1)} %get-tuple-element.65), channel_id=1, replica_groups=mesh['z'=16,'x'=4,'y'=4,'c'=2] {'x','y','c'}, dimensions={0} | all-to-all | bytes 262144 | tf_op jit(solution)/shard_map/all_to_all | solution.py:666
  128.6 1.4 shard_map.91
  130.0 15.9 %all_to_all.40.refs_0_ = f32[16,1,128]{2,1,0:T(1,128)S(1)} all-to-all(f32[16,1,128]{2,1,0:T(1,128)S(1)} %get-tuple-element.69), channel_id=1, replica_groups=mesh['z'=16,'x'=4,'y'=4,'c'=2] {'z'}, dimensions={0} | all-to-all | bytes 16384 | tf_op jit(solution)/shard_map/all_to_all | solution.py:670
  145.9 1.0 shard_map.92
  (1 shorter events, 0.0 us)
Async XLA Ops:
  1.8 13.9 %collective-permute-start = (f32[48,128]{1,0:T(8,128)}, f32[48,128]{1,0:T(8,128)S(1)}, u32[]{:S(2)}, u32[]{:S(2)}) collective-permute-start(f32[48,128]{1,0:T(8,128)} %get-tuple-element.39.refs_0_), channel_id=1, source_target_pairs={{0,32},{32,64},{64,96},{96,128},{128,160},{160,192},{192,224},{224... | collective-permute-start | bytes 73736 | tf_op jit(solution)/shard_map/ppermute | solution.py:617
  6.2 11.4 %collective-permute-start.2 = (f32[48,128]{1,0:T(8,128)}, f32[48,128]{1,0:T(8,128)S(1)}, u32[]{:S(2)}, u32[]{:S(2)}) collective-permute-start(f32[48,128]{1,0:T(8,128)} %get-tuple-element.39.refs_0_), channel_id=1, source_target_pairs={{0,480},{32,0},{64,32},{96,64},{128,96},{160,128},{192,160},{224,1... | collective-permute-start | bytes 73736 | tf_op jit(solution)/shard_map/ppermute | solution.py:617
  15.7 8.0 %collective-permute-start.1 = (f32[48,128]{1,0:T(8,128)S(1)}, f32[48,128]{1,0:T(8,128)S(1)}, u32[]{:S(2)}, u32[]{:S(2)}) collective-permute-start(f32[48,128]{1,0:T(8,128)S(1)} %collective-permute-done.refs_1_), channel_id=1, source_target_pairs={{0,32},{32,64},{64,96},{96,128},{128,160},{160,192},{192,224},{224... | collective-permute-start | bytes 73736 | tf_op jit(solution)/shard_map/ppermute | solution.py:617
  17.6 6.1 %collective-permute-start.3 = (f32[48,128]{1,0:T(8,128)S(1)}, f32[48,128]{1,0:T(8,128)S(1)}, u32[]{:S(2)}, u32[]{:S(2)}) collective-permute-start(f32[48,128]{1,0:T(8,128)S(1)} %collective-permute-done.2.refs_3_), channel_id=1, source_target_pairs={{0,480},{32,0},{64,32},{96,64},{128,96},{160,128},{192,160},{224,1... | collective-permute-start | bytes 73736 | tf_op jit(solution)/shard_map/ppermute | solution.py:617
  22.2 0.7 copy-start.2
  22.9 0.7 copy-start.3
  24.8 6.9 %copy-start = (f32[1,32,2048]{2,1,0:T(8,128)S(1)}, f32[1,32,2048]{2,1,0:T(8,128)}, u32[]{:S(2)}) copy-start(f32[1,32,2048]{2,1,0:T(8,128)} %param.15) | copy-start | bytes 786436
  24.9 24.0 %all-to-all-start = ((f32[16,152,128]{2,1,0:T(8,128)}), f32[16,152,128]{2,1,0:T(8,128)S(1)}, u32[]{:S(2)}, u32[]{:S(2)}) async-start(f32[16,152,128]{2,1,0:T(8,128)} %shard_map.84), calls=%async_computation | async-start | bytes 2490368 | tf_op jit(solution)/shard_map/all_to_all | solution.py:640
  31.8 8.8 %collective-permute-start.4 = (f32[32,2048]{1,0:T(8,128)S(1)}, f32[32,2048]{1,0:T(8,128)S(1)}, u32[]{:S(2)}, u32[]{:S(2)}) collective-permute-start(f32[32,2048]{1,0:T(8,128)S(1)} %bitcast.8), channel_id=1, source_target_pairs={{0,32},{32,64},{64,96},{96,128},{128,160},{160,192},{192,224},{224... | collective-permute-start | bytes 786440 | tf_op jit(solution)/shard_map/ppermute | solution.py:617
  33.7 8.8 %collective-permute-start.6 = (f32[32,2048]{1,0:T(8,128)S(1)}, f32[32,2048]{1,0:T(8,128)S(1)}, u32[]{:S(2)}, u32[]{:S(2)}) collective-permute-start(f32[32,2048]{1,0:T(8,128)S(1)} %bitcast.9), channel_id=1, source_target_pairs={{0,480},{32,0},{64,32},{96,64},{128,96},{160,128},{192,160},{224,1... | collective-permute-start | bytes 786440 | tf_op jit(solution)/shard_map/ppermute | solution.py:617
  40.5 19.7 %collective-permute-start.5 = (f32[32,2048]{1,0:T(8,128)S(1)}, f32[32,2048]{1,0:T(8,128)S(1)}, u32[]{:S(2)}, u32[]{:S(2)}) collective-permute-start(f32[32,2048]{1,0:T(8,128)S(1)} %collective-permute-done.4.refs_3_.refs_5_), channel_id=1, source_target_pairs={{0,32},{32,64},{64,96},{96,128},{128,160},{160,192},{192,224},{224... | collective-permute-start | bytes 786440 | tf_op jit(solution)/shard_map/ppermute | solution.py:617
  42.4 17.8 %collective-permute-start.7 = (f32[32,2048]{1,0:T(8,128)S(1)}, f32[32,2048]{1,0:T(8,128)S(1)}, u32[]{:S(2)}, u32[]{:S(2)}) collective-permute-start(f32[32,2048]{1,0:T(8,128)S(1)} %collective-permute-done.6.refs_5_.refs_7_), channel_id=1, source_target_pairs={{0,480},{32,0},{64,32},{96,64},{128,96},{160,128},{192,160},{224,1... | collective-permute-start | bytes 786440 | tf_op jit(solution)/shard_map/ppermute | solution.py:617
  57.9 1.6 %copy-start.1 = (f32[8,32,128]{2,1,0:T(8,128)S(1)}, f32[8,32,128]{2,1,0:T(8,128)}, u32[]{:S(2)}) copy-start(f32[8,32,128]{2,1,0:T(8,128)} %get-tuple-element.44.refs_0_.refs_4_) | copy-start | bytes 393220
